TPU v7x, 128 devices: a whole 4x4x4 slice. The times are simulated.
128 devices in a mesh: gx: 16 (over z_hi, x, core), gy: 8 (over y, z_lo).
Axes of the slice: x: 4, y: 4, z: 4 (z_hi: 2, z_lo: 2; z = z_hi * 2 + z_lo), core: 2. Of those that a mesh axis runs over, the one named last changes fastest.
Arguments:
- object_field: float32 [2, 16384, 8192], P(None, 'gx', 'gy'), may hold values from -5 to 5
- probe: float32 [2, 256, 256], replicated, may hold values from -5 to 5
- centers: int32 [2048, 2], P(('gx', 'gy')), may hold values from 0 to 1023
- live: int32 [2048], P(('gx', 'gy')), may hold values from 0 to 1, as said below
- measured: float32 [2048, 256, 256], P(('gx', 'gy')), may hold values from 0.5 to 2.5
Outputs:
- object_grad: float32 [2, 16384, 8192], P(None, 'gx', 'gy')
- probe_grad: float32 [2, 256, 256], replicated
- slot_loss: float32 [2048], P(('gx', 'gy'))
Inputs may be any that keep to these rules, and one draw needn't show every extreme that they name: In each tile's 16 slots the live ones come first; every tile has at least one live slot, and some tile has all 16 live.
All inputs are finite; a program needn't handle non-finite values.
Results may differ from a plain program's by a relative error of at most 0.0001.
Values sent between devices are 32-bit elements; how exact they have to be, the bound alone decides.
A program may use at most 192 MiB of HBM per device.

v0:
```python
import math

import jax
import jax.numpy as jnp
from jax import lax
from jax.sharding import PartitionSpec as P


def with_halo(cells, sides, width):
    for axis, dim in sides:
        count = lax.axis_size(axis)
        ends = count - 1
        head = lax.slice_in_dim(cells, 0, width, axis=dim)
        tail = lax.slice_in_dim(cells, cells.shape[dim] - width, cells.shape[dim], axis=dim)
        cells = jnp.concatenate(
            [
                lax.ppermute(tail, axis, [(i, (i + 1) % count) for i in range(ends)]),
                cells,
                lax.ppermute(head, axis, [((i + 1) % count, i) for i in range(ends)]),
            ],
            axis=dim,
        )
    return cells


def dft_tables(extent):
    steps_k = jnp.arange(extent, dtype=jnp.int32)
    phase = (steps_k[:, None] * steps_k[None, :] % extent).astype(jnp.float32)
    angle = phase * (-2.0 * math.pi / extent)
    norm_c = 1.0 / math.sqrt(extent)
    return (jnp.cos(angle) * norm_c, jnp.sin(angle) * norm_c)


def product(left, right):
    return jnp.dot(left, right, precision=lax.Precision.HIGHEST, preferred_element_type=jnp.float32)


def transform(real_in, imag_in, cos_table, sin_table):
    left_re = product(cos_table, real_in) - product(sin_table, imag_in)
    left_im = product(cos_table, imag_in) + product(sin_table, real_in)
    out_re = product(left_re, cos_table) - product(left_im, sin_table)
    out_im = product(left_re, sin_table) + product(left_im, cos_table)
    return (out_re, out_im)


def fold_rows(padded, half_width):
    total = padded.shape[1]
    middle = padded[:, 2 * half_width : total - 2 * half_width]
    inner = middle.shape[1]
    middle = middle.at[:, :half_width].add(padded[:, :half_width])
    middle = middle.at[:, inner - half_width :].add(padded[:, total - half_width :])
    return middle


def fold_cols(padded, half_width):
    total = padded.shape[2]
    middle = padded[:, :, 2 * half_width : total - 2 * half_width]
    inner = middle.shape[2]
    middle = middle.at[:, :, :half_width].add(padded[:, :, :half_width])
    middle = middle.at[:, :, inner - half_width :].add(padded[:, :, total - half_width :])
    return middle


def on_device(object_field, probe, centers, live, measured):
    extent = probe.shape[1]
    half_width = extent // 2
    local_slots = centers.shape[0]
    extended = with_halo(object_field, (("gx", 1), ("gy", 2)), half_width)
    cos_table, sin_table = dft_tables(extent)
    back_sin = -sin_table
    probe_re = probe[0]
    probe_im = probe[1]

    def visit(slot_index, state_now):
        grad_ext, acc_re, acc_im, losses = state_now
        row_at = centers[slot_index, 0]
        col_at = centers[slot_index, 1]
        zero_at = jnp.zeros((), jnp.int32)
        patch_obj = lax.dynamic_slice(extended, (zero_at, row_at, col_at), (2, extent, extent))
        obj_re = patch_obj[0]
        obj_im = patch_obj[1]
        wave_re = probe_re * obj_re - probe_im * obj_im
        wave_im = probe_re * obj_im + probe_im * obj_re
        far_re, far_im = transform(wave_re, wave_im, cos_table, sin_table)
        modulus = jnp.sqrt(far_re * far_re + far_im * far_im + 1.0)
        differ = modulus - measured[slot_index]
        weight = live[slot_index].astype(jnp.float32)
        factor = differ / modulus * weight
        back_re, back_im = transform(far_re * factor, far_im * factor, cos_table, back_sin)
        grad_re = probe_re * back_re + probe_im * back_im
        grad_im = probe_re * back_im - probe_im * back_re
        old_patch = lax.dynamic_slice(grad_ext, (zero_at, row_at, col_at), (2, extent, extent))
        grad_ext = lax.dynamic_update_slice(
            grad_ext, old_patch + jnp.stack([grad_re, grad_im]), (zero_at, row_at, col_at)
        )
        acc_re = acc_re + obj_re * back_re + obj_im * back_im
        acc_im = acc_im + obj_re * back_im - obj_im * back_re
        loss = 0.5 * weight * jnp.sum(differ * differ) / (extent * extent)
        losses = losses.at[slot_index].set(loss)
        return (grad_ext, acc_re, acc_im, losses)

    start = (
        jnp.zeros(extended.shape, jnp.float32),
        jnp.zeros(probe_re.shape, jnp.float32),
        jnp.zeros(probe_re.shape, jnp.float32),
        jnp.zeros((local_slots,), jnp.float32),
    )
    final = lax.fori_loop(0, local_slots, visit, start)
    grad_ext, acc_re, acc_im, slot_loss = final
    padded = with_halo(grad_ext, (("gx", 1), ("gy", 2)), half_width)
    object_grad = fold_cols(fold_rows(padded, half_width), half_width)
    totals = lax.psum((acc_re, acc_im), ("gx", "gy"))
    slots_all = local_slots * lax.axis_size("gx") * lax.axis_size("gy")
    probe_grad = jnp.stack([totals[0], totals[1]]) / math.sqrt(slots_all)
    return (object_grad, probe_grad, slot_loss)


def solution(mesh):
    placed = (
        P(None, "gx", "gy"),
        P(),
        P(("gx", "gy"), None),
        P(("gx", "gy")),
        P(("gx", "gy"), None, None),
    )
    return jax.shard_map(
        on_device,
        mesh=mesh,
        in_specs=placed,
        out_specs=(P(None, "gx", "gy"), P(), P(("gx", "gy"))),
        check_vma=False,
    )
```

profile of v0, /device:TPU:1, one launch (start us, length us, event | category | flops | bytes accessed | tf_op | source)
XLA Modules:
  0.0 1060.0 jit_solution(8235465235481876779)
XLA Ops:
  8.9 4.5 collective-permute-start
  15.3 9.8 collective-permute-done
  25.2 4.3 constant_dynamic-update-slice_fusion.1
  29.7 3.9 copy-done
  35.3 3.6 collective-permute-start.2
  40.3 45.6 %collective-permute-done.2 = f32[2,1280,128]{2,1,0:T(8,128)S(1)} collective-permute-done((f32[2,1280,128]{2,1,0:T(8,128)}, f32[2,1280,128]{2,1,0:T(8,128)S(1)}, u32[]{:S(2)}, u32[]{:S(2)}) %collective-permute-start.2) | collective-permute-done | bytes 1310752 | tf_op jit(solution)/shard_map/ppermute | solution.py:17
  85.9 10.1 pad_maximum_fusion.1
  96.0 5.6 broadcast_in_dim.8
  101.6 679.7 %while.26 = (s32[]{:T(128)}, f32[2,1280,1280]{2,1,0:T(8,128)}, f32[256,256]{1,0:T(8,128)S(1)}, f32[256,256]{1,0:T(8,128)S(1)}, f32[16]{0:T(128)S(1)}, /*index=5*...) while((s32[]{:T(128)}, f32[2,1280,1280]{2,1,0:T(8,128)}, ...), condition=%wide.region_2.3_spmd.clone.clone, body=%wide.region_0.2_spmd.clone.clone.sunk | while | flops 3240296448 | bytes 19137056 | solution.py:108
  119.0 3.1 multiply_reduce_fusion.2
  133.4 2.7 fusion.189
  137.5 6.8 dynamic_update_slice.10
  161.7 3.1 multiply_reduce_fusion.2
  180.2 6.7 dynamic_update_slice.10
  204.3 3.1 multiply_reduce_fusion.2
  218.7 2.7 fusion.189
  222.8 6.4 dynamic_update_slice.10
  246.6 3.1 multiply_reduce_fusion.2
  261.0 2.7 fusion.189
  265.1 6.8 dynamic_update_slice.10
  289.3 3.1 multiply_reduce_fusion.2
  303.7 2.7 fusion.189
  307.8 6.8 dynamic_update_slice.10
  332.0 3.1 multiply_reduce_fusion.2
  350.4 6.0 dynamic_update_slice.10
  373.8 3.1 multiply_reduce_fusion.2
  388.2 2.7 fusion.189
  392.3 6.8 dynamic_update_slice.10
  416.6 3.1 multiply_reduce_fusion.2
  430.9 2.7 fusion.189
  435.0 6.5 dynamic_update_slice.10
  459.0 3.1 multiply_reduce_fusion.2
  473.3 2.7 fusion.189
  477.4 6.8 dynamic_update_slice.10
  501.6 3.1 multiply_reduce_fusion.2
  515.9 2.7 fusion.189
  520.1 6.5 dynamic_update_slice.10
  544.0 3.1 multiply_reduce_fusion.2
  558.3 2.7 fusion.189
  562.5 6.8 dynamic_update_slice.10
  586.7 3.1 multiply_reduce_fusion.2
  601.0 2.7 fusion.189
  605.1 6.8 dynamic_update_slice.10
  629.3 3.1 multiply_reduce_fusion.2
  643.7 2.7 fusion.189
  647.8 6.8 dynamic_update_slice.10
  672.0 3.1 multiply_reduce_fusion.2
  690.5 6.2 dynamic_update_slice.10
  714.1 3.1 multiply_reduce_fusion.2
  732.5 6.2 dynamic_update_slice.10
  756.1 3.1 multiply_reduce_fusion.2
  774.5 6.8 dynamic_update_slice.10
  783.5 15.1 %collective-permute-start.4 = (f32[2,128,1280]{2,1,0:T(8,128)S(1)}, f32[2,128,1280]{2,1,0:T(8,128)S(1)}, u32[]{:S(2)}, u32[]{:S(2)}) collective-permute-start(f32[2,128,1280]{2,1,0:T(8,128)S(1)} %get-tuple-element.478), channel_id=1, source_target_pairs={{0,8},{8,16},{16,24},{24,32},{32,40},{40,48},{48,56},{56,64},{64,7... | collective-permute-start | bytes 3932168 | tf_op jit(solution)/shard_map/ppermute | solution.py:17
  800.5 12.6 %collective-permute-done.4 = f32[2,128,1280]{2,1,0:T(8,128)S(1)} collective-permute-done((f32[2,128,1280]{2,1,0:T(8,128)S(1)}, f32[2,128,1280]{2,1,0:T(8,128)S(1)}, u32[]{:S(2)}, u32[]{:S(2)}) %collective-permute-start.4) | collective-permute-done | bytes 1310752 | tf_op jit(solution)/shard_map/ppermute | solution.py:17
  814.3 10.3 constant_dynamic-update-slice_fusion.4
  827.1 3.8 fusion.114
  830.9 3.6 collective-permute-start.6
  835.8 174.2 %all-reduce.3.cloned.1.call-done = (f32[1,256,256]{2,1,0:T(8,128)}, f32[1,256,256]{2,1,0:T(8,128)}) async-done(((f32[1,256,256]{2,1,0:T(8,128)}, f32[1,256,256]{2,1,0:T(8,128)}), (f32[1,256,256]{2,1,0:T(8,128)}, f32[1,256,256]{2,1,0:T(8,128)})) %all-reduce.3.cloned.1.call-update) | async-done | bytes 524304 | tf_op jit(solution)/shard_map/psum | solution.py:112
  1011.9 13.6 %pad_maximum_fusion = f32[2,1536,1536]{2,1,0:T(8,128)} fusion(f32[2,1536,128]{2,1,0:T(8,128)S(1)} %collective-permute-done.7, f32[2,1536,1280]{2,1,0:T(8,128)} %constant_dynamic-update-slice_fusion.3, f32[2,1536,128]{2,1,0:T(8,128)S(1)} %collective-permute-done.6), kind=kLoop, calls=%fused_computation.136 | loop fusion | flops 9437184 | bytes 37748736 | tf_op jit(solution)/shard_map/concatenate | solution.py:15
  1025.5 10.5 slice.205
  1036.0 3.1 fusion.111
  1039.1 3.2 fusion.110
  1042.2 4.2 slice.207
  1049.7 3.4 copy-done.1
  (348 shorter events, 430.2 us)
Async XLA Ops:
  7.2 1002.9 %all-reduce.3.cloned.1.call-start = ((), (), s32[]{:S(2)}) async-start(), calls=%async_computation | async-start | bytes 1048576 | tf_op jit(solution)/shard_map/psum | solution.py:112
  8.9 16.2 %collective-permute-start = (f32[2,128,1024]{2,1,0:T(8,128)S(1)}, f32[2,128,1024]{2,1,0:T(8,128)S(1)}, u32[]{:S(2)}, u32[]{:S(2)}) collective-permute-start(f32[2,128,1024]{2,1,0:T(8,128)S(1)} %get-tuple-element.482), channel_id=1, source_target_pairs={{0,8},{8,16},{16,24},{24,32},{32,40},{40,48},{48,56},{56,64},{64,7... | collective-permute-start | bytes 3145736 | tf_op jit(solution)/shard_map/ppermute | solution.py:17
  13.4 16.1 %collective-permute-start.1 = (f32[2,128,1024]{2,1,0:T(8,128)S(1)}, f32[2,128,1024]{2,1,0:T(8,128)S(1)}, u32[]{:S(2)}, u32[]{:S(2)}) collective-permute-start(f32[2,128,1024]{2,1,0:T(8,128)S(1)} %get-tuple-element.481), channel_id=1, source_target_pairs={{8,0},{16,8},{24,16},{32,24},{40,32},{48,40},{56,48},{64,56},{72,6... | collective-permute-start | bytes 3145736 | tf_op jit(solution)/shard_map/ppermute | solution.py:19
  25.2 15.0 %copy-start.4 = (f32[2,256,256]{2,1,0:T(8,128)S(1)}, f32[2,256,256]{2,1,0:T(8,128)}, u32[]{:S(2)}) copy-start(f32[2,256,256]{2,1,0:T(8,128)} %param.18) | copy-start | bytes 1572868
  29.6 3.9 copy-start
  35.3 50.6 %collective-permute-start.2 = (f32[2,1280,128]{2,1,0:T(8,128)}, f32[2,1280,128]{2,1,0:T(8,128)S(1)}, u32[]{:S(2)}, u32[]{:S(2)}) collective-permute-start(f32[2,1280,128]{2,1,0:T(8,128)} %get-tuple-element.479), channel_id=1, source_target_pairs={{0,1},{1,2},{2,3},{3,4},{4,5},{5,6},{6,7},{8,9},{9,10},{10,11},{11... | collective-permute-start | bytes 3932168 | tf_op jit(solution)/shard_map/ppermute | solution.py:17
  38.9 47.0 %collective-permute-start.3 = (f32[2,1280,128]{2,1,0:T(8,128)}, f32[2,1280,128]{2,1,0:T(8,128)}, u32[]{:S(2)}, u32[]{:S(2)}) collective-permute-start(f32[2,1280,128]{2,1,0:T(8,128)} %get-tuple-element.480), channel_id=1, source_target_pairs={{1,0},{2,1},{3,2},{4,3},{5,4},{6,5},{7,6},{9,8},{10,9},{11,10},{12... | collective-permute-start | bytes 3932168 | tf_op jit(solution)/shard_map/ppermute | solution.py:19
  96.0 5.6 copy-start.5
  96.0 5.6 copy-start.7
  781.3 43.3 %copy-start.2 = (f32[256,256]{1,0:T(8,128)}, f32[256,256]{1,0:T(8,128)S(1)}, u32[]{:S(2)}) copy-start(f32[256,256]{1,0:T(8,128)S(1)} %get-tuple-element.346) | copy-start | bytes 786436
  781.3 43.3 %copy-start.3 = (f32[256,256]{1,0:T(8,128)}, f32[256,256]{1,0:T(8,128)S(1)}, u32[]{:S(2)}) copy-start(f32[256,256]{1,0:T(8,128)S(1)} %get-tuple-element.345) | copy-start | bytes 786436
  781.3 43.3 %copy-start.6 = (f32[16]{0:T(128)}, f32[16]{0:T(128)S(1)}, u32[]{:S(2)}) copy-start(f32[16]{0:T(128)S(1)} %get-tuple-element.343) | copy-start | bytes 196
  783.5 29.6 %collective-permute-start.4 = (f32[2,128,1280]{2,1,0:T(8,128)S(1)}, f32[2,128,1280]{2,1,0:T(8,128)S(1)}, u32[]{:S(2)}, u32[]{:S(2)}) collective-permute-start(f32[2,128,1280]{2,1,0:T(8,128)S(1)} %get-tuple-element.478), channel_id=1, source_target_pairs={{0,8},{8,16},{16,24},{24,32},{32,40},{40,48},{48,56},{56,64},{64,7... | collective-permute-start | bytes 3932168 | tf_op jit(solution)/shard_map/ppermute | solution.py:17
  798.6 26.1 %collective-permute-start.5 = (f32[2,128,1280]{2,1,0:T(8,128)S(1)}, f32[2,128,1280]{2,1,0:T(8,128)}, u32[]{:S(2)}, u32[]{:S(2)}) collective-permute-start(f32[2,128,1280]{2,1,0:T(8,128)S(1)} %get-tuple-element.477), channel_id=1, source_target_pairs={{8,0},{16,8},{24,16},{32,24},{40,32},{48,40},{56,48},{64,56},{72,6... | collective-permute-start | bytes 3932168 | tf_op jit(solution)/shard_map/ppermute | solution.py:19
  830.9 181.0 %collective-permute-start.6 = (f32[2,1536,128]{2,1,0:T(8,128)}, f32[2,1536,128]{2,1,0:T(8,128)S(1)}, u32[]{:S(2)}, u32[]{:S(2)}) collective-permute-start(f32[2,1536,128]{2,1,0:T(8,128)} %get-tuple-element.475), channel_id=1, source_target_pairs={{0,1},{1,2},{2,3},{3,4},{4,5},{5,6},{6,7},{8,9},{9,10},{10,11},{11... | collective-permute-start | bytes 4718600 | tf_op jit(solution)/shard_map/ppermute | solution.py:17
  834.5 177.4 %collective-permute-start.7 = (f32[2,1536,128]{2,1,0:T(8,128)}, f32[2,1536,128]{2,1,0:T(8,128)S(1)}, u32[]{:S(2)}, u32[]{:S(2)}) collective-permute-start(f32[2,1536,128]{2,1,0:T(8,128)} %get-tuple-element.476), channel_id=1, source_target_pairs={{1,0},{2,1},{3,2},{4,3},{5,4},{6,5},{7,6},{9,8},{10,9},{11,10},{12... | collective-permute-start | bytes 4718600 | tf_op jit(solution)/shard_map/ppermute | solution.py:19
  1049.7 3.4 copy-start.1
Sparse Core Ops, SparseCore 0:
  836.0 174.0 all-reduce.2
where the time goes:
time: 1070 us; the launch traced here: 1060 us
  matrix products  424 us (40%)
  waiting for transfers between devices  242 us (23%)
  local copies, waits for them, and re-layouts  180 us (17%)
  loops' own time  85.2 us (8%)
  other arithmetic  81.3 us (8%)
  starting transfers between devices  33.3 us (3%)
  between operations  14.2 us (1%)
    dot_general x256, matrix products, product(): jnp.dot(left, right, precision=lax.Precision.HIGHEST, preferred_element_t...  424 us
    psum x1, waiting for transfers between devices, on_device(): totals = lax.psum((acc_re, acc_im), ('gx', 'gy'))  174 us
    dynamic_update_slice x16, local copies, waits for them, and re-layouts, visit(): lax.dynamic_update_slice(grad_ext, old_patch + jnp.stack([grad_re, grad_i...  106 us
    another operation x1, loops' own time, on_device(): final = lax.fori_loop(0, local_slots, visit, start)  85.2 us
    ppermute x4, waiting for transfers between devices, with_halo(): lax.ppermute(tail, axis, [(i, (i + 1) % count) for i in range(ends)])  68 us
    ppermute x4, starting transfers between devices, with_halo(): lax.ppermute(tail, axis, [(i, (i + 1) % count) for i in range(ends)])  26.8 us
    concatenate x2, other arithmetic, with_halo(): jnp.concatenate([lax.ppermute(tail, axis, [(i, (i + 1) % count) for i in...  23.7 us
    unnamed x20, local copies, waits for them, and re-layouts  23.2 us
  transfers between devices with their start and end apart: 9, of which 4 were waited for; matrix products, arithmetic and copies ran while one was open for 2% of the time, Pallas kernels for 0%

commit v1 on v0

v1 whole, which is shorter than its diff:
```python
import functools
import math

import jax
import jax.numpy as jnp
import ml_dtypes
import numpy as np
from jax import lax
from jax.experimental import pallas as pl
from jax.experimental.pallas import tpu as pltpu
from jax.sharding import PartitionSpec as P

M = 256
HALF = 128
TILE = 1024
SLOTS_HERE = 16
ROWS = TILE + 2 * HALF
VMEM = 60 * 1024 * 1024


def split_host(table):
    high = table.astype(ml_dtypes.bfloat16)
    low = (table - high.astype(np.float64)).astype(ml_dtypes.bfloat16)
    return high, low


def host_tables():
    n = np.arange(HALF)
    lefts, rights = [], []
    for odd in (0, 1):
        k = 2 * np.arange(HALF) + odd
        angle = 2.0 * np.pi * (np.outer(k, n) % M) / M
        c, s = np.cos(angle) / 16.0, np.sin(angle) / 16.0
        both = np.block([[c, s], [-s, c]])
        for table in (both, both.T):
            high, low = split_host(table)
            lefts.append(np.concatenate([high, low, high], axis=1))
            rights.append(np.concatenate([high, high, low], axis=0))
    pick = np.zeros((M, M))
    pick[2 * n, n] = 1.0
    pick[2 * n + 1, HALF + n] = 1.0
    pick = pick.astype(ml_dtypes.bfloat16)
    return np.stack(lefts), np.stack(rights), np.concatenate([pick, pick], axis=0)


def halves(x):
    high = x.astype(jnp.bfloat16)
    low = (x - high.astype(jnp.float32)).astype(jnp.bfloat16)
    return high, low


def left_product(table, x):
    high, low = halves(x)
    return jnp.dot(table, jnp.concatenate([high, high, low], axis=0), preferred_element_type=jnp.float32)


def right_product(x, table):
    high, low = halves(x)
    return jnp.dot(jnp.concatenate([high, low, high], axis=1), table, preferred_element_type=jnp.float32)


def visit(obj, grad, probe, seen, slot, lefts, rights, pick, acc, row, block, block_end, shift):
    lane = lax.broadcasted_iota(jnp.int32, (M, HALF), 1)
    wraps = lane < shift
    rows = pl.ds(row, M)

    def window(part):
        first = jnp.where(wraps, obj[part, block_end, rows, :], obj[part, block, rows, :])
        return jnp.concatenate([first, obj[part, block + 1, rows, :]], axis=1)

    obj_re, obj_im = window(0), window(1)
    probe_re = pltpu.roll(probe[0], shift, 1)
    probe_im = pltpu.roll(probe[1], shift, 1)
    wave_re = probe_re * obj_re - probe_im * obj_im
    wave_im = probe_re * obj_im + probe_im * obj_re
    top, low = slice(0, HALF), slice(HALF, M)
    even = left_product(lefts[0], jnp.concatenate([wave_re[top] + wave_re[low], wave_im[top] + wave_im[low]], axis=0))
    odd = left_product(lefts[2], jnp.concatenate([wave_re[top] - wave_re[low], wave_im[top] - wave_im[low]], axis=0))
    half_re = jnp.concatenate([even[top], odd[top]], axis=0)
    half_im = jnp.concatenate([even[low], odd[low]], axis=0)
    far_e = right_product(
        jnp.concatenate([half_re[:, top] + half_re[:, low], half_im[:, top] + half_im[:, low]], axis=1), rights[1]
    )
    far_o = right_product(
        jnp.concatenate([half_re[:, top] - half_re[:, low], half_im[:, top] - half_im[:, low]], axis=1), rights[3]
    )
    meas = jnp.concatenate(
        [
            jnp.concatenate([seen[slot, side, pl.ds(odd, HALF, stride=2), :] for side in range(2)], axis=1)
            for odd in range(2)
        ],
        axis=0,
    )
    meas = jnp.dot(jnp.concatenate(halves(meas), axis=1), pick[...], preferred_element_type=jnp.float32)

    def residual(far, seen):
        squares = far * far
        total = squares[:, top] + squares[:, low] + 1.0
        inverse = lax.rsqrt(total)
        differ = total * inverse - seen
        factor = differ * inverse
        return far * jnp.concatenate([factor, factor], axis=1), differ * differ

    back_e, loss_e = residual(far_e, meas[:, top])
    back_o, loss_o = residual(far_o, meas[:, low])
    loss = jnp.sum(loss_e + loss_o) * (0.5 / (M * M))
    up = right_product(back_e, rights[0])
    vp = right_product(back_o, rights[2])
    plus, minus = up + vp, up - vp
    half_re = jnp.concatenate([plus[:, top], minus[:, top]], axis=1)
    half_im = jnp.concatenate([plus[:, low], minus[:, low]], axis=1)
    up = left_product(lefts[1], jnp.concatenate([half_re[top], half_im[top]], axis=0))
    vp = left_product(lefts[3], jnp.concatenate([half_re[low], half_im[low]], axis=0))
    plus, minus = up + vp, up - vp
    back_re = jnp.concatenate([plus[top], minus[top]], axis=0)
    back_im = jnp.concatenate([plus[low], minus[low]], axis=0)

    grads = (probe_re * back_re + probe_im * back_im, probe_re * back_im - probe_im * back_re)
    for part, g in enumerate(grads):
        first = g[:, top]
        grad[part, block, rows, :] += jnp.where(wraps, 0.0, first)
        grad[part, block + 1, rows, :] += g[:, low]
        grad[part, block_end, rows, :] += jnp.where(wraps, first, 0.0)
    unshift = lax.rem(M - shift, M)
    terms = (obj_re * back_re + obj_im * back_im, obj_re * back_im - obj_im * back_re)
    for part, term in enumerate(terms):
        turned = pltpu.roll(term, unshift, 1)
        acc[part, 0] += turned[:, top]
        acc[part, 1] += turned[:, low]
    return loss


EDGE = slice(HALF, HALF + TILE)
STRIP = (0, 1, 6, 7)
CORE = TILE - 2 * HALF


def start_all(pairs, sems):
    copies = [pltpu.make_async_copy(source, target, sems.at[i]) for i, (source, target) in enumerate(pairs)]
    for copy in copies:
        copy.start()
    return copies


def wait_all(copies):
    for copy in copies:
        copy.wait()


def block_of(ref, index):
    return ref.at[:, :, pl.ds(HALF * index, HALF)]


def tile_pairs(tile, up, down, buffer, slots):
    pairs = []
    for place, block in slots:
        pairs.append((block_of(tile, block), buffer.at[:, place, pl.ds(HALF, TILE)]))
        pairs.append((block_of(up, block), buffer.at[:, place, pl.ds(0, HALF)]))
        pairs.append((block_of(down, block), buffer.at[:, place, pl.ds(HALF + TILE, HALF)]))
    return pairs


def side_pairs(edge, core, above, below, side, buffer, place):
    return [
        (edge.at[:, pl.ds(0, HALF)], buffer.at[:, place, pl.ds(HALF, HALF)]),
        (core, buffer.at[:, place, pl.ds(2 * HALF, CORE)]),
        (edge.at[:, pl.ds(HALF, HALF)], buffer.at[:, place, pl.ds(TILE, HALF)]),
        (block_of(above, side), buffer.at[:, place, pl.ds(0, HALF)]),
        (block_of(below, side), buffer.at[:, place, pl.ds(HALF + TILE, HALF)]),
    ]


def flipped(pairs):
    return [(target, source) for source, target in pairs]


def slot_copies(measured, seen, slot_sems, s):
    return [
        pltpu.make_async_copy(measured.at[s, :, pl.ds(HALF * side, HALF)], seen.at[s, side], slot_sems.at[s, side])
        for side in range(2)
    ]


def fetch_slots(live, centers, wanted, measured, seen, slot_sems):
    def fetch(s, carry):
        @pl.when(wanted(live[s], centers[s, 1]))
        def _():
            for copy in slot_copies(measured, seen, slot_sems, s):
                copy.start()

        return carry

    lax.fori_loop(0, SLOTS_HERE, fetch, 0)


def run_slots(live, centers, wanted, place, measured, seen, slot_sems, losses, body):
    def step(s, carry):
        column = centers[s, 1]

        @pl.when(wanted(live[s], column))
        def _():
            wait_all(slot_copies(measured, seen, slot_sems, s))
            block, block_end, shift = place(column)
            losses[s] = body(s, centers[s, 0], block, block_end, shift)

        return carry

    lax.fori_loop(0, SLOTS_HERE, step, 0)


def is_inner(alive, column):
    return (alive > 0) & (column >= HALF) & (column <= TILE - HALF)


def is_outer(alive, column):
    return (alive > 0) & ((column < HALF) | (column > TILE - HALF))


def inner_kernel(
    centers, live, probe, lefts, rights, pick, field, up, down, measured,
    grad_out, up_out, down_out, acc, losses, obj, grad, seen, sems, slot_sems,
):
    slots = [(j, j) for j in range(8)]
    loads = start_all(tile_pairs(field, up, down, obj, slots), sems)
    fetch_slots(live, centers, is_inner, measured, seen, slot_sems)
    grad[...] = jnp.zeros_like(grad)
    acc[...] = jnp.zeros_like(acc)
    for s in range(SLOTS_HERE):
        losses[s] = 0.0
    wait_all(loads)

    def place(column):
        start = column - HALF
        block = lax.div(start, HALF)
        return block, jnp.minimum(block + 2, 7), lax.rem(start, HALF)

    def body(s, row, block, block_end, shift):
        return visit(obj, grad, probe, seen, s, lefts, rights, pick, acc, row, block, block_end, shift)

    run_slots(live, centers, is_inner, place, measured, seen, slot_sems, losses, body)
    wait_all(start_all(flipped(tile_pairs(grad_out, up_out, down_out, grad, slots)), sems))


def outer_kernel(
    centers, live, probe, lefts, rights, pick, field, up, down, measured,
    left_edge, left_core, right_edge, right_core, above, below, grad_in, up_in, down_in, acc_in, losses_in,
    grad_out, up_out, down_out, acc, losses, gleft_edge, gleft_core, gright_edge, gright_core, gabove, gbelow,
    obj, grad, seen, sems, slot_sems,
):
    slots = list(zip((1, 2, 3, 4), STRIP))
    loads = start_all(
        tile_pairs(field, up, down, obj, slots)
        + side_pairs(left_edge, left_core, above, below, 0, obj, 0)
        + side_pairs(right_edge, right_core, above, below, 1, obj, 5)
        + tile_pairs(grad_in, up_in, down_in, grad, slots),
        sems,
    )
    fetch_slots(live, centers, is_outer, measured, seen, slot_sems)
    for place_at in (0, 5):
        grad[:, place_at] = jnp.zeros((2, ROWS, HALF), jnp.float32)
    acc[...] = acc_in[...]
    for s in range(SLOTS_HERE):
        losses[s] = losses_in[s]
    wait_all(loads)

    def place(column):
        at_left = column < HALF
        block = jnp.where(at_left, 0, 3)
        return block, block + 2, jnp.where(at_left, column, column - (TILE - HALF))

    def body(s, row, block, block_end, shift):
        return visit(obj, grad, probe, seen, s, lefts, rights, pick, acc, row, block, block_end, shift)

    run_slots(live, centers, is_outer, place, measured, seen, slot_sems, losses, body)
    wait_all(
        start_all(
            flipped(
                tile_pairs(grad_out, up_out, down_out, grad, slots)
                + side_pairs(gleft_edge, gleft_core, gabove, gbelow, 0, grad, 0)
                + side_pairs(gright_edge, gright_core, gabove, gbelow, 1, grad, 5)
            ),
            sems,
        )
    )


VMEM_SPEC = pl.BlockSpec(memory_space=pltpu.VMEM)
SMEM_SPEC = pl.BlockSpec(memory_space=pltpu.SMEM)
HBM_SPEC = pl.BlockSpec(memory_space=pl.ANY)


def shaped(*shape):
    return jax.ShapeDtypeStruct(shape, jnp.float32)


def slot_scratch(blocks, copies):
    return [
        pltpu.VMEM((2, blocks, ROWS, HALF), jnp.float32),
        pltpu.VMEM((2, blocks, ROWS, HALF), jnp.float32),
        pltpu.VMEM((SLOTS_HERE, 2, M, HALF), jnp.float32),
        pltpu.SemaphoreType.DMA((copies,)),
        pltpu.SemaphoreType.DMA((SLOTS_HERE, 2)),
    ]


def cost(slots):
    return pl.CostEstimate(flops=slots * 26 * 2 * M**3, bytes_accessed=30 << 20, transcendentals=slots * M * M)


TILE_OUT = (shaped(2, TILE, TILE), shaped(2, HALF, TILE), shaped(2, HALF, TILE), shaped(2, 2, M, HALF), shaped(SLOTS_HERE))


def inner_slots(centers, live, probe, tables, field, up, down, measured):
    return pl.pallas_call(
        inner_kernel,
        out_shape=TILE_OUT,
        in_specs=[SMEM_SPEC] * 2 + [VMEM_SPEC] * 4 + [HBM_SPEC] * 4,
        out_specs=(HBM_SPEC, HBM_SPEC, HBM_SPEC, VMEM_SPEC, SMEM_SPEC),
        scratch_shapes=slot_scratch(8, 24),
        compiler_params=pltpu.CompilerParams(vmem_limit_bytes=VMEM),
        cost_estimate=cost(SLOTS_HERE),
        name="inner_slots",
    )(centers, live, probe, *tables, field, up, down, measured)


def outer_slots(centers, live, probe, tables, field, up, down, measured, halos, partial):
    return pl.pallas_call(
        outer_kernel,
        out_shape=TILE_OUT
        + (shaped(2, 2 * HALF, HALF), shaped(2, CORE, HALF)) * 2
        + (shaped(2, HALF, 2 * HALF),) * 2,
        in_specs=[SMEM_SPEC] * 2 + [VMEM_SPEC] * 4 + [HBM_SPEC] * 4 + [HBM_SPEC] * 9 + [VMEM_SPEC, SMEM_SPEC],
        out_specs=(HBM_SPEC, HBM_SPEC, HBM_SPEC, VMEM_SPEC, SMEM_SPEC) + (HBM_SPEC,) * 6,
        scratch_shapes=slot_scratch(6, 34),
        input_output_aliases={16: 0, 17: 1, 18: 2},
        compiler_params=pltpu.CompilerParams(vmem_limit_bytes=VMEM),
        cost_estimate=cost(SLOTS_HERE // 2),
        name="outer_slots",
    )(centers, live, probe, *tables, field, up, down, measured, *halos, *partial)


def fold_kernel(pieces, *refs):
    sources, (tile, out), (have, got, sems) = refs[: len(pieces)], refs[len(pieces) : len(pieces) + 2], refs[len(pieces) + 2 :]
    pairs, targets = [], []
    for source, (take, at, size, lanes, width, base) in zip(sources, pieces):
        pairs.append((source.at[:, pl.ds(take, size)], got.at[:, pl.ds(base, size)]))
        pairs.append((tile.at[:, pl.ds(at, size), pl.ds(lanes, width)], have.at[:, pl.ds(base, size)]))
        targets.append((have.at[:, pl.ds(base, size)], out.at[:, pl.ds(at, size), pl.ds(lanes, width)]))
    wait_all(start_all(pairs, sems))
    have[...] += got[...]
    wait_all(start_all(targets, sems))


def fold(tile, sources, pieces, rows, width):
    n = len(pieces)
    return pl.pallas_call(
        functools.partial(fold_kernel, pieces),
        out_shape=shaped(2, TILE, TILE),
        in_specs=[HBM_SPEC] * (n + 1),
        out_specs=HBM_SPEC,
        scratch_shapes=[
            pltpu.VMEM((2, rows, width), jnp.float32),
            pltpu.VMEM((2, rows, width), jnp.float32),
            pltpu.SemaphoreType.DMA((2 * n,)),
        ],
        input_output_aliases={n: 0},
        compiler_params=pltpu.CompilerParams(vmem_limit_bytes=VMEM),
        cost_estimate=pl.CostEstimate(flops=2 * rows * width, bytes_accessed=24 * rows * width, transcendentals=0),
        name="fold",
    )(*sources, tile)


MESH = pl.DeviceIdType.MESH
SHARE = 8


def sum_kernel(scale, part, out, first, second, third, kept1, kept2, kept3, full, send_sems, recv_sems):
    gx, gy = lax.axis_index("gx"), lax.axis_index("gy")
    core = lax.rem(gx, 2)
    spot = lax.rem(lax.div(gx, 2), 4)
    upper = lax.div(gx, 8)
    group = upper * 8 + gy

    def at_core(k):
        return (gx - core + k, gy)

    def at_spot(k):
        return (gx + 2 * (k - spot), gy)

    def at_group(k):
        return (gx + 8 * (lax.div(k, 8) - upper), lax.rem(k, 8))

    other = at_core(1 - core)
    spots = [lax.rem(spot + d, 4) for d in range(1, 4)]
    groups = [lax.rem(group + d, 16) for d in range(1, 16)]
    barrier = pltpu.get_barrier_semaphore()
    partners = [other] + [at_spot(k) for k in spots] + [at_group(k) for k in groups]
    for device in partners:
        pl.semaphore_signal(barrier, inc=1, device_id=device, device_id_type=MESH)
    pl.semaphore_wait(barrier, len(partners))

    def rows(start, size):
        return pl.ds(pl.multiple_of(start, 8), size)

    count = [0]

    def send(source, target, device):
        i = count[0]
        count[0] += 1
        copy = pltpu.make_async_remote_copy(
            src_ref=source, dst_ref=target, send_sem=send_sems.at[i], recv_sem=recv_sems.at[i],
            device_id=device, device_id_type=MESH,
        )
        copy.start()
        return copy

    def exchange(copies):
        for copy in copies:
            copy.wait_recv()
        return copies

    sent = exchange([send(part.at[rows((1 - core) * 512, 512)], first, other)])
    kept1[...] = part[rows(core * 512, 512), :] + first[...]
    sent += exchange(
        [send(kept1.at[rows(k * 128, 128)], second.at[d], at_spot(k)) for d, k in enumerate(spots)]
    )
    kept2[...] = kept1[rows(spot * 128, 128), :] + (second[0] + second[1] + second[2])
    sent += exchange(
        [send(kept2.at[rows(k * SHARE, SHARE)], third.at[d], at_group(k)) for d, k in enumerate(groups)]
    )
    total = kept2[rows(group * SHARE, SHARE), :]
    for d in range(15):
        total = total + third[d]
    kept3[...] = total * scale
    mine = rows(core * 512 + spot * 128 + group * SHARE, SHARE)
    full[mine, :] = kept3[...]
    sent += exchange([send(kept3, full.at[mine], at_group(k)) for k in groups])
    quarter = full.at[rows(core * 512 + spot * 128, 128)]
    sent += exchange([send(quarter, quarter, at_spot(k)) for k in spots])
    whole = full.at[rows(core * 512, 512)]
    sent += exchange([send(whole, whole, other)])
    for part_at in range(2):
        for side in range(2):
            out[part_at, :, HALF * side : HALF * (side + 1)] = full[pl.ds((part_at * 2 + side) * M, M), :]
    for copy in sent:
        copy.wait_send()


def sum_everywhere(part, scale):
    copies = 2 * (1 + 3 + 15)
    return pl.pallas_call(
        functools.partial(sum_kernel, scale),
        out_shape=shaped(2, M, M),
        in_specs=[VMEM_SPEC],
        out_specs=VMEM_SPEC,
        scratch_shapes=[
            pltpu.VMEM((512, HALF), jnp.float32),
            pltpu.VMEM((3, 128, HALF), jnp.float32),
            pltpu.VMEM((15, SHARE, HALF), jnp.float32),
            pltpu.VMEM((512, HALF), jnp.float32),
            pltpu.VMEM((128, HALF), jnp.float32),
            pltpu.VMEM((SHARE, HALF), jnp.float32),
            pltpu.VMEM((1024, HALF), jnp.float32),
            pltpu.SemaphoreType.DMA((copies,)),
            pltpu.SemaphoreType.DMA((copies,)),
        ],
        compiler_params=pltpu.CompilerParams(collective_id=0, has_side_effects=True),
        cost_estimate=pl.CostEstimate(flops=M * M * 8, bytes_accessed=16 << 20, transcendentals=0),
        name="sum_everywhere",
    )(part.reshape(1024, HALF))


def shift_by_one(x, axis, forward):
    count = lax.axis_size(axis)
    steps = [(i, i + 1) if forward else (i + 1, i) for i in range(count - 1)]
    return lax.ppermute(x, axis, steps)


def to_right(x):
    return shift_by_one(x, "gy", True)


def to_left(x):
    return shift_by_one(x, "gy", False)


def to_down(x):
    return shift_by_one(x, "gx", True)


def to_up(x):
    return shift_by_one(x, "gx", False)


def ends(strip):
    return jnp.concatenate([strip[:, :HALF], strip[:, TILE - HALF :]], axis=1)


def on_device(field, probe, centers, live, measured):
    tables = tuple(jnp.asarray(t) for t in host_tables())
    first, last = field[:, :, :HALF], field[:, :, TILE - HALF :]
    left_edge, right_edge = to_right(ends(last)), to_left(ends(first))
    left_core, right_core = to_right(last[:, HALF : TILE - HALF]), to_left(first[:, HALF : TILE - HALF])
    up, down = to_down(field[:, TILE - HALF :]), to_up(field[:, :HALF])
    above = to_down(jnp.concatenate([left_edge[:, HALF:], right_edge[:, HALF:]], axis=2))
    below = to_up(jnp.concatenate([left_edge[:, :HALF], right_edge[:, :HALF]], axis=2))
    halos = (left_edge, left_core, right_edge, right_core, above, below)
    partial = inner_slots(centers, live, probe, tables, field, up, down, measured)
    grad, gup, gdown, acc, losses, gle, glc, gre, grc, gabove, gbelow = outer_slots(
        centers, live, probe, tables, field, up, down, measured, halos, partial
    )
    from_right_core, from_left_core = to_left(glc), to_right(grc)
    from_down, from_up = to_up(gabove), to_down(gbelow)
    more_left = jnp.concatenate([from_up[:, :, :HALF], from_down[:, :, :HALF]], axis=1)
    more_right = jnp.concatenate([from_up[:, :, HALF:], from_down[:, :, HALF:]], axis=1)
    from_right_edge, from_left_edge = to_left(gle + more_left), to_right(gre + more_right)
    row_down, row_up = to_up(gup), to_down(gdown)
    slots_all = SLOTS_HERE * lax.axis_size("gx") * lax.axis_size("gy")
    probe_grad = sum_everywhere(acc, 1.0 / math.sqrt(slots_all))
    end = TILE - HALF
    grad = fold(
        grad, (row_up, row_down), ((0, 0, HALF, 0, TILE, 0), (0, end, HALF, 0, TILE, HALF)), 2 * HALF, TILE
    )
    grad = fold(
        grad,
        (from_left_edge, from_left_core, from_left_edge, from_right_edge, from_right_core, from_right_edge),
        (
            (0, 0, HALF, 0, HALF, 0),
            (0, HALF, CORE, 0, HALF, HALF),
            (HALF, end, HALF, 0, HALF, end),
            (0, 0, HALF, end, HALF, TILE),
            (0, HALF, CORE, end, HALF, TILE + HALF),
            (HALF, end, HALF, end, HALF, TILE + end),
        ),
        2 * TILE,
        HALF,
    )
    return grad, probe_grad, losses


def solution(mesh):
    placed = (
        P(None, "gx", "gy"),
        P(),
        P(("gx", "gy"), None),
        P(("gx", "gy")),
        P(("gx", "gy"), None, None),
    )
    return jax.shard_map(
        on_device,
        mesh=mesh,
        in_specs=placed,
        out_specs=(P(None, "gx", "gy"), P(), P(("gx", "gy"))),
        check_vma=False,
    )
```

time: 1070 us -> 206 us (0.19)
  matrix products: 424 us -> 0 us
  waiting for transfers between devices: 242 us -> 10.6 us
  local copies, waits for them, and re-layouts: 180 us -> 11.9 us
  Pallas kernels: 0 us -> 105 us
  loops' own time: 85.2 us -> 0 us
  other arithmetic: 81.3 us -> 6.34 us
  starting transfers between devices: 33.3 us -> 70.2 us
  between operations: 14.2 us -> 1.04 us
    dot_general x256 -> x0, matrix products: 424 us -> none  [product(): jnp.dot(left, right, precision=lax.Precision.HIGHEST, preferred_element_t...]
    psum x1 -> x0, waiting for transfers between devices: 174 us -> none  [on_device(): totals = lax.psum((acc_re, acc_im), ('gx', 'gy'))]
    dynamic_update_slice x16 -> x0, local copies, waits for them, and re-layouts: 106 us -> none  [visit(): lax.dynamic_update_slice(grad_ext, old_patch + jnp.stack([grad_re, grad_i...]
    pallas_call x0 -> x5, Pallas kernels: none -> 105 us  [the longest x1 48.9 us: sum_everywhere(): pl.pallas_call(functools.partial(sum_kernel, scale), out_shape=shaped(2,...]
    another operation x1 -> x0, loops' own time: 85.2 us -> none  [on_device(): final = lax.fori_loop(0, local_slots, visit, start)]
    ppermute x8 -> x16, waiting for transfers between devices: 68.1 us -> 10.6 us  [shift_by_one(): return lax.ppermute(x, axis, steps)]
    add x32 -> x2, other arithmetic: 43.4 us -> 3.36 us  [the longest x1 1.69 us: on_device(): gre + more_right]
    ppermute x8 -> x16, starting transfers between devices: 33.3 us -> 70.2 us  [shift_by_one(): return lax.ppermute(x, axis, steps)]
  transfers between devices with their start and end apart: 9 -> 16, of which waited for: 4 -> 1; matrix products, arithmetic and copies ran while one was open for 2% -> 6% of each run, Pallas kernels for 0% -> 41%
where the time goes in v1:
time: 206 us; the launch traced here: 205 us
  Pallas kernels  105 us (51%)
  starting transfers between devices  70.2 us (34%)
  local copies, waits for them, and re-layouts  11.9 us (6%)
  waiting for transfers between devices  10.6 us (5%)
  other arithmetic  6.34 us (3%)
    ppermute x16, starting transfers between devices, shift_by_one(): return lax.ppermute(x, axis, steps)  70.2 us
    pallas_call x1, Pallas kernels, sum_everywhere(): pl.pallas_call(functools.partial(sum_kernel, scale), out_shape=shaped(2,...  48.9 us
    pallas_call x1, Pallas kernels, inner_slots(): pl.pallas_call(inner_kernel, out_shape=TILE_OUT, in_specs=[SMEM_SPEC] * 2...  32.3 us
    pallas_call x1, Pallas kernels, outer_slots(): pl.pallas_call(outer_kernel, out_shape=TILE_OUT + (shaped(2, 2 * HALF, HA...  16.1 us
    ppermute x16, waiting for transfers between devices, shift_by_one(): return lax.ppermute(x, axis, steps)  10.6 us
    pallas_call x2, Pallas kernels, fold(): pl.pallas_call(functools.partial(fold_kernel, pieces), out_shape=shaped(2...  7.56 us
    unnamed x28, local copies, waits for them, and re-layouts  5.16 us
  transfers between devices with their start and end apart: 16, of which 1 were waited for; matrix products, arithmetic and copies ran while one was open for 6% of the time, Pallas kernels for 41%

profile of v1, /device:TPU:1, one launch (start us, length us, event | category | flops | bytes accessed | tf_op | source)
XLA Modules:
  0.0 204.9 jit_solution(8643814885453369195)
XLA Ops:
  0.6 0.0 copy-start.12
  0.6 1.1 fusion.1
  1.8 0.7 pad_maximum_fusion
  2.5 4.4 %collective-permute-start.2 = (f32[2,256,128]{2,1,0:T(8,128)}, f32[2,256,128]{2,1,0:T(8,128)S(1)}, u32[]{:S(2)}, u32[]{:S(2)}) collective-permute-start(f32[2,256,128]{2,1,0:T(8,128)} %pad_maximum_fusion), channel_id=1, source_target_pairs={{0,1},{1,2},{2,3},{3,4},{4,5},{5,6},{6,7},{8,9},{9,10},{10,11},{11... | collective-permute-start | bytes 786440 | tf_op jit(solution)/shard_map/ppermute | solution.py:476
  6.9 3.1 %fusion.2 = (f32[2,128,1024]{2,1,0:T(8,128)}, f32[2,128,1024]{2,1,0:T(8,128)}) fusion(f32[2,1024,1024]{2,1,0:T(8,128)} %field.3), kind=kLoop, calls=%fused_computation.8 | loop fusion | bytes 4194304 | tf_op jit(solution)/shard_map/slice | solution.py:504
  10.0 2.9 %collective-permute-start.1 = (f32[2,128,1024]{2,1,0:T(8,128)}, f32[2,128,1024]{2,1,0:T(8,128)S(1)}, u32[]{:S(2)}, u32[]{:S(2)}) collective-permute-start(f32[2,128,1024]{2,1,0:T(8,128)} %get-tuple-element.41), channel_id=1, source_target_pairs={{8,0},{16,8},{24,16},{32,24},{40,32},{48,40},{56,48},{64,56},{72,6... | collective-permute-start | bytes 3145736 | tf_op jit(solution)/shard_map/ppermute | solution.py:476
  12.9 3.0 %collective-permute-start = (f32[2,128,1024]{2,1,0:T(8,128)}, f32[2,128,1024]{2,1,0:T(8,128)S(1)}, u32[]{:S(2)}, u32[]{:S(2)}) collective-permute-start(f32[2,128,1024]{2,1,0:T(8,128)} %get-tuple-element.42), channel_id=1, source_target_pairs={{0,8},{8,16},{16,24},{24,32},{32,40},{40,48},{48,56},{56,64},{64,7... | collective-permute-start | bytes 3145736 | tf_op jit(solution)/shard_map/ppermute | solution.py:476
  15.9 0.7 pad_maximum_fusion.1
  16.6 1.3 collective-permute-start.4
  17.9 2.4 %fusion = (f32[2,768,128]{2,1,0:T(8,128)}, f32[2,768,128]{2,1,0:T(8,128)S(1)}) fusion(f32[2,1024,1024]{2,1,0:T(8,128)} %field.3), kind=kLoop, calls=%fused_computation.6 | loop fusion | bytes 3145728 | tf_op jit(solution)/shard_map/slice | solution.py:503
  20.3 1.3 collective-permute-start.5
  21.6 0.0 copy-done.12
  21.6 0.7 copy.17.centers
  22.3 0.0 collective-permute-done.2.left_edge
  22.3 5.5 %collective-permute-start.3 = (f32[2,768,128]{2,1,0:T(8,128)S(1)}, f32[2,768,128]{2,1,0:T(8,128)}, u32[]{:S(2)}, u32[]{:S(2)}) collective-permute-start(f32[2,768,128]{2,1,0:T(8,128)S(1)} %get-tuple-element.36), channel_id=1, source_target_pairs={{0,1},{1,2},{2,3},{3,4},{4,5},{5,6},{6,7},{8,9},{9,10},{10,11},{11... | collective-permute-start | bytes 2359304 | tf_op jit(solution)/shard_map/ppermute | solution.py:476
  27.8 10.6 %collective-permute-done.4.right_edge = f32[2,256,128]{2,1,0:T(8,128)S(1)} collective-permute-done((f32[2,256,128]{2,1,0:T(8,128)}, f32[2,256,128]{2,1,0:T(8,128)S(1)}, u32[]{:S(2)}, u32[]{:S(2)}) %collective-permute-start.4) | collective-permute-done | bytes 262176 | tf_op jit(solution)/shard_map/ppermute | solution.py:476
  38.4 0.8 pad_maximum_fusion.2
  39.2 1.9 collective-permute-start.6
  41.1 0.7 pad_maximum_fusion.3
  41.8 0.0 collective-permute-done.1.down
  41.9 2.4 %collective-permute-start.7 = (f32[2,128,256]{2,1,0:T(8,128)}, f32[2,128,256]{2,1,0:T(8,128)S(1)}, u32[]{:S(2)}, u32[]{:S(2)}) collective-permute-start(f32[2,128,256]{2,1,0:T(8,128)} %pad_maximum_fusion.3), channel_id=1, source_target_pairs={{8,0},{16,8},{24,16},{32,24},{40,32},{48,40},{56,48},{64,56},{72,6... | collective-permute-start | bytes 786440 | tf_op jit(solution)/shard_map/ppermute | solution.py:476
  44.3 0.0 collective-permute-done.up
  44.3 0.0 copy-done.5
  44.3 0.0 copy-start.6
  44.3 1.0 copy-done.6
  45.3 32.3 %inner_slots.1 = (f32[2,1024,1024]{2,1,0:T(8,128)}, f32[2,128,1024]{2,1,0:T(8,128)}, f32[2,128,1024]{2,1,0:T(8,128)}, f32[2,2,256,128]{3,2,1,0:T(8,128)}, f32[16]{0:T(128)}) custom-call(s32[16,2]{1,0:T(8,128)} %copy.17.centers, s32[16]{0:T(128)} %live.3, f32[2,256,256]{2,1,0:T(8,128)} %probe.3, bf16[4,256,768]{2,1,0:T(8,128)(2,1)} %constant.6.clone.lefts, ...), custom_call_target="tpu_custom_call" | custom-call | flops 13958643712 | bytes 31457280 | tf_op jit(solution)/shard_map/inner_slots/pallas_call | solution.py:314
  77.5 0.0 copy-done.3
  77.5 0.0 copy-done.4
  77.6 0.0 collective-permute-done.6.above
  77.6 0.0 copy-start.10
  77.6 0.0 collective-permute-done.7.below
  77.6 0.0 copy-start.11
  77.6 0.0 collective-permute-done.5.right_core
  77.6 0.0 collective-permute-done.3.left_core
  77.6 0.7 copy-done.10
  78.3 0.1 copy-done.11
  78.4 16.1 %outer_slots.1 = (f32[2,1024,1024]{2,1,0:T(8,128)}, f32[2,128,1024]{2,1,0:T(8,128)}, f32[2,128,1024]{2,1,0:T(8,128)}, f32[2,2,256,128]{3,2,1,0:T(8,128)}, f32[16...) custom-call(s32[16,2]{1,0:T(8,128)} %copy.17.centers, ...), custom_call_target="tpu_custom_call", output_to_operand_aliasing={{0}: (16, {}), {1}: (17, {}), {2}: (18, {})} | custom-call | flops 6979321856 | bytes 31457280 | tf_op jit(solution)/shard_map/outer_slots/pallas_call | solution.py:327
  94.5 1.9 collective-permute-start.8
  96.4 1.9 collective-permute-start.14
  98.4 2.5 %collective-permute-start.9 = (f32[2,128,256]{2,1,0:T(8,128)}, f32[2,128,256]{2,1,0:T(8,128)S(1)}, u32[]{:S(2)}, u32[]{:S(2)}) collective-permute-start(f32[2,128,256]{2,1,0:T(8,128)} %get-tuple-element.26), channel_id=1, source_target_pairs={{8,0},{16,8},{24,16},{32,24},{40,32},{48,40},{56,48},{64,56},{72,6... | collective-permute-start | bytes 786440 | tf_op jit(solution)/shard_map/ppermute | solution.py:476
  100.8 4.5 %collective-permute-start.11 = (f32[2,768,128]{2,1,0:T(8,128)}, f32[2,768,128]{2,1,0:T(8,128)S(1)}, u32[]{:S(2)}, u32[]{:S(2)}) collective-permute-start(f32[2,768,128]{2,1,0:T(8,128)} %get-tuple-element.27), channel_id=1, source_target_pairs={{0,1},{1,2},{2,3},{3,4},{4,5},{5,6},{6,7},{8,9},{9,10},{10,11},{11... | collective-permute-start | bytes 2359304 | tf_op jit(solution)/shard_map/ppermute | solution.py:476
  105.3 1.3 collective-permute-start.13
  106.6 0.0 collective-permute-done.8
  106.6 1.9 collective-permute-start.15
  108.6 0.0 collective-permute-done.9
  108.6 1.7 maximum_add_fusion.1
  110.3 1.3 collective-permute-start.12
  111.6 1.7 maximum_add_fusion
  113.3 0.0 collective-permute-done.14.refs_0_
  113.3 32.3 %collective-permute-start.10 = (f32[2,256,128]{2,1,0:T(8,128)}, f32[2,256,128]{2,1,0:T(8,128)S(1)}, u32[]{:S(2)}, u32[]{:S(2)}) collective-permute-start(f32[2,256,128]{2,1,0:T(8,128)} %maximum_add_fusion), channel_id=1, source_target_pairs={{0,1},{1,2},{2,3},{3,4},{4,5},{5,6},{6,7},{8,9},{9,10},{10,11},{11... | collective-permute-start | bytes 786440 | tf_op jit(solution)/shard_map/ppermute | solution.py:476
  145.6 48.9 %sum_everywhere.1 = f32[2,256,256]{2,1,0:T(8,128)} custom-call(f32[1024,128]{1,0:T(8,128)} %bitcast.1), custom_call_target="tpu_custom_call" | custom-call | flops 524288 | bytes 16777216 | tf_op jit(solution)/shard_map/sum_everywhere/pallas_call | solution.py:451
  194.5 0.0 collective-permute-done.15.refs_1_
  194.5 0.9 copy-done.8
  195.4 3.7 %fold.2.refs_6_ = f32[2,1024,1024]{2,1,0:T(8,128)} custom-call(f32[2,128,1024]{2,1,0:T(8,128)} %copy-done.7, f32[2,128,1024]{2,1,0:T(8,128)} %copy-done.8, f32[2,1024,1024]{2,1,0:T(8,128)} %get-tuple-element.32.refs_2_), custom_call_target="tpu_custom_call", output_to_operand_aliasing={{}: (2, {})} | custom-call | flops 524288 | bytes 6291456 | tf_op jit(solution)/shard_map/fold/pallas_call | solution.py:356
  199.2 0.0 collective-permute-done.12.refs_3_.refs_5_
  199.2 0.0 collective-permute-done.10.refs_0_.refs_2_
  199.2 0.0 copy-start.2
  199.2 0.0 collective-permute-done.11.refs_1_
  199.2 0.0 collective-permute-done.13.refs_4_
  199.3 0.6 copy-done.1
  199.9 0.1 copy-done.2
  200.0 0.3 copy-done.9
  200.3 3.8 %fold.3 = f32[2,1024,1024]{2,1,0:T(8,128)} custom-call(f32[2,256,128]{2,1,0:T(8,128)} %copy-done.2, f32[2,768,128]{2,1,0:T(8,128)} %copy-done.9, f32[2,256,128]{2,1,0:T(8,128)} %copy-done.2, f32[2,256,128]{2,1,0:T(8,128)} %copy-done.1, f32[2,768,128]{2,1,0:T(8,128)} %collective-permute-done.13.refs_4_, ...), custom_call_target="tpu_custom_call", output_to_operand_aliasing={{}: (6, {})} | custom-call | flops 524288 | bytes 6291456 | tf_op jit(solution)/shard_map/fold/pallas_call | solution.py:356
  204.1 0.8 copy.24
  (14 shorter events, 0.1 us)
Async XLA Ops:
  0.6 21.0 %copy-start.12 = (s32[16,2]{0,1:T(2,128)S(1)}, s32[16,2]{0,1:T(2,128)}, u32[]{:S(2)}) copy-start(s32[16,2]{0,1:T(2,128)} %param.10) | copy-start | bytes 388
  2.5 19.8 %collective-permute-start.2 = (f32[2,256,128]{2,1,0:T(8,128)}, f32[2,256,128]{2,1,0:T(8,128)S(1)}, u32[]{:S(2)}, u32[]{:S(2)}) collective-permute-start(f32[2,256,128]{2,1,0:T(8,128)} %pad_maximum_fusion), channel_id=1, source_target_pairs={{0,1},{1,2},{2,3},{3,4},{4,5},{5,6},{6,7},{8,9},{9,10},{10,11},{11... | collective-permute-start | bytes 786440 | tf_op jit(solution)/shard_map/ppermute | solution.py:476
  10.0 31.8 %collective-permute-start.1 = (f32[2,128,1024]{2,1,0:T(8,128)}, f32[2,128,1024]{2,1,0:T(8,128)S(1)}, u32[]{:S(2)}, u32[]{:S(2)}) collective-permute-start(f32[2,128,1024]{2,1,0:T(8,128)} %get-tuple-element.41), channel_id=1, source_target_pairs={{8,0},{16,8},{24,16},{32,24},{40,32},{48,40},{56,48},{64,56},{72,6... | collective-permute-start | bytes 3145736 | tf_op jit(solution)/shard_map/ppermute | solution.py:476
  12.9 31.4 %collective-permute-start = (f32[2,128,1024]{2,1,0:T(8,128)}, f32[2,128,1024]{2,1,0:T(8,128)S(1)}, u32[]{:S(2)}, u32[]{:S(2)}) collective-permute-start(f32[2,128,1024]{2,1,0:T(8,128)} %get-tuple-element.42), channel_id=1, source_target_pairs={{0,8},{8,16},{16,24},{24,32},{32,40},{40,48},{48,56},{56,64},{64,7... | collective-permute-start | bytes 3145736 | tf_op jit(solution)/shard_map/ppermute | solution.py:476
  16.6 21.8 %collective-permute-start.4 = (f32[2,256,128]{2,1,0:T(8,128)}, f32[2,256,128]{2,1,0:T(8,128)S(1)}, u32[]{:S(2)}, u32[]{:S(2)}) collective-permute-start(f32[2,256,128]{2,1,0:T(8,128)} %pad_maximum_fusion.1), channel_id=1, source_target_pairs={{1,0},{2,1},{3,2},{4,3},{5,4},{6,5},{7,6},{9,8},{10,9},{11,10},{12... | collective-permute-start | bytes 786440 | tf_op jit(solution)/shard_map/ppermute | solution.py:476
  20.3 57.3 %collective-permute-start.5 = (f32[2,768,128]{2,1,0:T(8,128)}, f32[2,768,128]{2,1,0:T(8,128)}, u32[]{:S(2)}, u32[]{:S(2)}) collective-permute-start(f32[2,768,128]{2,1,0:T(8,128)} %get-tuple-element.35), channel_id=1, source_target_pairs={{1,0},{2,1},{3,2},{4,3},{5,4},{6,5},{7,6},{9,8},{10,9},{11,10},{12... | collective-permute-start | bytes 2359304 | tf_op jit(solution)/shard_map/ppermute | solution.py:476
  22.3 55.3 %copy-start.3 = (f32[2,256,128]{2,1,0:T(8,128)}, f32[2,256,128]{2,1,0:T(8,128)S(1)}, u32[]{:S(2)}) copy-start(f32[2,256,128]{2,1,0:T(8,128)S(1)} %collective-permute-done.2.left_edge) | copy-start | bytes 786436
  22.3 55.3 %collective-permute-start.3 = (f32[2,768,128]{2,1,0:T(8,128)S(1)}, f32[2,768,128]{2,1,0:T(8,128)}, u32[]{:S(2)}, u32[]{:S(2)}) collective-permute-start(f32[2,768,128]{2,1,0:T(8,128)S(1)} %get-tuple-element.36), channel_id=1, source_target_pairs={{0,1},{1,2},{2,3},{3,4},{4,5},{5,6},{6,7},{8,9},{9,10},{10,11},{11... | collective-permute-start | bytes 2359304 | tf_op jit(solution)/shard_map/ppermute | solution.py:476
  38.4 39.2 %copy-start.4 = (f32[2,256,128]{2,1,0:T(8,128)}, f32[2,256,128]{2,1,0:T(8,128)S(1)}, u32[]{:S(2)}) copy-start(f32[2,256,128]{2,1,0:T(8,128)S(1)} %collective-permute-done.4.right_edge) | copy-start | bytes 786436
  39.2 38.4 %collective-permute-start.6 = (f32[2,128,256]{2,1,0:T(8,128)}, f32[2,128,256]{2,1,0:T(8,128)S(1)}, u32[]{:S(2)}, u32[]{:S(2)}) collective-permute-start(f32[2,128,256]{2,1,0:T(8,128)} %pad_maximum_fusion.2), channel_id=1, source_target_pairs={{0,8},{8,16},{16,24},{24,32},{32,40},{40,48},{48,56},{56,64},{64,7... | collective-permute-start | bytes 786440 | tf_op jit(solution)/shard_map/ppermute | solution.py:476
  41.8 2.4 %copy-start.5 = (f32[2,128,1024]{2,1,0:T(8,128)}, f32[2,128,1024]{2,1,0:T(8,128)S(1)}, u32[]{:S(2)}) copy-start(f32[2,128,1024]{2,1,0:T(8,128)S(1)} %collective-permute-done.1.down) | copy-start | bytes 3145732
  41.9 35.7 %collective-permute-start.7 = (f32[2,128,256]{2,1,0:T(8,128)}, f32[2,128,256]{2,1,0:T(8,128)S(1)}, u32[]{:S(2)}, u32[]{:S(2)}) collective-permute-start(f32[2,128,256]{2,1,0:T(8,128)} %pad_maximum_fusion.3), channel_id=1, source_target_pairs={{8,0},{16,8},{24,16},{32,24},{40,32},{48,40},{56,48},{64,56},{72,6... | collective-permute-start | bytes 786440 | tf_op jit(solution)/shard_map/ppermute | solution.py:476
  44.3 1.0 copy-start.6
  77.6 0.7 copy-start.10
  77.6 0.8 copy-start.11
  94.5 12.1 %collective-permute-start.8 = (f32[2,128,256]{2,1,0:T(8,128)}, f32[2,128,256]{2,1,0:T(8,128)S(1)}, u32[]{:S(2)}, u32[]{:S(2)}) collective-permute-start(f32[2,128,256]{2,1,0:T(8,128)} %get-tuple-element.25), channel_id=1, source_target_pairs={{0,8},{8,16},{16,24},{24,32},{32,40},{40,48},{48,56},{56,64},{64,7... | collective-permute-start | bytes 786440 | tf_op jit(solution)/shard_map/ppermute | solution.py:476
  96.4 16.9 %collective-permute-start.14 = (f32[2,128,1024]{2,1,0:T(8,128)}, f32[2,128,1024]{2,1,0:T(8,128)S(1)}, u32[]{:S(2)}, u32[]{:S(2)}) collective-permute-start(f32[2,128,1024]{2,1,0:T(8,128)} %get-tuple-element.30), channel_id=1, source_target_pairs={{0,8},{8,16},{16,24},{24,32},{32,40},{40,48},{48,56},{56,64},{64,7... | collective-permute-start | bytes 3145736 | tf_op jit(solution)/shard_map/ppermute | solution.py:476
  98.4 10.2 %collective-permute-start.9 = (f32[2,128,256]{2,1,0:T(8,128)}, f32[2,128,256]{2,1,0:T(8,128)S(1)}, u32[]{:S(2)}, u32[]{:S(2)}) collective-permute-start(f32[2,128,256]{2,1,0:T(8,128)} %get-tuple-element.26), channel_id=1, source_target_pairs={{8,0},{16,8},{24,16},{32,24},{40,32},{48,40},{56,48},{64,56},{72,6... | collective-permute-start | bytes 786440 | tf_op jit(solution)/shard_map/ppermute | solution.py:476
  100.8 98.4 %collective-permute-start.11 = (f32[2,768,128]{2,1,0:T(8,128)}, f32[2,768,128]{2,1,0:T(8,128)S(1)}, u32[]{:S(2)}, u32[]{:S(2)}) collective-permute-start(f32[2,768,128]{2,1,0:T(8,128)} %get-tuple-element.27), channel_id=1, source_target_pairs={{0,1},{1,2},{2,3},{3,4},{4,5},{5,6},{6,7},{8,9},{9,10},{10,11},{11... | collective-permute-start | bytes 2359304 | tf_op jit(solution)/shard_map/ppermute | solution.py:476
  105.3 93.9 %collective-permute-start.13 = (f32[2,768,128]{2,1,0:T(8,128)}, f32[2,768,128]{2,1,0:T(8,128)}, u32[]{:S(2)}, u32[]{:S(2)}) collective-permute-start(f32[2,768,128]{2,1,0:T(8,128)} %get-tuple-element.29), channel_id=1, source_target_pairs={{1,0},{2,1},{3,2},{4,3},{5,4},{6,5},{7,6},{9,8},{10,9},{11,10},{12... | collective-permute-start | bytes 2359304 | tf_op jit(solution)/shard_map/ppermute | solution.py:476
  106.6 87.8 %collective-permute-start.15 = (f32[2,128,1024]{2,1,0:T(8,128)}, f32[2,128,1024]{2,1,0:T(8,128)S(1)}, u32[]{:S(2)}, u32[]{:S(2)}) collective-permute-start(f32[2,128,1024]{2,1,0:T(8,128)} %get-tuple-element.31), channel_id=1, source_target_pairs={{8,0},{16,8},{24,16},{32,24},{40,32},{48,40},{56,48},{64,56},{72,6... | collective-permute-start | bytes 3145736 | tf_op jit(solution)/shard_map/ppermute | solution.py:476
  110.3 88.9 %collective-permute-start.12 = (f32[2,256,128]{2,1,0:T(8,128)}, f32[2,256,128]{2,1,0:T(8,128)S(1)}, u32[]{:S(2)}, u32[]{:S(2)}) collective-permute-start(f32[2,256,128]{2,1,0:T(8,128)} %maximum_add_fusion.1), channel_id=1, source_target_pairs={{1,0},{2,1},{3,2},{4,3},{5,4},{6,5},{7,6},{9,8},{10,9},{11,10},{12... | collective-permute-start | bytes 786440 | tf_op jit(solution)/shard_map/ppermute | solution.py:476
  113.3 81.2 %copy-start.7 = (f32[2,128,1024]{2,1,0:T(8,128)}, f32[2,128,1024]{2,1,0:T(8,128)S(1)}, u32[]{:S(2)}) copy-start(f32[2,128,1024]{2,1,0:T(8,128)S(1)} %collective-permute-done.14.refs_0_) | copy-start | bytes 3145732
  113.3 85.9 %collective-permute-start.10 = (f32[2,256,128]{2,1,0:T(8,128)}, f32[2,256,128]{2,1,0:T(8,128)S(1)}, u32[]{:S(2)}, u32[]{:S(2)}) collective-permute-start(f32[2,256,128]{2,1,0:T(8,128)} %maximum_add_fusion), channel_id=1, source_target_pairs={{0,1},{1,2},{2,3},{3,4},{4,5},{5,6},{6,7},{8,9},{9,10},{10,11},{11... | collective-permute-start | bytes 786440 | tf_op jit(solution)/shard_map/ppermute | solution.py:476
  194.5 1.0 copy-start.8
  199.2 4.9 %copy-start = (f32[2,256,256]{2,1,0:T(8,128)S(1)}, f32[2,256,256]{2,1,0:T(8,128)}, u32[]{:S(2)}) copy-start(f32[2,256,256]{2,1,0:T(8,128)} %sum_everywhere.1) | copy-start | bytes 1572868
  199.2 0.7 copy-start.1
  199.2 0.8 copy-start.2
  199.2 1.0 copy-start.9

commit v2 on v1

--- a/solution.py
+++ b/solution.py
@@ -160,11 +160,19 @@
     return pairs
 
 
-def side_pairs(edge, core, above, below, side, buffer, place):
+def halo_pairs(edge, core, above, below, side, buffer, place):
     return [
         (edge.at[:, pl.ds(0, HALF)], buffer.at[:, place, pl.ds(HALF, HALF)]),
         (core, buffer.at[:, place, pl.ds(2 * HALF, CORE)]),
         (edge.at[:, pl.ds(HALF, HALF)], buffer.at[:, place, pl.ds(TILE, HALF)]),
+        (block_of(above, side), buffer.at[:, place, pl.ds(0, HALF)]),
+        (block_of(below, side), buffer.at[:, place, pl.ds(HALF + TILE, HALF)]),
+    ]
+
+
+def strip_pairs(strip, above, below, side, buffer, place):
+    return [
+        (strip, buffer.at[:, place, pl.ds(HALF, TILE)]),
         (block_of(above, side), buffer.at[:, place, pl.ds(0, HALF)]),
         (block_of(below, side), buffer.at[:, place, pl.ds(HALF + TILE, HALF)]),
     ]
@@ -244,14 +252,14 @@
 def outer_kernel(
     centers, live, probe, lefts, rights, pick, field, up, down, measured,
     left_edge, left_core, right_edge, right_core, above, below, grad_in, up_in, down_in, acc_in, losses_in,
-    grad_out, up_out, down_out, acc, losses, gleft_edge, gleft_core, gright_edge, gright_core, gabove, gbelow,
+    grad_out, up_out, down_out, acc, losses, gleft, gright, gabove, gbelow,
     obj, grad, seen, sems, slot_sems,
 ):
     slots = list(zip((1, 2, 3, 4), STRIP))
     loads = start_all(
         tile_pairs(field, up, down, obj, slots)
-        + side_pairs(left_edge, left_core, above, below, 0, obj, 0)
-        + side_pairs(right_edge, right_core, above, below, 1, obj, 5)
+        + halo_pairs(left_edge, left_core, above, below, 0, obj, 0)
+        + halo_pairs(right_edge, right_core, above, below, 1, obj, 5)
         + tile_pairs(grad_in, up_in, down_in, grad, slots),
         sems,
     )
@@ -276,8 +284,8 @@
         start_all(
             flipped(
                 tile_pairs(grad_out, up_out, down_out, grad, slots)
-                + side_pairs(gleft_edge, gleft_core, gabove, gbelow, 0, grad, 0)
-                + side_pairs(gright_edge, gright_core, gabove, gbelow, 1, grad, 5)
+                + strip_pairs(gleft, gabove, gbelow, 0, grad, 0)
+                + strip_pairs(gright, gabove, gbelow, 1, grad, 5)
             ),
             sems,
         )
@@ -327,10 +335,10 @@
     return pl.pallas_call(
         outer_kernel,
         out_shape=TILE_OUT
-        + (shaped(2, 2 * HALF, HALF), shaped(2, CORE, HALF)) * 2
+        + (shaped(2, TILE, HALF),) * 2
         + (shaped(2, HALF, 2 * HALF),) * 2,
         in_specs=[SMEM_SPEC] * 2 + [VMEM_SPEC] * 4 + [HBM_SPEC] * 4 + [HBM_SPEC] * 9 + [VMEM_SPEC, SMEM_SPEC],
-        out_specs=(HBM_SPEC, HBM_SPEC, HBM_SPEC, VMEM_SPEC, SMEM_SPEC) + (HBM_SPEC,) * 6,
+        out_specs=(HBM_SPEC, HBM_SPEC, HBM_SPEC, VMEM_SPEC, SMEM_SPEC) + (HBM_SPEC,) * 4,
         scratch_shapes=slot_scratch(6, 34),
         input_output_aliases={16: 0, 17: 1, 18: 2},
         compiler_params=pltpu.CompilerParams(vmem_limit_bytes=VMEM),
@@ -339,50 +347,32 @@
     )(centers, live, probe, *tables, field, up, down, measured, *halos, *partial)
 
 
-def fold_kernel(pieces, *refs):
-    sources, (tile, out), (have, got, sems) = refs[: len(pieces)], refs[len(pieces) : len(pieces) + 2], refs[len(pieces) + 2 :]
-    pairs, targets = [], []
-    for source, (take, at, size, lanes, width, base) in zip(sources, pieces):
-        pairs.append((source.at[:, pl.ds(take, size)], got.at[:, pl.ds(base, size)]))
-        pairs.append((tile.at[:, pl.ds(at, size), pl.ds(lanes, width)], have.at[:, pl.ds(base, size)]))
-        targets.append((have.at[:, pl.ds(base, size)], out.at[:, pl.ds(at, size), pl.ds(lanes, width)]))
-    wait_all(start_all(pairs, sems))
-    have[...] += got[...]
-    wait_all(start_all(targets, sems))
-
-
-def fold(tile, sources, pieces, rows, width):
-    n = len(pieces)
-    return pl.pallas_call(
-        functools.partial(fold_kernel, pieces),
-        out_shape=shaped(2, TILE, TILE),
-        in_specs=[HBM_SPEC] * (n + 1),
-        out_specs=HBM_SPEC,
-        scratch_shapes=[
-            pltpu.VMEM((2, rows, width), jnp.float32),
-            pltpu.VMEM((2, rows, width), jnp.float32),
-            pltpu.SemaphoreType.DMA((2 * n,)),
-        ],
-        input_output_aliases={n: 0},
-        compiler_params=pltpu.CompilerParams(vmem_limit_bytes=VMEM),
-        cost_estimate=pl.CostEstimate(flops=2 * rows * width, bytes_accessed=24 * rows * width, transcendentals=0),
-        name="fold",
-    )(*sources, tile)
-
-
 MESH = pl.DeviceIdType.MESH
 SHARE = 8
-
-
-def sum_kernel(scale, part, out, first, second, third, kept1, kept2, kept3, full, send_sems, recv_sems):
+PIECES = CORE // HALF
+ROW_PIECES = 4
+ROW_STEP = HALF // ROW_PIECES
+
+
+def return_kernel(
+    scale, gleft, gright, gabove, gbelow, gup, gdown, part,
+    got_left, got_right, got_up, got_down, out,
+    first, second, third, kept1, kept2, kept3, full, edges, from_up, from_down, relay,
+    sum_send, sum_recv, strip_send, strip_recv, row_send, row_recv, relay_send, relay_recv, corner_send, corner_recv, local,
+):
     gx, gy = lax.axis_index("gx"), lax.axis_index("gy")
     core = lax.rem(gx, 2)
     spot = lax.rem(lax.div(gx, 2), 4)
     upper = lax.div(gx, 8)
     group = upper * 8 + gy
-
-    def at_core(k):
-        return (gx - core + k, gy)
+    odd = lax.rem(gy, 2)
+    has_up, has_down, has_left, has_right = gx > 0, gx < 15, gy > 0, gy < 7
+    crosses = gx == 8
+    relays = ((gx == 7) & (odd == 1)) | ((gx == 8) & (odd == 0))
+    cross_target = (jnp.where(odd == 0, 7, 8), jnp.where(odd == 0, gy + 1, gy - 1))
+    relay_target = (7, jnp.where(gx == 7, gy - 1, gy + 1))
+    up, down, left, right = (gx - 1, gy), (gx + 1, gy), (gx, gy - 1), (gx, gy + 1)
+    far_pair = (15 - gx, jnp.where(gx == 7, gy - 1, gy + 1))
 
     def at_spot(k):
         return (gx + 2 * (k - spot), gy)
@@ -390,14 +380,97 @@
     def at_group(k):
         return (gx + 8 * (lax.div(k, 8) - upper), lax.rem(k, 8))
 
-    other = at_core(1 - core)
+    other = (gx + 1 - 2 * core, gy)
     spots = [lax.rem(spot + d, 4) for d in range(1, 4)]
     groups = [lax.rem(group + d, 16) for d in range(1, 16)]
     barrier = pltpu.get_barrier_semaphore()
-    partners = [other] + [at_spot(k) for k in spots] + [at_group(k) for k in groups]
-    for device in partners:
+
+    def greet(device):
         pl.semaphore_signal(barrier, inc=1, device_id=device, device_id_type=MESH)
-    pl.semaphore_wait(barrier, len(partners))
+
+    sides = ((has_up, up), (has_down, down), (has_left, left), (has_right, right), (relays, far_pair))
+    for there, device in sides:
+        pl.when(there)(functools.partial(greet, device))
+    always = [other] + [at_spot(k) for k in spots] + [at_group(k) for k in groups]
+    for device in always:
+        greet(device)
+    expected = len(always)
+    for there, _ in sides:
+        expected = expected + there.astype(jnp.int32)
+    pl.semaphore_wait(barrier, expected)
+
+    def remote(source, target, send_sem, recv_sem, device):
+        return pltpu.make_async_remote_copy(
+            src_ref=source, dst_ref=target, send_sem=send_sem, recv_sem=recv_sem, device_id=device, device_id_type=MESH
+        )
+
+    corner_up = remote(gabove, from_down, corner_send.at[0], corner_recv.at[0], up)
+    corner_down = remote(gbelow, from_up, corner_send.at[1], corner_recv.at[1], down)
+    pl.when(has_up)(corner_up.start)
+    pl.when(has_down)(corner_down.start)
+    strips = (gleft, gright)
+    loads = [
+        pltpu.make_async_copy(strips[side].at[:, pl.ds(at, HALF)], edges.at[side, :, pl.ds(to, HALF)], local.at[2 * side + i])
+        for side in range(2)
+        for i, (at, to) in enumerate(((0, 0), (TILE - HALF, HALF)))
+    ]
+    for copy in loads:
+        copy.start()
+
+    def strip_copy(side, piece):
+        if piece < PIECES:
+            source = strips[side].at[:, pl.ds(HALF * (piece + 1), HALF)]
+            place = HALF * (piece + 1)
+        else:
+            end = piece - PIECES
+            source = edges.at[side, :, pl.ds(HALF * end, HALF)]
+            place = (TILE - HALF) * end
+        target = (got_right, got_left)[side].at[:, pl.ds(place, HALF)]
+        return remote(source, target, strip_send.at[side, piece], strip_recv.at[side, piece], (left, right)[side])
+
+    def strip_start(piece):
+        pl.when(has_left)(lambda: strip_copy(0, piece).start())
+        pl.when(has_right)(lambda: strip_copy(1, piece).start())
+
+    def strip_sent(piece):
+        pl.when(has_left)(lambda: strip_copy(0, piece).wait_send())
+        pl.when(has_right)(lambda: strip_copy(1, piece).wait_send())
+
+    def strip_got(piece):
+        pl.when(has_right)(lambda: strip_copy(0, piece).wait_recv())
+        pl.when(has_left)(lambda: strip_copy(1, piece).wait_recv())
+
+    def row_rows(piece):
+        return pl.ds(ROW_STEP * piece, ROW_STEP)
+
+    def row_up(piece, direct):
+        source = gup.at[:, row_rows(piece)]
+        if direct:
+            return remote(source, got_down.at[:, row_rows(piece)], row_send.at[0, piece], row_recv.at[0, piece], up)
+        return remote(source, relay.at[:, row_rows(piece)], row_send.at[0, piece], relay_recv.at[piece], cross_target)
+
+    def row_forward(piece):
+        return remote(
+            relay.at[:, row_rows(piece)], got_down.at[:, row_rows(piece)], relay_send.at[piece], row_recv.at[0, piece], relay_target
+        )
+
+    def row_down(piece):
+        rows = row_rows(piece)
+        return remote(gdown.at[:, rows], got_up.at[:, rows], row_send.at[1, piece], row_recv.at[1, piece], down)
+
+    straight = has_up & (gx != 8)
+
+    def row_start(piece):
+        pl.when(straight)(lambda: row_up(piece, True).start())
+        pl.when(crosses)(lambda: row_up(piece, False).start())
+        pl.when(has_down)(lambda: row_down(piece).start())
+
+    def relay_on(piece):
+        def go():
+            row_up(piece, False).wait_recv()
+            row_forward(piece).start()
+
+        pl.when(relays)(go)
 
     def rows(start, size):
         return pl.ds(pl.multiple_of(start, 8), size)
@@ -407,52 +480,103 @@
     def send(source, target, device):
         i = count[0]
         count[0] += 1
-        copy = pltpu.make_async_remote_copy(
-            src_ref=source, dst_ref=target, send_sem=send_sems.at[i], recv_sem=recv_sems.at[i],
-            device_id=device, device_id_type=MESH,
-        )
+        copy = remote(source, target, sum_send.at[i], sum_recv.at[i], device)
         copy.start()
         return copy
 
-    def exchange(copies):
+    def arrive(copies):
         for copy in copies:
             copy.wait_recv()
-        return copies
-
-    sent = exchange([send(part.at[rows((1 - core) * 512, 512)], first, other)])
+
+    strip_start(0)
+    stage = [send(part.at[rows((1 - core) * 512, 512)], first, other)]
+    sent = list(stage)
+    row_start(0)
+    strip_start(1)
+    arrive(stage)
     kept1[...] = part[rows(core * 512, 512), :] + first[...]
-    sent += exchange(
-        [send(kept1.at[rows(k * 128, 128)], second.at[d], at_spot(k)) for d, k in enumerate(spots)]
-    )
+    stage = [send(kept1.at[rows(k * 128, 128)], second.at[d], at_spot(k)) for d, k in enumerate(spots)]
+    sent += stage
+    for copy in loads:
+        copy.wait()
+
+    @pl.when(has_down)
+    def _():
+        corner_up.wait_recv()
+        for side in range(2):
+            edges[side, :, HALF:] += from_down[:, :, HALF * side : HALF * (side + 1)]
+
+    @pl.when(has_up)
+    def _():
+        corner_down.wait_recv()
+        for side in range(2):
+            edges[side, :, :HALF] += from_up[:, :, HALF * side : HALF * (side + 1)]
+
+    row_start(1)
+    strip_start(2)
+    strip_sent(0)
+    arrive(stage)
     kept2[...] = kept1[rows(spot * 128, 128), :] + (second[0] + second[1] + second[2])
-    sent += exchange(
-        [send(kept2.at[rows(k * SHARE, SHARE)], third.at[d], at_group(k)) for d, k in enumerate(groups)]
-    )
+    stage = [send(kept2.at[rows(k * SHARE, SHARE)], third.at[d], at_group(k)) for d, k in enumerate(groups)]
+    sent += stage
+    relay_on(0)
+    row_start(2)
+    strip_start(3)
+    strip_sent(1)
+    arrive(stage)
     total = kept2[rows(group * SHARE, SHARE), :]
     for d in range(15):
         total = total + third[d]
     kept3[...] = total * scale
     mine = rows(core * 512 + spot * 128 + group * SHARE, SHARE)
     full[mine, :] = kept3[...]
-    sent += exchange([send(kept3, full.at[mine], at_group(k)) for k in groups])
+    stage = [send(kept3, full.at[mine], at_group(k)) for k in groups]
+    sent += stage
+    relay_on(1)
+    row_start(3)
+    strip_start(4)
+    strip_sent(2)
+    arrive(stage)
     quarter = full.at[rows(core * 512 + spot * 128, 128)]
-    sent += exchange([send(quarter, quarter, at_spot(k)) for k in spots])
+    stage = [send(quarter, quarter, at_spot(k)) for k in spots]
+    sent += stage
+    relay_on(2)
+    strip_start(5)
+    strip_sent(3)
+    arrive(stage)
     whole = full.at[rows(core * 512, 512)]
-    sent += exchange([send(whole, whole, other)])
+    stage = [send(whole, whole, other)]
+    sent += stage
+    relay_on(3)
+    strip_start(6)
+    strip_start(7)
+    arrive(stage)
     for part_at in range(2):
         for side in range(2):
             out[part_at, :, HALF * side : HALF * (side + 1)] = full[pl.ds((part_at * 2 + side) * M, M), :]
+    for piece in range(4, PIECES + 2):
+        strip_sent(piece)
+    for piece in range(PIECES + 2):
+        strip_got(piece)
+    for piece in range(ROW_PIECES):
+        pl.when(has_down)(lambda: row_down(piece).wait_send())
+        pl.when(has_up)(lambda: row_up(piece, True).wait_send())
+        pl.when(relays)(lambda: row_forward(piece).wait_send())
+        pl.when(has_down)(lambda: row_up(piece, True).wait_recv())
+        pl.when(has_up)(lambda: row_down(piece).wait_recv())
+    pl.when(has_up)(corner_up.wait_send)
+    pl.when(has_down)(corner_down.wait_send)
     for copy in sent:
         copy.wait_send()
 
 
-def sum_everywhere(part, scale):
+def send_back(gleft, gright, gabove, gbelow, gup, gdown, part, scale):
     copies = 2 * (1 + 3 + 15)
     return pl.pallas_call(
-        functools.partial(sum_kernel, scale),
-        out_shape=shaped(2, M, M),
-        in_specs=[VMEM_SPEC],
-        out_specs=VMEM_SPEC,
+        functools.partial(return_kernel, scale),
+        out_shape=(shaped(2, TILE, HALF),) * 2 + (shaped(2, HALF, TILE),) * 2 + (shaped(2, M, M),),
+        in_specs=[HBM_SPEC] * 6 + [VMEM_SPEC],
+        out_specs=(HBM_SPEC,) * 4 + (VMEM_SPEC,),
         scratch_shapes=[
             pltpu.VMEM((512, HALF), jnp.float32),
             pltpu.VMEM((3, 128, HALF), jnp.float32),
@@ -461,13 +585,80 @@
             pltpu.VMEM((128, HALF), jnp.float32),
             pltpu.VMEM((SHARE, HALF), jnp.float32),
             pltpu.VMEM((1024, HALF), jnp.float32),
+            pltpu.VMEM((2, 2, 2 * HALF, HALF), jnp.float32),
+            pltpu.VMEM((2, HALF, 2 * HALF), jnp.float32),
+            pltpu.VMEM((2, HALF, 2 * HALF), jnp.float32),
+            pltpu.VMEM((2, HALF, TILE), jnp.float32),
             pltpu.SemaphoreType.DMA((copies,)),
             pltpu.SemaphoreType.DMA((copies,)),
+            pltpu.SemaphoreType.DMA((2, PIECES + 2)),
+            pltpu.SemaphoreType.DMA((2, PIECES + 2)),
+            pltpu.SemaphoreType.DMA((2, ROW_PIECES)),
+            pltpu.SemaphoreType.DMA((2, ROW_PIECES)),
+            pltpu.SemaphoreType.DMA((ROW_PIECES,)),
+            pltpu.SemaphoreType.DMA((ROW_PIECES,)),
+            pltpu.SemaphoreType.DMA((2,)),
+            pltpu.SemaphoreType.DMA((2,)),
+            pltpu.SemaphoreType.DMA((4,)),
         ],
-        compiler_params=pltpu.CompilerParams(collective_id=0, has_side_effects=True),
-        cost_estimate=pl.CostEstimate(flops=M * M * 8, bytes_accessed=16 << 20, transcendentals=0),
-        name="sum_everywhere",
-    )(part.reshape(1024, HALF))
+        compiler_params=pltpu.CompilerParams(collective_id=0, has_side_effects=True, vmem_limit_bytes=VMEM),
+        cost_estimate=pl.CostEstimate(flops=M * M * 8, bytes_accessed=100 << 20, transcendentals=0),
+        name="send_back",
+    )(gleft, gright, gabove, gbelow, gup, gdown, part.reshape(1024, HALF))
+
+
+def fold_kernel(got_left, got_right, got_up, got_down, tile, out, band, side_band, row_in, strip_in, sems):
+    gx, gy = lax.axis_index("gx"), lax.axis_index("gy")
+    end = TILE - HALF
+    frame = [
+        (tile.at[:, pl.ds(0, HALF)], band.at[0]),
+        (tile.at[:, pl.ds(end, HALF)], band.at[1]),
+        (tile.at[:, pl.ds(HALF, CORE), pl.ds(0, HALF)], side_band.at[0]),
+        (tile.at[:, pl.ds(HALF, CORE), pl.ds(end, HALF)], side_band.at[1]),
+    ]
+    arrived = [(got_up, row_in.at[0]), (got_down, row_in.at[1]), (got_left, strip_in.at[0]), (got_right, strip_in.at[1])]
+    loads = start_all(frame + arrived, sems)
+    wait_all(loads)
+    for i, there in enumerate((gx > 0, gx < 15)):
+        @pl.when(there)
+        def _():
+            band[i] += row_in[i]
+
+    for i, there in enumerate((gy > 0, gy < 7)):
+        lanes = slice(end * i, end * i + HALF)
+
+        @pl.when(there)
+        def _():
+            band[0, :, :, lanes] += strip_in[i, :, :HALF]
+            side_band[i] += strip_in[i, :, HALF:end]
+            band[1, :, :, lanes] += strip_in[i, :, end:]
+
+    back = [
+        (band.at[0], out.at[:, pl.ds(0, HALF)]),
+        (band.at[1], out.at[:, pl.ds(end, HALF)]),
+        (side_band.at[0], out.at[:, pl.ds(HALF, CORE), pl.ds(0, HALF)]),
+        (side_band.at[1], out.at[:, pl.ds(HALF, CORE), pl.ds(end, HALF)]),
+    ]
+    wait_all(start_all(back, sems))
+
+
+def fold(tile, got_left, got_right, got_up, got_down):
+    return pl.pallas_call(
+        fold_kernel,
+        out_shape=shaped(2, TILE, TILE),
+        in_specs=[HBM_SPEC] * 5,
+        out_specs=HBM_SPEC,
+        scratch_shapes=[
+            pltpu.VMEM((2, 2, HALF, TILE), jnp.float32),
+            pltpu.VMEM((2, 2, CORE, HALF), jnp.float32),
+            pltpu.VMEM((2, 2, HALF, TILE), jnp.float32),
+            pltpu.VMEM((2, 2, TILE, HALF), jnp.float32),
+            pltpu.SemaphoreType.DMA((8,)),
+        ],
+        input_output_aliases={4: 0},
+        compiler_params=pltpu.CompilerParams(vmem_limit_bytes=VMEM),
+        name="fold",
+    )(got_left, got_right, got_up, got_down, tile)
 
 
 def shift_by_one(x, axis, forward):
@@ -490,6 +681,21 @@
 
 def to_up(x):
     return shift_by_one(x, "gx", False)
+
+
+def joint(x, pairs):
+    return lax.ppermute(x, ("gx", "gy"), [(8 * a + b, 8 * c + d) for (a, b), (c, d) in pairs])
+
+
+def to_up_relayed(x):
+    straight = lax.ppermute(x, "gx", [(i + 1, i) for i in range(15) if i != 7])
+    once = joint(
+        x, [((8, 2 * y), (7, 2 * y + 1)) for y in range(4)] + [((8, 2 * y + 1), (8, 2 * y)) for y in range(4)]
+    )
+    twice = joint(
+        once, [((7, 2 * y + 1), (7, 2 * y)) for y in range(4)] + [((8, 2 * y), (7, 2 * y + 1)) for y in range(4)]
+    )
+    return straight + twice
 
 
 def ends(strip):
@@ -501,41 +707,17 @@
     first, last = field[:, :, :HALF], field[:, :, TILE - HALF :]
     left_edge, right_edge = to_right(ends(last)), to_left(ends(first))
     left_core, right_core = to_right(last[:, HALF : TILE - HALF]), to_left(first[:, HALF : TILE - HALF])
-    up, down = to_down(field[:, TILE - HALF :]), to_up(field[:, :HALF])
+    up, down = to_down(field[:, TILE - HALF :]), to_up_relayed(field[:, :HALF])
     above = to_down(jnp.concatenate([left_edge[:, HALF:], right_edge[:, HALF:]], axis=2))
     below = to_up(jnp.concatenate([left_edge[:, :HALF], right_edge[:, :HALF]], axis=2))
     halos = (left_edge, left_core, right_edge, right_core, above, below)
     partial = inner_slots(centers, live, probe, tables, field, up, down, measured)
-    grad, gup, gdown, acc, losses, gle, glc, gre, grc, gabove, gbelow = outer_slots(
+    grad, gup, gdown, acc, losses, gleft, gright, gabove, gbelow = outer_slots(
         centers, live, probe, tables, field, up, down, measured, halos, partial
     )
-    from_right_core, from_left_core = to_left(glc), to_right(grc)
-    from_down, from_up = to_up(gabove), to_down(gbelow)
-    more_left = jnp.concatenate([from_up[:, :, :HALF], from_down[:, :, :HALF]], axis=1)
-    more_right = jnp.concatenate([from_up[:, :, HALF:], from_down[:, :, HALF:]], axis=1)
-    from_right_edge, from_left_edge = to_left(gle + more_left), to_right(gre + more_right)
-    row_down, row_up = to_up(gup), to_down(gdown)
     slots_all = SLOTS_HERE * lax.axis_size("gx") * lax.axis_size("gy")
-    probe_grad = sum_everywhere(acc, 1.0 / math.sqrt(slots_all))
-    end = TILE - HALF
-    grad = fold(
-        grad, (row_up, row_down), ((0, 0, HALF, 0, TILE, 0), (0, end, HALF, 0, TILE, HALF)), 2 * HALF, TILE
-    )
-    grad = fold(
-        grad,
-        (from_left_edge, from_left_core, from_left_edge, from_right_edge, from_right_core, from_right_edge),
-        (
-            (0, 0, HALF, 0, HALF, 0),
-            (0, HALF, CORE, 0, HALF, HALF),
-            (HALF, end, HALF, 0, HALF, end),
-            (0, 0, HALF, end, HALF, TILE),
-            (0, HALF, CORE, end, HALF, TILE + HALF),
-            (HALF, end, HALF, end, HALF, TILE + end),
-        ),
-        2 * TILE,
-        HALF,
-    )
-    return grad, probe_grad, losses
+    *got, probe_grad = send_back(gleft, gright, gabove, gbelow, gup, gdown, acc, 1.0 / math.sqrt(slots_all))
+    return fold(grad, *got), probe_grad, losses
 
 
 def solution(mesh):

time: 206 us -> 201 us (0.976)
  the two profiles are of different devices: /device:TPU:1 before, /device:TPU:12 now
where the time goes in v2:
time: 201 us; the launch traced here: 200 us
  Pallas kernels  150 us (75%)
  starting transfers between devices  26.3 us (13%)
  local copies, waits for them, and re-layouts  9.29 us (5%)
  waiting for transfers between devices  8.2 us (4%)
  other arithmetic  5.25 us (3%)
    pallas_call x1, Pallas kernels, send_back(): pl.pallas_call(functools.partial(return_kernel, scale), out_shape=(shaped...  119 us
    ppermute x7, starting transfers between devices, shift_by_one(): return lax.ppermute(x, axis, steps)  21.1 us
    pallas_call x1, Pallas kernels, inner_slots(): pl.pallas_call(inner_kernel, out_shape=TILE_OUT, in_specs=[SMEM_SPEC] * 2...  13.8 us
    pallas_call x1, Pallas kernels, outer_slots(): pl.pallas_call(outer_kernel, out_shape=TILE_OUT + (shaped(2, TILE, HALF),...  11.7 us
    ppermute x7, waiting for transfers between devices, shift_by_one(): return lax.ppermute(x, axis, steps)  8.19 us
    pallas_call x1, Pallas kernels, fold(): pl.pallas_call(fold_kernel, out_shape=shaped(2, TILE, TILE), in_specs=[HB...  5.71 us
  transfers between devices with their start and end apart: 10, of which 2 were waited for; matrix products, arithmetic and copies ran while one was open for 5% of the time, Pallas kernels for 7%

profile of v2, /device:TPU:12, one launch (start us, length us, event | category | flops | bytes accessed | tf_op | source)
XLA Modules:
  0.0 200.3 jit_solution(5302472561334407283)
XLA Ops:
  0.6 0.0 copy-start.6
  0.6 3.1 %fusion.2 = (f32[2,128,1024]{2,1,0:T(8,128)}, f32[2,128,1024]{2,1,0:T(8,128)}) fusion(f32[2,1024,1024]{2,1,0:T(8,128)} %field.3), kind=kLoop, calls=%fused_computation.6 | loop fusion | bytes 4194304 | tf_op jit(solution)/shard_map/slice | solution.py:710
  3.8 1.7 collective-permute-start.2
  5.4 1.9 collective-permute-start.1
  7.4 1.1 fusion.1
  8.5 0.7 pad_maximum_fusion
  9.2 3.8 %collective-permute-start.4 = (f32[2,256,128]{2,1,0:T(8,128)}, f32[2,256,128]{2,1,0:T(8,128)S(1)}, u32[]{:S(2)}, u32[]{:S(2)}) collective-permute-start(f32[2,256,128]{2,1,0:T(8,128)} %pad_maximum_fusion), channel_id=1, source_target_pairs={{0,1},{1,2},{2,3},{3,4},{4,5},{5,6},{6,7},{8,9},{9,10},{10,11},{11... | collective-permute-start | bytes 786440 | tf_op jit(solution)/shard_map/ppermute | solution.py:667
  13.0 2.1 %collective-permute-start = (f32[2,128,1024]{2,1,0:T(8,128)}, f32[2,128,1024]{2,1,0:T(8,128)S(1)}, u32[]{:S(2)}, u32[]{:S(2)}) collective-permute-start(f32[2,128,1024]{2,1,0:T(8,128)} %get-tuple-element.48), channel_id=1, source_target_pairs={{0,8},{8,16},{16,24},{24,32},{32,40},{40,48},{48,56},{56,64},{64,7... | collective-permute-start | bytes 3145736 | tf_op jit(solution)/shard_map/ppermute | solution.py:667
  15.2 0.0 collective-permute-done.2
  15.2 1.6 collective-permute-start.3
  16.8 0.7 pad_maximum_fusion.1
  17.5 2.9 %collective-permute-start.6 = (f32[2,256,128]{2,1,0:T(8,128)}, f32[2,256,128]{2,1,0:T(8,128)S(1)}, u32[]{:S(2)}, u32[]{:S(2)}) collective-permute-start(f32[2,256,128]{2,1,0:T(8,128)} %pad_maximum_fusion.1), channel_id=1, source_target_pairs={{1,0},{2,1},{3,2},{4,3},{5,4},{6,5},{7,6},{9,8},{10,9},{11,10},{12... | collective-permute-start | bytes 786440 | tf_op jit(solution)/shard_map/ppermute | solution.py:667
  20.5 2.4 %fusion = (f32[2,768,128]{2,1,0:T(8,128)}, f32[2,768,128]{2,1,0:T(8,128)S(1)}) fusion(f32[2,1024,1024]{2,1,0:T(8,128)} %field.3), kind=kLoop, calls=%fused_computation.4 | loop fusion | bytes 3145728 | tf_op jit(solution)/shard_map/slice | solution.py:709
  22.9 0.0 copy-done.6
  22.9 0.7 copy.16.centers
  23.5 0.0 collective-permute-done.4.left_edge
  23.5 0.0 copy-start
  23.5 2.8 %collective-permute-start.7 = (f32[2,768,128]{2,1,0:T(8,128)}, f32[2,768,128]{2,1,0:T(8,128)}, u32[]{:S(2)}, u32[]{:S(2)}) collective-permute-start(f32[2,768,128]{2,1,0:T(8,128)} %get-tuple-element.41), channel_id=1, source_target_pairs={{1,0},{2,1},{3,2},{4,3},{5,4},{6,5},{7,6},{9,8},{10,9},{11,10},{12... | collective-permute-start | bytes 2359304 | tf_op jit(solution)/shard_map/ppermute | solution.py:667
  26.4 2.1 %collective-permute-done.6.right_edge = f32[2,256,128]{2,1,0:T(8,128)S(1)} collective-permute-done((f32[2,256,128]{2,1,0:T(8,128)}, f32[2,256,128]{2,1,0:T(8,128)S(1)}, u32[]{:S(2)}, u32[]{:S(2)}) %collective-permute-start.6) | collective-permute-done | bytes 262176 | tf_op jit(solution)/shard_map/ppermute | solution.py:667
  28.5 0.0 copy-start.1
  28.5 3.9 %collective-permute-start.5 = (f32[2,768,128]{2,1,0:T(8,128)S(1)}, f32[2,768,128]{2,1,0:T(8,128)}, u32[]{:S(2)}, u32[]{:S(2)}) collective-permute-start(f32[2,768,128]{2,1,0:T(8,128)S(1)} %get-tuple-element.42), channel_id=1, source_target_pairs={{0,1},{1,2},{2,3},{3,4},{4,5},{5,6},{6,7},{8,9},{9,10},{10,11},{11... | collective-permute-start | bytes 2359304 | tf_op jit(solution)/shard_map/ppermute | solution.py:667
  32.5 0.7 pad_maximum_fusion.3
  33.2 0.7 pad_maximum_fusion.2
  33.9 0.0 collective-permute-done.1
  33.9 1.9 collective-permute-start.8
  35.8 0.0 collective-permute-done.3
  35.9 3.6 %collective-permute-start.9 = (f32[2,128,256]{2,1,0:T(8,128)}, f32[2,128,256]{2,1,0:T(8,128)S(1)}, u32[]{:S(2)}, u32[]{:S(2)}) collective-permute-start(f32[2,128,256]{2,1,0:T(8,128)} %pad_maximum_fusion.3), channel_id=1, source_target_pairs={{8,0},{16,8},{24,16},{32,24},{40,32},{48,40},{56,48},{64,56},{72,6... | collective-permute-start | bytes 786440 | tf_op jit(solution)/shard_map/ppermute | solution.py:667
  39.5 2.4 %add.3.down = f32[2,128,1024]{2,1,0:T(8,128)} add(f32[2,128,1024]{2,1,0:T(8,128)S(1)} %collective-permute-done.1, f32[2,128,1024]{2,1,0:T(8,128)} %collective-permute-done.3) | non-fusion elementwise | flops 262144 | bytes 3145728 | tf_op jit(solution)/shard_map/add | solution.py:698
  41.9 0.0 collective-permute-done.up
  41.9 0.0 copy-start.2
  41.9 1.1 copy-done.2
  43.0 13.8 %inner_slots.1 = (f32[2,1024,1024]{2,1,0:T(8,128)}, f32[2,128,1024]{2,1,0:T(8,128)}, f32[2,128,1024]{2,1,0:T(8,128)}, f32[2,2,256,128]{3,2,1,0:T(8,128)}, f32[16]{0:T(128)}) custom-call(s32[16,2]{1,0:T(8,128)} %copy.16.centers, s32[16]{0:T(128)} %live.3, f32[2,256,256]{2,1,0:T(8,128)} %probe.3, bf16[4,256,768]{2,1,0:T(8,128)(2,1)} %constant.6.clone.lefts, ...), custom_call_target="tpu_custom_call" | custom-call | flops 13958643712 | bytes 31457280 | tf_op jit(solution)/shard_map/inner_slots/pallas_call | solution.py:322
  56.8 0.0 copy-done
  56.8 0.0 copy-done.1
  56.8 0.0 collective-permute-done.8.above
  56.8 0.0 copy-start.4
  56.8 0.0 collective-permute-done.9.below
  56.8 0.0 copy-start.5
  56.9 6.0 %collective-permute-done.7.right_core = f32[2,768,128]{2,1,0:T(8,128)} collective-permute-done((f32[2,768,128]{2,1,0:T(8,128)}, f32[2,768,128]{2,1,0:T(8,128)}, u32[]{:S(2)}, u32[]{:S(2)}) %collective-permute-start.7) | collective-permute-done | bytes 786464 | tf_op jit(solution)/shard_map/ppermute | solution.py:667
  62.9 0.0 collective-permute-done.5.left_core
  62.9 0.0 copy-done.4
  62.9 0.0 copy-done.5
  62.9 11.7 %outer_slots.1 = (f32[2,1024,1024]{2,1,0:T(8,128)}, f32[2,128,1024]{2,1,0:T(8,128)}, f32[2,128,1024]{2,1,0:T(8,128)}, f32[2,2,256,128]{3,2,1,0:T(8,128)}, f32[16...) custom-call(s32[16,2]{1,0:T(8,128)} %copy.16.centers, ...), custom_call_target="tpu_custom_call", output_to_operand_aliasing={{0}: (16, {}), {1}: (17, {}), {2}: (18, {})} | custom-call | flops 6979321856 | bytes 31457280 | tf_op jit(solution)/shard_map/outer_slots/pallas_call | solution.py:335
  74.6 119.1 %send_back.1 = (f32[2,1024,128]{2,1,0:T(8,128)}, f32[2,1024,128]{2,1,0:T(8,128)}, f32[2,128,1024]{2,1,0:T(8,128)}, f32[2,128,1024]{2,1,0:T(8,128)}, f32[2,256,256]{2,1,0:T(8,128)}) custom-call(f32[2,1024,128]{2,1,0:T(8,128)} %get-tuple-element.27.gleft, f32[2,1024,128]{2,1,0:T(8,128)} %get-tuple-element.28.gright, f32[2,128,256]{2,1,0:T(8,128)} %get-tuple-element.29.gabove, ...), custom_call_target="tpu_custom_call" | custom-call | flops 524288 | bytes 104857600 | tf_op jit(solution)/shard_map/send_back/pallas_call | solution.py:575
  193.8 0.0 copy-start.3
  193.8 5.7 %fold.1 = f32[2,1024,1024]{2,1,0:T(8,128)} custom-call(f32[2,1024,128]{2,1,0:T(8,128)} %get-tuple-element.34.got_left, f32[2,1024,128]{2,1,0:T(8,128)} %get-tuple-element.35.got_right, f32[2,128,1024]{2,1,0:T(8,128)} %get-tuple-element.36.got_up, f32[2,128,1024]{2,1,0:T(8,128)} %get-tuple-element.37.got_down, ...), custom_call_target="tpu_custom_call", output_to_operand_aliasing={{}: (4, {})} | custom-call | tf_op jit(solution)/shard_map/fold/pallas_call | solution.py:646
  199.5 0.0 copy-done.3
  199.5 0.8 copy.22
  (2 shorter events, 0.0 us)
Async XLA Ops:
  0.6 22.2 %copy-start.6 = (s32[16,2]{0,1:T(2,128)S(1)}, s32[16,2]{0,1:T(2,128)}, u32[]{:S(2)}) copy-start(s32[16,2]{0,1:T(2,128)} %param.10) | copy-start | bytes 388
  3.8 11.4 %collective-permute-start.2 = (f32[2,128,1024]{2,1,0:T(8,128)}, f32[2,128,1024]{2,1,0:T(8,128)}, u32[]{:S(2)}, u32[]{:S(2)}) collective-permute-start(f32[2,128,1024]{2,1,0:T(8,128)} %get-tuple-element.47), channel_id=1, source_target_pairs={{64,57},{66,59},{68,61},{70,63},{65,64},{67,66},{69,68},{71,70}} | collective-permute-start | bytes 3145736 | tf_op jit(solution)/shard_map/ppermute | solution.py:687
  5.4 28.5 %collective-permute-start.1 = (f32[2,128,1024]{2,1,0:T(8,128)}, f32[2,128,1024]{2,1,0:T(8,128)S(1)}, u32[]{:S(2)}, u32[]{:S(2)}) collective-permute-start(f32[2,128,1024]{2,1,0:T(8,128)} %get-tuple-element.47), channel_id=1, source_target_pairs={{8,0},{16,8},{24,16},{32,24},{40,32},{48,40},{56,48},{72,64},{80,7... | collective-permute-start | bytes 3145736 | tf_op jit(solution)/shard_map/ppermute | solution.py:691
  9.2 14.3 %collective-permute-start.4 = (f32[2,256,128]{2,1,0:T(8,128)}, f32[2,256,128]{2,1,0:T(8,128)S(1)}, u32[]{:S(2)}, u32[]{:S(2)}) collective-permute-start(f32[2,256,128]{2,1,0:T(8,128)} %pad_maximum_fusion), channel_id=1, source_target_pairs={{0,1},{1,2},{2,3},{3,4},{4,5},{5,6},{6,7},{8,9},{9,10},{10,11},{11... | collective-permute-start | bytes 786440 | tf_op jit(solution)/shard_map/ppermute | solution.py:667
  13.0 28.8 %collective-permute-start = (f32[2,128,1024]{2,1,0:T(8,128)}, f32[2,128,1024]{2,1,0:T(8,128)S(1)}, u32[]{:S(2)}, u32[]{:S(2)}) collective-permute-start(f32[2,128,1024]{2,1,0:T(8,128)} %get-tuple-element.48), channel_id=1, source_target_pairs={{0,8},{8,16},{16,24},{24,32},{32,40},{40,48},{48,56},{56,64},{64,7... | collective-permute-start | bytes 3145736 | tf_op jit(solution)/shard_map/ppermute | solution.py:667
  15.2 20.7 %collective-permute-start.3 = (f32[2,128,1024]{2,1,0:T(8,128)}, f32[2,128,1024]{2,1,0:T(8,128)}, u32[]{:S(2)}, u32[]{:S(2)}) collective-permute-start(f32[2,128,1024]{2,1,0:T(8,128)} %collective-permute-done.2), channel_id=1, source_target_pairs={{57,56},{59,58},{61,60},{63,62},{64,57},{66,59},{68,61},{70,63}} | collective-permute-start | bytes 3145736 | tf_op jit(solution)/shard_map/ppermute | solution.py:687
  17.5 11.0 %collective-permute-start.6 = (f32[2,256,128]{2,1,0:T(8,128)}, f32[2,256,128]{2,1,0:T(8,128)S(1)}, u32[]{:S(2)}, u32[]{:S(2)}) collective-permute-start(f32[2,256,128]{2,1,0:T(8,128)} %pad_maximum_fusion.1), channel_id=1, source_target_pairs={{1,0},{2,1},{3,2},{4,3},{5,4},{6,5},{7,6},{9,8},{10,9},{11,10},{12... | collective-permute-start | bytes 786440 | tf_op jit(solution)/shard_map/ppermute | solution.py:667
  23.5 33.3 %copy-start = (f32[2,256,128]{2,1,0:T(8,128)}, f32[2,256,128]{2,1,0:T(8,128)S(1)}, u32[]{:S(2)}) copy-start(f32[2,256,128]{2,1,0:T(8,128)S(1)} %collective-permute-done.4.left_edge) | copy-start | bytes 786436
  23.5 39.4 %collective-permute-start.7 = (f32[2,768,128]{2,1,0:T(8,128)}, f32[2,768,128]{2,1,0:T(8,128)}, u32[]{:S(2)}, u32[]{:S(2)}) collective-permute-start(f32[2,768,128]{2,1,0:T(8,128)} %get-tuple-element.41), channel_id=1, source_target_pairs={{1,0},{2,1},{3,2},{4,3},{5,4},{6,5},{7,6},{9,8},{10,9},{11,10},{12... | collective-permute-start | bytes 2359304 | tf_op jit(solution)/shard_map/ppermute | solution.py:667
  28.5 28.3 %copy-start.1 = (f32[2,256,128]{2,1,0:T(8,128)}, f32[2,256,128]{2,1,0:T(8,128)S(1)}, u32[]{:S(2)}) copy-start(f32[2,256,128]{2,1,0:T(8,128)S(1)} %collective-permute-done.6.right_edge) | copy-start | bytes 786436
  28.5 34.4 %collective-permute-start.5 = (f32[2,768,128]{2,1,0:T(8,128)S(1)}, f32[2,768,128]{2,1,0:T(8,128)}, u32[]{:S(2)}, u32[]{:S(2)}) collective-permute-start(f32[2,768,128]{2,1,0:T(8,128)S(1)} %get-tuple-element.42), channel_id=1, source_target_pairs={{0,1},{1,2},{2,3},{3,4},{4,5},{5,6},{6,7},{8,9},{9,10},{10,11},{11... | collective-permute-start | bytes 2359304 | tf_op jit(solution)/shard_map/ppermute | solution.py:667
  33.9 22.9 %collective-permute-start.8 = (f32[2,128,256]{2,1,0:T(8,128)}, f32[2,128,256]{2,1,0:T(8,128)S(1)}, u32[]{:S(2)}, u32[]{:S(2)}) collective-permute-start(f32[2,128,256]{2,1,0:T(8,128)} %pad_maximum_fusion.2), channel_id=1, source_target_pairs={{0,8},{8,16},{16,24},{24,32},{32,40},{40,48},{48,56},{56,64},{64,7... | collective-permute-start | bytes 786440 | tf_op jit(solution)/shard_map/ppermute | solution.py:667
  35.9 21.0 %collective-permute-start.9 = (f32[2,128,256]{2,1,0:T(8,128)}, f32[2,128,256]{2,1,0:T(8,128)S(1)}, u32[]{:S(2)}, u32[]{:S(2)}) collective-permute-start(f32[2,128,256]{2,1,0:T(8,128)} %pad_maximum_fusion.3), channel_id=1, source_target_pairs={{8,0},{16,8},{24,16},{32,24},{40,32},{48,40},{56,48},{64,56},{72,6... | collective-permute-start | bytes 786440 | tf_op jit(solution)/shard_map/ppermute | solution.py:667
  41.9 1.1 copy-start.2
  56.8 6.1 %copy-start.4 = (f32[2,128,256]{2,1,0:T(8,128)}, f32[2,128,256]{2,1,0:T(8,128)S(1)}, u32[]{:S(2)}) copy-start(f32[2,128,256]{2,1,0:T(8,128)S(1)} %collective-permute-done.8.above) | copy-start | bytes 786436
  56.8 6.1 %copy-start.5 = (f32[2,128,256]{2,1,0:T(8,128)}, f32[2,128,256]{2,1,0:T(8,128)S(1)}, u32[]{:S(2)}) copy-start(f32[2,128,256]{2,1,0:T(8,128)S(1)} %collective-permute-done.9.below) | copy-start | bytes 786436
  193.8 5.7 %copy-start.3 = (f32[2,256,256]{2,1,0:T(8,128)S(1)}, f32[2,256,256]{2,1,0:T(8,128)}, u32[]{:S(2)}) copy-start(f32[2,256,256]{2,1,0:T(8,128)} %get-tuple-element.57) | copy-start | bytes 1572868

commit v3 on v2

--- a/solution.py
+++ b/solution.py
@@ -130,8 +130,7 @@
     return loss
 
 
-EDGE = slice(HALF, HALF + TILE)
-STRIP = (0, 1, 6, 7)
+INNER_COST = SLOTS_HERE
 CORE = TILE - 2 * HALF
 
 
@@ -151,23 +150,16 @@
     return ref.at[:, :, pl.ds(HALF * index, HALF)]
 
 
-def tile_pairs(tile, up, down, buffer, slots):
+def inner_pairs(tile, buffer, slots, first_row):
+    return [(block_of(tile, block), buffer.at[:, place, pl.ds(first_row, TILE)]) for place, block in slots]
+
+
+def band_pairs(up, down, buffer, slots):
     pairs = []
     for place, block in slots:
-        pairs.append((block_of(tile, block), buffer.at[:, place, pl.ds(HALF, TILE)]))
         pairs.append((block_of(up, block), buffer.at[:, place, pl.ds(0, HALF)]))
         pairs.append((block_of(down, block), buffer.at[:, place, pl.ds(HALF + TILE, HALF)]))
     return pairs
-
-
-def halo_pairs(edge, core, above, below, side, buffer, place):
-    return [
-        (edge.at[:, pl.ds(0, HALF)], buffer.at[:, place, pl.ds(HALF, HALF)]),
-        (core, buffer.at[:, place, pl.ds(2 * HALF, CORE)]),
-        (edge.at[:, pl.ds(HALF, HALF)], buffer.at[:, place, pl.ds(TILE, HALF)]),
-        (block_of(above, side), buffer.at[:, place, pl.ds(0, HALF)]),
-        (block_of(below, side), buffer.at[:, place, pl.ds(HALF + TILE, HALF)]),
-    ]
 
 
 def strip_pairs(strip, above, below, side, buffer, place):
@@ -191,7 +183,7 @@
 
 def fetch_slots(live, centers, wanted, measured, seen, slot_sems):
     def fetch(s, carry):
-        @pl.when(wanted(live[s], centers[s, 1]))
+        @pl.when(wanted(live[s], centers[s, 0], centers[s, 1]))
         def _():
             for copy in slot_copies(measured, seen, slot_sems, s):
                 copy.start()
@@ -201,35 +193,38 @@
     lax.fori_loop(0, SLOTS_HERE, fetch, 0)
 
 
-def run_slots(live, centers, wanted, place, measured, seen, slot_sems, losses, body):
+def run_slots(live, centers, wanted, offset, blocks, measured, seen, slot_sems, losses, body):
     def step(s, carry):
-        column = centers[s, 1]
-
-        @pl.when(wanted(live[s], column))
+        row, column = centers[s, 0], centers[s, 1]
+
+        @pl.when(wanted(live[s], row, column))
         def _():
             wait_all(slot_copies(measured, seen, slot_sems, s))
-            block, block_end, shift = place(column)
-            losses[s] = body(s, centers[s, 0], block, block_end, shift)
+            block = lax.div(column - offset, HALF)
+            losses[s] = body(s, row - offset, block, jnp.minimum(block + 2, blocks - 1), lax.rem(column - offset, HALF))
 
         return carry
 
     lax.fori_loop(0, SLOTS_HERE, step, 0)
 
 
-def is_inner(alive, column):
-    return (alive > 0) & (column >= HALF) & (column <= TILE - HALF)
-
-
-def is_outer(alive, column):
-    return (alive > 0) & ((column < HALF) | (column > TILE - HALF))
+def within(row, column):
+    return (row >= HALF) & (row <= TILE - HALF) & (column >= HALF) & (column <= TILE - HALF)
+
+
+def is_inner(alive, row, column):
+    return (alive > 0) & within(row, column)
+
+
+def is_outer(alive, row, column):
+    return (alive > 0) & jnp.logical_not(within(row, column))
 
 
 def inner_kernel(
-    centers, live, probe, lefts, rights, pick, field, up, down, measured,
-    grad_out, up_out, down_out, acc, losses, obj, grad, seen, sems, slot_sems,
+    centers, live, probe, lefts, rights, pick, field, measured, grad_out, acc, losses, obj, grad, seen, sems, slot_sems
 ):
     slots = [(j, j) for j in range(8)]
-    loads = start_all(tile_pairs(field, up, down, obj, slots), sems)
+    loads = start_all(inner_pairs(field, obj, slots, 0), sems)
     fetch_slots(live, centers, is_inner, measured, seen, slot_sems)
     grad[...] = jnp.zeros_like(grad)
     acc[...] = jnp.zeros_like(acc)
@@ -237,55 +232,49 @@
         losses[s] = 0.0
     wait_all(loads)
 
-    def place(column):
-        start = column - HALF
-        block = lax.div(start, HALF)
-        return block, jnp.minimum(block + 2, 7), lax.rem(start, HALF)
-
     def body(s, row, block, block_end, shift):
         return visit(obj, grad, probe, seen, s, lefts, rights, pick, acc, row, block, block_end, shift)
 
-    run_slots(live, centers, is_inner, place, measured, seen, slot_sems, losses, body)
-    wait_all(start_all(flipped(tile_pairs(grad_out, up_out, down_out, grad, slots)), sems))
+    run_slots(live, centers, is_inner, HALF, 8, measured, seen, slot_sems, losses, body)
+    wait_all(start_all(flipped(inner_pairs(grad_out, grad, slots, 0)), sems))
 
 
 def outer_kernel(
     centers, live, probe, lefts, rights, pick, field, up, down, measured,
-    left_edge, left_core, right_edge, right_core, above, below, grad_in, up_in, down_in, acc_in, losses_in,
-    grad_out, up_out, down_out, acc, losses, gleft, gright, gabove, gbelow,
+    left, right, above, below, grad_in, acc_in, losses_in,
+    grad_out, acc, losses, up_out, down_out, gleft, gright, gabove, gbelow,
     obj, grad, seen, sems, slot_sems,
 ):
-    slots = list(zip((1, 2, 3, 4), STRIP))
+    slots = [(j + 1, j) for j in range(8)]
     loads = start_all(
-        tile_pairs(field, up, down, obj, slots)
-        + halo_pairs(left_edge, left_core, above, below, 0, obj, 0)
-        + halo_pairs(right_edge, right_core, above, below, 1, obj, 5)
-        + tile_pairs(grad_in, up_in, down_in, grad, slots),
+        inner_pairs(field, obj, slots, HALF)
+        + band_pairs(up, down, obj, slots)
+        + strip_pairs(left, above, below, 0, obj, 0)
+        + strip_pairs(right, above, below, 1, obj, 9)
+        + inner_pairs(grad_in, grad, slots, HALF),
         sems,
     )
     fetch_slots(live, centers, is_outer, measured, seen, slot_sems)
-    for place_at in (0, 5):
+    for place_at in (0, 9):
         grad[:, place_at] = jnp.zeros((2, ROWS, HALF), jnp.float32)
+    for row_at in (0, HALF + TILE):
+        grad[:, 1:9, row_at : row_at + HALF] = jnp.zeros((2, 8, HALF, HALF), jnp.float32)
     acc[...] = acc_in[...]
     for s in range(SLOTS_HERE):
         losses[s] = losses_in[s]
     wait_all(loads)
 
-    def place(column):
-        at_left = column < HALF
-        block = jnp.where(at_left, 0, 3)
-        return block, block + 2, jnp.where(at_left, column, column - (TILE - HALF))
-
     def body(s, row, block, block_end, shift):
         return visit(obj, grad, probe, seen, s, lefts, rights, pick, acc, row, block, block_end, shift)
 
-    run_slots(live, centers, is_outer, place, measured, seen, slot_sems, losses, body)
+    run_slots(live, centers, is_outer, 0, 10, measured, seen, slot_sems, losses, body)
     wait_all(
         start_all(
             flipped(
-                tile_pairs(grad_out, up_out, down_out, grad, slots)
+                inner_pairs(grad_out, grad, slots, HALF)
+                + band_pairs(up_out, down_out, grad, slots)
                 + strip_pairs(gleft, gabove, gbelow, 0, grad, 0)
-                + strip_pairs(gright, gabove, gbelow, 1, grad, 5)
+                + strip_pairs(gright, gabove, gbelow, 1, grad, 9)
             ),
             sems,
         )
@@ -303,8 +292,8 @@
 
 def slot_scratch(blocks, copies):
     return [
-        pltpu.VMEM((2, blocks, ROWS, HALF), jnp.float32),
-        pltpu.VMEM((2, blocks, ROWS, HALF), jnp.float32),
+        pltpu.VMEM((2, blocks, HALF * blocks, HALF), jnp.float32),
+        pltpu.VMEM((2, blocks, HALF * blocks, HALF), jnp.float32),
         pltpu.VMEM((SLOTS_HERE, 2, M, HALF), jnp.float32),
         pltpu.SemaphoreType.DMA((copies,)),
         pltpu.SemaphoreType.DMA((SLOTS_HERE, 2)),
@@ -315,32 +304,31 @@
     return pl.CostEstimate(flops=slots * 26 * 2 * M**3, bytes_accessed=30 << 20, transcendentals=slots * M * M)
 
 
-TILE_OUT = (shaped(2, TILE, TILE), shaped(2, HALF, TILE), shaped(2, HALF, TILE), shaped(2, 2, M, HALF), shaped(SLOTS_HERE))
-
-
-def inner_slots(centers, live, probe, tables, field, up, down, measured):
+TILE_OUT = (shaped(2, TILE, TILE), shaped(2, 2, M, HALF), shaped(SLOTS_HERE))
+TILE_SPECS = (HBM_SPEC, VMEM_SPEC, SMEM_SPEC)
+
+
+def inner_slots(centers, live, probe, tables, field, measured):
     return pl.pallas_call(
         inner_kernel,
         out_shape=TILE_OUT,
-        in_specs=[SMEM_SPEC] * 2 + [VMEM_SPEC] * 4 + [HBM_SPEC] * 4,
-        out_specs=(HBM_SPEC, HBM_SPEC, HBM_SPEC, VMEM_SPEC, SMEM_SPEC),
-        scratch_shapes=slot_scratch(8, 24),
+        in_specs=[SMEM_SPEC] * 2 + [VMEM_SPEC] * 4 + [HBM_SPEC] * 2,
+        out_specs=TILE_SPECS,
+        scratch_shapes=slot_scratch(8, 8),
         compiler_params=pltpu.CompilerParams(vmem_limit_bytes=VMEM),
-        cost_estimate=cost(SLOTS_HERE),
+        cost_estimate=cost(INNER_COST),
         name="inner_slots",
-    )(centers, live, probe, *tables, field, up, down, measured)
+    )(centers, live, probe, *tables, field, measured)
 
 
 def outer_slots(centers, live, probe, tables, field, up, down, measured, halos, partial):
     return pl.pallas_call(
         outer_kernel,
-        out_shape=TILE_OUT
-        + (shaped(2, TILE, HALF),) * 2
-        + (shaped(2, HALF, 2 * HALF),) * 2,
-        in_specs=[SMEM_SPEC] * 2 + [VMEM_SPEC] * 4 + [HBM_SPEC] * 4 + [HBM_SPEC] * 9 + [VMEM_SPEC, SMEM_SPEC],
-        out_specs=(HBM_SPEC, HBM_SPEC, HBM_SPEC, VMEM_SPEC, SMEM_SPEC) + (HBM_SPEC,) * 4,
-        scratch_shapes=slot_scratch(6, 34),
-        input_output_aliases={16: 0, 17: 1, 18: 2},
+        out_shape=TILE_OUT + (shaped(2, HALF, TILE),) * 2 + (shaped(2, TILE, HALF),) * 2 + (shaped(2, HALF, 2 * HALF),) * 2,
+        in_specs=[SMEM_SPEC] * 2 + [VMEM_SPEC] * 4 + [HBM_SPEC] * 9 + [VMEM_SPEC, SMEM_SPEC],
+        out_specs=TILE_SPECS + (HBM_SPEC,) * 6,
+        scratch_shapes=slot_scratch(10, 38),
+        input_output_aliases={14: 0},
         compiler_params=pltpu.CompilerParams(vmem_limit_bytes=VMEM),
         cost_estimate=cost(SLOTS_HERE // 2),
         name="outer_slots",
@@ -687,32 +675,35 @@
     return lax.ppermute(x, ("gx", "gy"), [(8 * a + b, 8 * c + d) for (a, b), (c, d) in pairs])
 
 
-def to_up_relayed(x):
-    straight = lax.ppermute(x, "gx", [(i + 1, i) for i in range(15) if i != 7])
-    once = joint(
+def crossing_first(x):
+    return joint(
         x, [((8, 2 * y), (7, 2 * y + 1)) for y in range(4)] + [((8, 2 * y + 1), (8, 2 * y)) for y in range(4)]
     )
-    twice = joint(
-        once, [((7, 2 * y + 1), (7, 2 * y)) for y in range(4)] + [((8, 2 * y), (7, 2 * y + 1)) for y in range(4)]
-    )
-    return straight + twice
-
-
-def ends(strip):
-    return jnp.concatenate([strip[:, :HALF], strip[:, TILE - HALF :]], axis=1)
+
+
+def crossing_second(x):
+    return joint(x, [((7, 2 * y + 1), (7, 2 * y)) for y in range(4)] + [((8, 2 * y), (7, 2 * y + 1)) for y in range(4)])
+
+
+def to_up_straight(x):
+    return lax.ppermute(x, "gx", [(i + 1, i) for i in range(15) if i != 7])
 
 
 def on_device(field, probe, centers, live, measured):
     tables = tuple(jnp.asarray(t) for t in host_tables())
-    first, last = field[:, :, :HALF], field[:, :, TILE - HALF :]
-    left_edge, right_edge = to_right(ends(last)), to_left(ends(first))
-    left_core, right_core = to_right(last[:, HALF : TILE - HALF]), to_left(first[:, HALF : TILE - HALF])
-    up, down = to_down(field[:, TILE - HALF :]), to_up_relayed(field[:, :HALF])
-    above = to_down(jnp.concatenate([left_edge[:, HALF:], right_edge[:, HALF:]], axis=2))
-    below = to_up(jnp.concatenate([left_edge[:, :HALF], right_edge[:, :HALF]], axis=2))
-    halos = (left_edge, left_core, right_edge, right_core, above, below)
-    partial = inner_slots(centers, live, probe, tables, field, up, down, measured)
-    grad, gup, gdown, acc, losses, gleft, gright, gabove, gbelow = outer_slots(
+    left, right = to_right(field[:, :, TILE - HALF :]), to_left(field[:, :, :HALF])
+    top_rows = field[:, :HALF]
+    relayed, up, straight = crossing_first(top_rows), to_down(field[:, TILE - HALF :]), to_up_straight(top_rows)
+    grad, acc, losses = inner_slots(centers, live, probe, tables, field, measured)
+    relayed, acc = lax.optimization_barrier((relayed, acc))
+    second = crossing_second(relayed)
+    left, right, up, straight, acc = lax.optimization_barrier((left, right, up, straight, acc))
+    above = to_down(jnp.concatenate([left[:, TILE - HALF :], right[:, TILE - HALF :]], axis=2))
+    below = to_up(jnp.concatenate([left[:, :HALF], right[:, :HALF]], axis=2))
+    down = straight + second
+    halos = (left, right, above, below)
+    partial = (grad, acc, losses)
+    grad, acc, losses, gup, gdown, gleft, gright, gabove, gbelow = outer_slots(
         centers, live, probe, tables, field, up, down, measured, halos, partial
     )
     slots_all = SLOTS_HERE * lax.axis_size("gx") * lax.axis_size("gy")

time: 201 us -> 187 us (0.930)
  the two profiles are of different devices: /device:TPU:12 before, /device:TPU:1 now
where the time goes in v3:
time: 187 us; the launch traced here: 186 us
  Pallas kernels  116 us (62%)
  waiting for transfers between devices  40.1 us (21%)
  starting transfers between devices  19 us (10%)
  local copies, waits for them, and re-layouts  8.4 us (4%)
  other arithmetic  2.44 us (1%)
    pallas_call x1, Pallas kernels, send_back(): pl.pallas_call(functools.partial(return_kernel, scale), out_shape=(shaped...  73.3 us
    ppermute x5, waiting for transfers between devices, shift_by_one(): return lax.ppermute(x, axis, steps)  40 us
    pallas_call x1, Pallas kernels, outer_slots(): pl.pallas_call(outer_kernel, out_shape=TILE_OUT + (shaped(2, HALF, TILE),...  20.3 us
    pallas_call x1, Pallas kernels, inner_slots(): pl.pallas_call(inner_kernel, out_shape=TILE_OUT, in_specs=[SMEM_SPEC] * 2...  16.5 us
    ppermute x5, starting transfers between devices, shift_by_one(): return lax.ppermute(x, axis, steps)  13.3 us
    pallas_call x1, Pallas kernels, fold(): pl.pallas_call(fold_kernel, out_shape=shaped(2, TILE, TILE), in_specs=[HB...  5.58 us
  transfers between devices with their start and end apart: 8, of which 3 were waited for; matrix products, arithmetic and copies ran while one was open for 3% of the time, Pallas kernels for 9%

profile of v3, /device:TPU:1, one launch (start us, length us, event | category | flops | bytes accessed | tf_op | source)
XLA Modules:
  0.0 186.4 jit_solution(9600902153379327936)
XLA Ops:
  0.6 0.0 copy-start.6
  0.6 3.1 %fusion = (f32[2,128,1024]{2,1,0:T(8,128)}, f32[2,128,1024]{2,1,0:T(8,128)}) fusion(f32[2,1024,1024]{2,1,0:T(8,128)} %field.3), kind=kLoop, calls=%fused_computation.2 | loop fusion | bytes 4194304 | tf_op jit(solution)/shard_map/slice | solution.py:695
  3.8 1.6 collective-permute-start.4
  5.4 3.3 %collective-permute-start.3 = (f32[2,128,1024]{2,1,0:T(8,128)}, f32[2,128,1024]{2,1,0:T(8,128)}, u32[]{:S(2)}, u32[]{:S(2)}) collective-permute-start(f32[2,128,1024]{2,1,0:T(8,128)} %get-tuple-element.51), channel_id=1, source_target_pairs={{8,0},{16,8},{24,16},{32,24},{40,32},{48,40},{56,48},{72,64},{80,7... | collective-permute-start | bytes 3145736 | tf_op jit(solution)/shard_map/ppermute | solution.py:689
  8.8 3.1 %fusion.1 = (f32[2,1024,128]{2,1,0:T(8,128)}, f32[2,1024,128]{2,1,0:T(8,128)}) fusion(f32[2,1024,1024]{2,1,0:T(8,128)} %field.3), kind=kLoop, calls=%fused_computation.3 | loop fusion | bytes 4194304 | tf_op jit(solution)/shard_map/slice | solution.py:694
  11.8 1.3 collective-permute-start.1
  13.1 4.3 %collective-permute-start = (f32[2,1024,128]{2,1,0:T(8,128)}, f32[2,1024,128]{2,1,0:T(8,128)S(1)}, u32[]{:S(2)}, u32[]{:S(2)}) collective-permute-start(f32[2,1024,128]{2,1,0:T(8,128)} %get-tuple-element.54), channel_id=1, source_target_pairs={{0,1},{1,2},{2,3},{3,4},{4,5},{5,6},{6,7},{8,9},{9,10},{10,11},{11... | collective-permute-start | bytes 3145736 | tf_op jit(solution)/shard_map/ppermute | solution.py:655
  17.4 3.4 %collective-permute-start.2 = (f32[2,128,1024]{2,1,0:T(8,128)}, f32[2,128,1024]{2,1,0:T(8,128)S(1)}, u32[]{:S(2)}, u32[]{:S(2)}) collective-permute-start(f32[2,128,1024]{2,1,0:T(8,128)} %get-tuple-element.52), channel_id=1, source_target_pairs={{0,8},{8,16},{16,24},{24,32},{32,40},{40,48},{48,56},{56,64},{64,7... | collective-permute-start | bytes 3145736 | tf_op jit(solution)/shard_map/ppermute | solution.py:655
  20.8 0.0 copy-done.6
  20.8 0.7 copy.14.centers
  21.5 16.5 %inner_slots.1 = (f32[2,1024,1024]{2,1,0:T(8,128)}, f32[2,2,256,128]{3,2,1,0:T(8,128)}, f32[16]{0:T(128)}) custom-call(s32[16,2]{1,0:T(8,128)} %copy.14.centers, s32[16]{0:T(128)} %live.3, f32[2,256,256]{2,1,0:T(8,128)} %probe.3, bf16[4,256,768]{2,1,0:T(8,128)(2,1)} %constant.6.clone.lefts, bf16[4,768,256]{2,1,0:T(8,128)(2,1)} %constant.7.clone.rights, ...), custom_call_target="tpu_custom_call" | custom-call | flops 13958643712 | bytes 31457280 | tf_op jit(solution)/shard_map/inner_slots/pallas_call | solution.py:312
  38.0 0.0 collective-permute-done.4
  38.0 0.7 collective-permute-start.5
  38.8 11.1 %collective-permute-done.1.right = f32[2,1024,128]{2,1,0:T(8,128)S(1)} collective-permute-done((f32[2,1024,128]{2,1,0:T(8,128)}, f32[2,1024,128]{2,1,0:T(8,128)S(1)}, u32[]{:S(2)}, u32[]{:S(2)}) %collective-permute-start.1) | collective-permute-done | bytes 1048608 | tf_op jit(solution)/shard_map/ppermute | solution.py:655
  49.9 0.0 copy-start
  49.9 26.1 %collective-permute-done.left = f32[2,1024,128]{2,1,0:T(8,128)S(1)} collective-permute-done((f32[2,1024,128]{2,1,0:T(8,128)}, f32[2,1024,128]{2,1,0:T(8,128)S(1)}, u32[]{:S(2)}, u32[]{:S(2)}) %collective-permute-start) | collective-permute-done | bytes 1048608 | tf_op jit(solution)/shard_map/ppermute | solution.py:655
  76.0 0.0 copy-start.1
  76.0 0.0 collective-permute-done.2.up
  76.0 0.0 copy-start.2
  76.0 0.0 collective-permute-done.3
  76.1 1.9 %collective-permute-start.6 = (f32[2,128,256]{2,1,0:T(8,128)S(1)}, f32[2,128,256]{2,1,0:T(8,128)S(1)}, u32[]{:S(2)}, u32[]{:S(2)}) collective-permute-start(f32[2,128,256]{2,1,0:T(8,128)S(1)} %pad_maximum_fusion), channel_id=1, source_target_pairs={{0,8},{8,16},{16,24},{24,32},{32,40},{40,48},{48,56},{56,64},{64,7... | collective-permute-start | bytes 786440 | tf_op jit(solution)/shard_map/ppermute | solution.py:655
  78.0 2.4 %collective-permute-start.7 = (f32[2,128,256]{2,1,0:T(8,128)S(1)}, f32[2,128,256]{2,1,0:T(8,128)S(1)}, u32[]{:S(2)}, u32[]{:S(2)}) collective-permute-start(f32[2,128,256]{2,1,0:T(8,128)S(1)} %pad_maximum_fusion.1), channel_id=1, source_target_pairs={{8,0},{16,8},{24,16},{32,24},{40,32},{48,40},{56,48},{64,56},{72,6... | collective-permute-start | bytes 786440 | tf_op jit(solution)/shard_map/ppermute | solution.py:655
  80.4 0.0 collective-permute-done.5
  80.4 2.4 %add.3.down = f32[2,128,1024]{2,1,0:T(8,128)} add(f32[2,128,1024]{2,1,0:T(8,128)} %collective-permute-done.3, f32[2,128,1024]{2,1,0:T(8,128)S(1)} %collective-permute-done.5) | non-fusion elementwise | flops 262144 | bytes 3145728 | tf_op jit(solution)/shard_map/add | solution.py:703
  82.9 0.0 collective-permute-done.6.above
  82.9 0.0 copy-start.4
  82.9 2.8 %collective-permute-done.7.below = f32[2,128,256]{2,1,0:T(8,128)S(1)} collective-permute-done((f32[2,128,256]{2,1,0:T(8,128)S(1)}, f32[2,128,256]{2,1,0:T(8,128)S(1)}, u32[]{:S(2)}, u32[]{:S(2)}) %collective-permute-start.7) | collective-permute-done | bytes 262176 | tf_op jit(solution)/shard_map/ppermute | solution.py:655
  85.7 0.0 copy-start.5
  85.7 0.0 copy-done
  85.7 0.0 copy-done.1
  85.7 0.0 copy-done.2
  85.7 0.0 copy-done.4
  85.7 0.7 copy-done.5
  86.4 20.3 %outer_slots.1 = (f32[2,1024,1024]{2,1,0:T(8,128)}, f32[2,2,256,128]{3,2,1,0:T(8,128)}, f32[16]{0:T(128)}, f32[2,128,1024]{2,1,0:T(8,128)}, f32[2,128,1024]{2,1,...) custom-call(s32[16,2]{1,0:T(8,128)} %copy.14.centers, ...), custom_call_target="tpu_custom_call", output_to_operand_aliasing={{0}: (14, {})} | custom-call | flops 6979321856 | bytes 31457280 | tf_op jit(solution)/shard_map/outer_slots/pallas_call | solution.py:325
  106.8 73.3 %send_back.1 = (f32[2,1024,128]{2,1,0:T(8,128)}, f32[2,1024,128]{2,1,0:T(8,128)}, f32[2,128,1024]{2,1,0:T(8,128)}, f32[2,128,1024]{2,1,0:T(8,128)}, f32[2,256,256]{2,1,0:T(8,128)}) custom-call(f32[2,1024,128]{2,1,0:T(8,128)} %get-tuple-element.37.gleft, f32[2,1024,128]{2,1,0:T(8,128)} %get-tuple-element.38.gright, f32[2,128,256]{2,1,0:T(8,128)} %get-tuple-element.39.gabove, ...), custom_call_target="tpu_custom_call" | custom-call | flops 524288 | bytes 104857600 | tf_op jit(solution)/shard_map/send_back/pallas_call | solution.py:563
  180.0 0.0 copy-start.3
  180.1 5.6 %fold.1 = f32[2,1024,1024]{2,1,0:T(8,128)} custom-call(f32[2,1024,128]{2,1,0:T(8,128)} %get-tuple-element.44.got_left, f32[2,1024,128]{2,1,0:T(8,128)} %get-tuple-element.45.got_right, f32[2,128,1024]{2,1,0:T(8,128)} %get-tuple-element.46.got_up, f32[2,128,1024]{2,1,0:T(8,128)} %get-tuple-element.47.got_down, ...), custom_call_target="tpu_custom_call", output_to_operand_aliasing={{}: (4, {})} | custom-call | tf_op jit(solution)/shard_map/fold/pallas_call | solution.py:634
  185.6 0.0 copy-done.3
  185.6 0.8 copy.18
  (3 shorter events, 0.1 us)
Async XLA Ops:
  0.6 20.2 %copy-start.6 = (s32[16,2]{0,1:T(2,128)S(1)}, s32[16,2]{0,1:T(2,128)}, u32[]{:S(2)}) copy-start(s32[16,2]{0,1:T(2,128)} %param.10) | copy-start | bytes 388
  3.8 34.3 %collective-permute-start.4 = (f32[2,128,1024]{2,1,0:T(8,128)}, f32[2,128,1024]{2,1,0:T(8,128)}, u32[]{:S(2)}, u32[]{:S(2)}) collective-permute-start(f32[2,128,1024]{2,1,0:T(8,128)} %get-tuple-element.51), channel_id=1, source_target_pairs={{64,57},{66,59},{68,61},{70,63},{65,64},{67,66},{69,68},{71,70}} | collective-permute-start | bytes 3145736 | tf_op jit(solution)/shard_map/ppermute | solution.py:675
  5.4 70.6 %collective-permute-start.3 = (f32[2,128,1024]{2,1,0:T(8,128)}, f32[2,128,1024]{2,1,0:T(8,128)}, u32[]{:S(2)}, u32[]{:S(2)}) collective-permute-start(f32[2,128,1024]{2,1,0:T(8,128)} %get-tuple-element.51), channel_id=1, source_target_pairs={{8,0},{16,8},{24,16},{32,24},{40,32},{48,40},{56,48},{72,64},{80,7... | collective-permute-start | bytes 3145736 | tf_op jit(solution)/shard_map/ppermute | solution.py:689
  11.8 38.1 %collective-permute-start.1 = (f32[2,1024,128]{2,1,0:T(8,128)}, f32[2,1024,128]{2,1,0:T(8,128)S(1)}, u32[]{:S(2)}, u32[]{:S(2)}) collective-permute-start(f32[2,1024,128]{2,1,0:T(8,128)} %get-tuple-element.53), channel_id=1, source_target_pairs={{1,0},{2,1},{3,2},{4,3},{5,4},{6,5},{7,6},{9,8},{10,9},{11,10},{12... | collective-permute-start | bytes 3145736 | tf_op jit(solution)/shard_map/ppermute | solution.py:655
  13.1 62.9 %collective-permute-start = (f32[2,1024,128]{2,1,0:T(8,128)}, f32[2,1024,128]{2,1,0:T(8,128)S(1)}, u32[]{:S(2)}, u32[]{:S(2)}) collective-permute-start(f32[2,1024,128]{2,1,0:T(8,128)} %get-tuple-element.54), channel_id=1, source_target_pairs={{0,1},{1,2},{2,3},{3,4},{4,5},{5,6},{6,7},{8,9},{9,10},{10,11},{11... | collective-permute-start | bytes 3145736 | tf_op jit(solution)/shard_map/ppermute | solution.py:655
  17.4 58.5 %collective-permute-start.2 = (f32[2,128,1024]{2,1,0:T(8,128)}, f32[2,128,1024]{2,1,0:T(8,128)S(1)}, u32[]{:S(2)}, u32[]{:S(2)}) collective-permute-start(f32[2,128,1024]{2,1,0:T(8,128)} %get-tuple-element.52), channel_id=1, source_target_pairs={{0,8},{8,16},{16,24},{24,32},{32,40},{40,48},{48,56},{56,64},{64,7... | collective-permute-start | bytes 3145736 | tf_op jit(solution)/shard_map/ppermute | solution.py:655
  38.0 42.4 %collective-permute-start.5 = (f32[2,128,1024]{2,1,0:T(8,128)}, f32[2,128,1024]{2,1,0:T(8,128)S(1)}, u32[]{:S(2)}, u32[]{:S(2)}) collective-permute-start(f32[2,128,1024]{2,1,0:T(8,128)} %collective-permute-done.4), channel_id=1, source_target_pairs={{57,56},{59,58},{61,60},{63,62},{64,57},{66,59},{68,61},{70,63}} | collective-permute-start | bytes 3145736 | tf_op jit(solution)/shard_map/ppermute | solution.py:675
  49.9 35.8 %copy-start = (f32[2,1024,128]{2,1,0:T(8,128)}, f32[2,1024,128]{2,1,0:T(8,128)S(1)}, u32[]{:S(2)}) copy-start(f32[2,1024,128]{2,1,0:T(8,128)S(1)} %collective-permute-done.1.right) | copy-start | bytes 3145732
  76.0 9.7 %copy-start.1 = (f32[2,1024,128]{2,1,0:T(8,128)}, f32[2,1024,128]{2,1,0:T(8,128)S(1)}, u32[]{:S(2)}) copy-start(f32[2,1024,128]{2,1,0:T(8,128)S(1)} %collective-permute-done.left) | copy-start | bytes 3145732
  76.0 9.7 %copy-start.2 = (f32[2,128,1024]{2,1,0:T(8,128)}, f32[2,128,1024]{2,1,0:T(8,128)S(1)}, u32[]{:S(2)}) copy-start(f32[2,128,1024]{2,1,0:T(8,128)S(1)} %collective-permute-done.2.up) | copy-start | bytes 3145732
  76.1 6.8 %collective-permute-start.6 = (f32[2,128,256]{2,1,0:T(8,128)S(1)}, f32[2,128,256]{2,1,0:T(8,128)S(1)}, u32[]{:S(2)}, u32[]{:S(2)}) collective-permute-start(f32[2,128,256]{2,1,0:T(8,128)S(1)} %pad_maximum_fusion), channel_id=1, source_target_pairs={{0,8},{8,16},{16,24},{24,32},{32,40},{40,48},{48,56},{56,64},{64,7... | collective-permute-start | bytes 786440 | tf_op jit(solution)/shard_map/ppermute | solution.py:655
  78.0 7.7 %collective-permute-start.7 = (f32[2,128,256]{2,1,0:T(8,128)S(1)}, f32[2,128,256]{2,1,0:T(8,128)S(1)}, u32[]{:S(2)}, u32[]{:S(2)}) collective-permute-start(f32[2,128,256]{2,1,0:T(8,128)S(1)} %pad_maximum_fusion.1), channel_id=1, source_target_pairs={{8,0},{16,8},{24,16},{32,24},{40,32},{48,40},{56,48},{64,56},{72,6... | collective-permute-start | bytes 786440 | tf_op jit(solution)/shard_map/ppermute | solution.py:655
  82.9 2.9 %copy-start.4 = (f32[2,128,256]{2,1,0:T(8,128)}, f32[2,128,256]{2,1,0:T(8,128)S(1)}, u32[]{:S(2)}) copy-start(f32[2,128,256]{2,1,0:T(8,128)S(1)} %collective-permute-done.6.above) | copy-start | bytes 786436
  85.7 0.7 copy-start.5
  180.0 5.6 %copy-start.3 = (f32[2,256,256]{2,1,0:T(8,128)S(1)}, f32[2,256,256]{2,1,0:T(8,128)}, u32[]{:S(2)}) copy-start(f32[2,256,256]{2,1,0:T(8,128)} %get-tuple-element.65) | copy-start | bytes 1572868

commit v4 on v3

--- a/solution.py
+++ b/solution.py
@@ -59,7 +59,7 @@
     return jnp.dot(jnp.concatenate([high, low, high], axis=1), table, preferred_element_type=jnp.float32)
 
 
-def visit(obj, grad, probe, seen, slot, lefts, rights, pick, acc, row, block, block_end, shift):
+def visit(obj, grad, probe, seen, slot, lefts, rights, pick, acc, row, block, block_end, shift, ready=None):
     lane = lax.broadcasted_iota(jnp.int32, (M, HALF), 1)
     wraps = lane < shift
     rows = pl.ds(row, M)
@@ -116,6 +116,8 @@
     back_im = jnp.concatenate([plus[low], minus[low]], axis=0)
 
     grads = (probe_re * back_re + probe_im * back_im, probe_re * back_im - probe_im * back_re)
+    if ready is not None:
+        ready()
     for part, g in enumerate(grads):
         first = g[:, top]
         grad[part, block, rows, :] += jnp.where(wraps, 0.0, first)
@@ -154,6 +156,17 @@
     return [(block_of(tile, block), buffer.at[:, place, pl.ds(first_row, TILE)]) for place, block in slots]
 
 
+def border_pairs(tile, buffer, slots):
+    pairs = []
+    for place, block in slots:
+        spans = ((0, TILE),) if block in (0, 1, 6, 7) else ((0, 2 * HALF), (TILE - 2 * HALF, 2 * HALF))
+        for at, size in spans:
+            pairs.append(
+                (tile.at[:, pl.ds(at, size), pl.ds(HALF * block, HALF)], buffer.at[:, place, pl.ds(HALF + at, size)])
+            )
+    return pairs
+
+
 def band_pairs(up, down, buffer, slots):
     pairs = []
     for place, block in slots:
@@ -243,18 +256,18 @@
     centers, live, probe, lefts, rights, pick, field, up, down, measured,
     left, right, above, below, grad_in, acc_in, losses_in,
     grad_out, acc, losses, up_out, down_out, gleft, gright, gabove, gbelow,
-    obj, grad, seen, sems, slot_sems,
+    obj, grad, seen, sems, slot_sems, grad_sems, loaded,
 ):
     slots = [(j + 1, j) for j in range(8)]
     loads = start_all(
-        inner_pairs(field, obj, slots, HALF)
+        border_pairs(field, obj, slots)
         + band_pairs(up, down, obj, slots)
         + strip_pairs(left, above, below, 0, obj, 0)
-        + strip_pairs(right, above, below, 1, obj, 9)
-        + inner_pairs(grad_in, grad, slots, HALF),
+        + strip_pairs(right, above, below, 1, obj, 9),
         sems,
     )
     fetch_slots(live, centers, is_outer, measured, seen, slot_sems)
+    grad_loads = start_all(border_pairs(grad_in, grad, slots), grad_sems)
     for place_at in (0, 9):
         grad[:, place_at] = jnp.zeros((2, ROWS, HALF), jnp.float32)
     for row_at in (0, HALF + TILE):
@@ -263,18 +276,26 @@
     for s in range(SLOTS_HERE):
         losses[s] = losses_in[s]
     wait_all(loads)
+    loaded[0] = 0
+
+    def have_grads():
+        @pl.when(loaded[0] == 0)
+        def _():
+            wait_all(grad_loads)
+            loaded[0] = 1
 
     def body(s, row, block, block_end, shift):
-        return visit(obj, grad, probe, seen, s, lefts, rights, pick, acc, row, block, block_end, shift)
+        return visit(obj, grad, probe, seen, s, lefts, rights, pick, acc, row, block, block_end, shift, have_grads)
 
     run_slots(live, centers, is_outer, 0, 10, measured, seen, slot_sems, losses, body)
+    have_grads()
     wait_all(
         start_all(
             flipped(
-                inner_pairs(grad_out, grad, slots, HALF)
+                strip_pairs(gleft, gabove, gbelow, 0, grad, 0)
+                + strip_pairs(gright, gabove, gbelow, 1, grad, 9)
                 + band_pairs(up_out, down_out, grad, slots)
-                + strip_pairs(gleft, gabove, gbelow, 0, grad, 0)
-                + strip_pairs(gright, gabove, gbelow, 1, grad, 9)
+                + border_pairs(grad_out, grad, slots)
             ),
             sems,
         )
@@ -327,7 +348,7 @@
         out_shape=TILE_OUT + (shaped(2, HALF, TILE),) * 2 + (shaped(2, TILE, HALF),) * 2 + (shaped(2, HALF, 2 * HALF),) * 2,
         in_specs=[SMEM_SPEC] * 2 + [VMEM_SPEC] * 4 + [HBM_SPEC] * 9 + [VMEM_SPEC, SMEM_SPEC],
         out_specs=TILE_SPECS + (HBM_SPEC,) * 6,
-        scratch_shapes=slot_scratch(10, 38),
+        scratch_shapes=slot_scratch(10, 34) + [pltpu.SemaphoreType.DMA((12,)), pltpu.SMEM((1,), jnp.int32)],
         input_output_aliases={14: 0},
         compiler_params=pltpu.CompilerParams(vmem_limit_bytes=VMEM),
         cost_estimate=cost(SLOTS_HERE // 2),
@@ -691,9 +712,10 @@
 
 def on_device(field, probe, centers, live, measured):
     tables = tuple(jnp.asarray(t) for t in host_tables())
-    left, right = to_right(field[:, :, TILE - HALF :]), to_left(field[:, :, :HALF])
-    top_rows = field[:, :HALF]
-    relayed, up, straight = crossing_first(top_rows), to_down(field[:, TILE - HALF :]), to_up_straight(top_rows)
+    last, first, later = lax.optimization_barrier((field[:, :, TILE - HALF :], field[:, :, :HALF], field))
+    left, right = to_right(last), to_left(first)
+    top_rows = later[:, :HALF]
+    relayed, up, straight = crossing_first(top_rows), to_down(later[:, TILE - HALF :]), to_up_straight(top_rows)
     grad, acc, losses = inner_slots(centers, live, probe, tables, field, measured)
     relayed, acc = lax.optimization_barrier((relayed, acc))
     second = crossing_second(relayed)

time: 187 us -> 188 us (level)
  waiting for transfers between devices: 40.1 us -> 44 us
  Pallas kernels: 116 us -> 113 us
    pallas_call x1, Pallas kernels: 16.5 us -> 12.4 us  [inner_slots(): pl.pallas_call(inner_kernel, out_shape=TILE_OUT, in_specs=[SMEM_SPEC] * 2...]
    ppermute x5, waiting for transfers between devices: 40 us -> 44 us  [shift_by_one(): return lax.ppermute(x, axis, steps)]
    pallas_call x1, Pallas kernels: 73.3 us -> 75.4 us  [send_back(): pl.pallas_call(functools.partial(return_kernel, scale), out_shape=(shaped...]
  transfers between devices with their start and end apart: 8 -> 8, of which waited for: 3 -> 2; matrix products, arithmetic and copies ran while one was open for 3% -> 2% of each run, Pallas kernels for 9% -> 7%
where the time goes in v4:
time: 188 us; the launch traced here: 186 us
  Pallas kernels  113 us (60%)
  waiting for transfers between devices  44 us (23%)
  starting transfers between devices  18.3 us (10%)
  local copies, waits for them, and re-layouts  8.4 us (4%)
  other arithmetic  2.44 us (1%)
    pallas_call x1, Pallas kernels, send_back(): pl.pallas_call(functools.partial(return_kernel, scale), out_shape=(shaped...  75.4 us
    ppermute x5, waiting for transfers between devices, shift_by_one(): return lax.ppermute(x, axis, steps)  44 us
    pallas_call x1, Pallas kernels, outer_slots(): pl.pallas_call(outer_kernel, out_shape=TILE_OUT + (shaped(2, HALF, TILE),...  19.1 us
    ppermute x5, starting transfers between devices, shift_by_one(): return lax.ppermute(x, axis, steps)  12.6 us
    pallas_call x1, Pallas kernels, inner_slots(): pl.pallas_call(inner_kernel, out_shape=TILE_OUT, in_specs=[SMEM_SPEC] * 2...  12.4 us
    pallas_call x1, Pallas kernels, fold(): pl.pallas_call(fold_kernel, out_shape=shaped(2, TILE, TILE), in_specs=[HB...  5.58 us
  transfers between devices with their start and end apart: 8, of which 2 were waited for; matrix products, arithmetic and copies ran while one was open for 2% of the time, Pallas kernels for 7%

profile of v4, /device:TPU:1, one launch (start us, length us, event | category | flops | bytes accessed | tf_op | source)
XLA Modules:
  0.0 186.5 jit_solution(360074534349163572)
XLA Ops:
  0.6 0.0 copy-start.6
  0.6 3.1 %fusion.1 = (f32[2,1024,128]{2,1,0:T(8,128)}, f32[2,1024,128]{2,1,0:T(8,128)}) fusion(f32[2,1024,1024]{2,1,0:T(8,128)} %field.3), kind=kLoop, calls=%fused_computation.3 | loop fusion | bytes 4194304 | tf_op jit(solution)/shard_map/slice | solution.py:715
  3.7 3.1 %fusion = (f32[2,128,1024]{2,1,0:T(8,128)}, f32[2,128,1024]{2,1,0:T(8,128)}) fusion(f32[2,1024,1024]{2,1,0:T(8,128)} %field.3), kind=kLoop, calls=%fused_computation.2 | loop fusion | bytes 4194304 | tf_op jit(solution)/shard_map/slice | solution.py:717
  6.8 1.6 collective-permute-start.4
  8.5 3.3 %collective-permute-start.3 = (f32[2,128,1024]{2,1,0:T(8,128)}, f32[2,128,1024]{2,1,0:T(8,128)}, u32[]{:S(2)}, u32[]{:S(2)}) collective-permute-start(f32[2,128,1024]{2,1,0:T(8,128)} %get-tuple-element.57), channel_id=1, source_target_pairs={{8,0},{16,8},{24,16},{32,24},{40,32},{48,40},{56,48},{72,64},{80,7... | collective-permute-start | bytes 3145736 | tf_op jit(solution)/shard_map/ppermute | solution.py:710
  11.8 3.7 %collective-permute-start = (f32[2,1024,128]{2,1,0:T(8,128)}, f32[2,1024,128]{2,1,0:T(8,128)S(1)}, u32[]{:S(2)}, u32[]{:S(2)}) collective-permute-start(f32[2,1024,128]{2,1,0:T(8,128)} %get-tuple-element.30), channel_id=1, source_target_pairs={{0,1},{1,2},{2,3},{3,4},{4,5},{5,6},{6,7},{8,9},{9,10},{10,11},{11... | collective-permute-start | bytes 3145736 | tf_op jit(solution)/shard_map/ppermute | solution.py:676
  15.5 1.3 collective-permute-start.1
  16.8 3.3 %collective-permute-start.2 = (f32[2,128,1024]{2,1,0:T(8,128)}, f32[2,128,1024]{2,1,0:T(8,128)S(1)}, u32[]{:S(2)}, u32[]{:S(2)}) collective-permute-start(f32[2,128,1024]{2,1,0:T(8,128)} %get-tuple-element.58), channel_id=1, source_target_pairs={{0,8},{8,16},{16,24},{24,32},{32,40},{40,48},{48,56},{56,64},{64,7... | collective-permute-start | bytes 3145736 | tf_op jit(solution)/shard_map/ppermute | solution.py:676
  20.1 0.0 copy-done.6
  20.1 0.7 copy.14.centers
  20.8 12.4 %inner_slots.1 = (f32[2,1024,1024]{2,1,0:T(8,128)}, f32[2,2,256,128]{3,2,1,0:T(8,128)}, f32[16]{0:T(128)}) custom-call(s32[16,2]{1,0:T(8,128)} %copy.14.centers, s32[16]{0:T(128)} %live.3, f32[2,256,256]{2,1,0:T(8,128)} %probe.3, bf16[4,256,768]{2,1,0:T(8,128)(2,1)} %constant.6.clone.lefts, bf16[4,768,256]{2,1,0:T(8,128)(2,1)} %constant.7.clone.rights, ...), custom_call_target="tpu_custom_call" | custom-call | flops 13958643712 | bytes 31457280 | tf_op jit(solution)/shard_map/inner_slots/pallas_call | solution.py:333
  33.2 0.0 collective-permute-done.4
  33.2 0.7 collective-permute-start.5
  34.0 41.1 %collective-permute-done.left = f32[2,1024,128]{2,1,0:T(8,128)S(1)} collective-permute-done((f32[2,1024,128]{2,1,0:T(8,128)}, f32[2,1024,128]{2,1,0:T(8,128)S(1)}, u32[]{:S(2)}, u32[]{:S(2)}) %collective-permute-start) | collective-permute-done | bytes 1048608 | tf_op jit(solution)/shard_map/ppermute | solution.py:676
  75.1 0.0 copy-start
  75.1 0.0 collective-permute-done.1.right
  75.1 0.0 copy-start.1
  75.1 0.0 collective-permute-done.2.up
  75.1 0.0 copy-start.2
  75.1 0.0 collective-permute-done.3
  75.2 1.9 %collective-permute-start.6 = (f32[2,128,256]{2,1,0:T(8,128)S(1)}, f32[2,128,256]{2,1,0:T(8,128)S(1)}, u32[]{:S(2)}, u32[]{:S(2)}) collective-permute-start(f32[2,128,256]{2,1,0:T(8,128)S(1)} %pad_maximum_fusion), channel_id=1, source_target_pairs={{0,8},{8,16},{16,24},{24,32},{32,40},{40,48},{48,56},{56,64},{64,7... | collective-permute-start | bytes 786440 | tf_op jit(solution)/shard_map/ppermute | solution.py:676
  77.1 2.4 %collective-permute-start.7 = (f32[2,128,256]{2,1,0:T(8,128)S(1)}, f32[2,128,256]{2,1,0:T(8,128)S(1)}, u32[]{:S(2)}, u32[]{:S(2)}) collective-permute-start(f32[2,128,256]{2,1,0:T(8,128)S(1)} %pad_maximum_fusion.1), channel_id=1, source_target_pairs={{8,0},{16,8},{24,16},{32,24},{40,32},{48,40},{56,48},{64,56},{72,6... | collective-permute-start | bytes 786440 | tf_op jit(solution)/shard_map/ppermute | solution.py:676
  79.6 0.0 collective-permute-done.5
  79.6 2.4 %add.3.down = f32[2,128,1024]{2,1,0:T(8,128)} add(f32[2,128,1024]{2,1,0:T(8,128)} %collective-permute-done.3, f32[2,128,1024]{2,1,0:T(8,128)S(1)} %collective-permute-done.5) | non-fusion elementwise | flops 262144 | bytes 3145728 | tf_op jit(solution)/shard_map/add | solution.py:725
  82.0 0.0 collective-permute-done.6.above
  82.0 0.0 copy-start.4
  82.0 2.8 %collective-permute-done.7.below = f32[2,128,256]{2,1,0:T(8,128)S(1)} collective-permute-done((f32[2,128,256]{2,1,0:T(8,128)S(1)}, f32[2,128,256]{2,1,0:T(8,128)S(1)}, u32[]{:S(2)}, u32[]{:S(2)}) %collective-permute-start.7) | collective-permute-done | bytes 262176 | tf_op jit(solution)/shard_map/ppermute | solution.py:676
  84.8 0.0 copy-start.5
  84.8 0.0 copy-done
  84.8 0.0 copy-done.1
  84.8 0.0 copy-done.2
  84.8 0.0 copy-done.4
  84.9 0.7 copy-done.5
  85.5 19.1 %outer_slots.1 = (f32[2,1024,1024]{2,1,0:T(8,128)}, f32[2,2,256,128]{3,2,1,0:T(8,128)}, f32[16]{0:T(128)}, f32[2,128,1024]{2,1,0:T(8,128)}, f32[2,128,1024]{2,1,...) custom-call(s32[16,2]{1,0:T(8,128)} %copy.14.centers, ...), custom_call_target="tpu_custom_call", output_to_operand_aliasing={{0}: (14, {})} | custom-call | flops 6979321856 | bytes 31457280 | tf_op jit(solution)/shard_map/outer_slots/pallas_call | solution.py:346
  104.7 75.4 %send_back.1 = (f32[2,1024,128]{2,1,0:T(8,128)}, f32[2,1024,128]{2,1,0:T(8,128)}, f32[2,128,1024]{2,1,0:T(8,128)}, f32[2,128,1024]{2,1,0:T(8,128)}, f32[2,256,256]{2,1,0:T(8,128)}) custom-call(f32[2,1024,128]{2,1,0:T(8,128)} %get-tuple-element.43.gleft, f32[2,1024,128]{2,1,0:T(8,128)} %get-tuple-element.44.gright, f32[2,128,256]{2,1,0:T(8,128)} %get-tuple-element.45.gabove, ...), custom_call_target="tpu_custom_call" | custom-call | flops 524288 | bytes 104857600 | tf_op jit(solution)/shard_map/send_back/pallas_call | solution.py:584
  180.1 0.0 copy-start.3
  180.1 5.6 %fold.1 = f32[2,1024,1024]{2,1,0:T(8,128)} custom-call(f32[2,1024,128]{2,1,0:T(8,128)} %get-tuple-element.50.got_left, f32[2,1024,128]{2,1,0:T(8,128)} %get-tuple-element.51.got_right, f32[2,128,1024]{2,1,0:T(8,128)} %get-tuple-element.52.got_up, f32[2,128,1024]{2,1,0:T(8,128)} %get-tuple-element.53.got_down, ...), custom_call_target="tpu_custom_call", output_to_operand_aliasing={{}: (4, {})} | custom-call | tf_op jit(solution)/shard_map/fold/pallas_call | solution.py:655
  185.7 0.0 copy-done.3
  185.7 0.8 copy.18
  (3 shorter events, 0.1 us)
Async XLA Ops:
  0.6 19.5 %copy-start.6 = (s32[16,2]{0,1:T(2,128)S(1)}, s32[16,2]{0,1:T(2,128)}, u32[]{:S(2)}) copy-start(s32[16,2]{0,1:T(2,128)} %param.10) | copy-start | bytes 388
  6.8 26.4 %collective-permute-start.4 = (f32[2,128,1024]{2,1,0:T(8,128)}, f32[2,128,1024]{2,1,0:T(8,128)}, u32[]{:S(2)}, u32[]{:S(2)}) collective-permute-start(f32[2,128,1024]{2,1,0:T(8,128)} %get-tuple-element.57), channel_id=1, source_target_pairs={{64,57},{66,59},{68,61},{70,63},{65,64},{67,66},{69,68},{71,70}} | collective-permute-start | bytes 3145736 | tf_op jit(solution)/shard_map/ppermute | solution.py:696
  8.5 66.6 %collective-permute-start.3 = (f32[2,128,1024]{2,1,0:T(8,128)}, f32[2,128,1024]{2,1,0:T(8,128)}, u32[]{:S(2)}, u32[]{:S(2)}) collective-permute-start(f32[2,128,1024]{2,1,0:T(8,128)} %get-tuple-element.57), channel_id=1, source_target_pairs={{8,0},{16,8},{24,16},{32,24},{40,32},{48,40},{56,48},{72,64},{80,7... | collective-permute-start | bytes 3145736 | tf_op jit(solution)/shard_map/ppermute | solution.py:710
  11.8 63.3 %collective-permute-start = (f32[2,1024,128]{2,1,0:T(8,128)}, f32[2,1024,128]{2,1,0:T(8,128)S(1)}, u32[]{:S(2)}, u32[]{:S(2)}) collective-permute-start(f32[2,1024,128]{2,1,0:T(8,128)} %get-tuple-element.30), channel_id=1, source_target_pairs={{0,1},{1,2},{2,3},{3,4},{4,5},{5,6},{6,7},{8,9},{9,10},{10,11},{11... | collective-permute-start | bytes 3145736 | tf_op jit(solution)/shard_map/ppermute | solution.py:676
  15.5 59.6 %collective-permute-start.1 = (f32[2,1024,128]{2,1,0:T(8,128)}, f32[2,1024,128]{2,1,0:T(8,128)S(1)}, u32[]{:S(2)}, u32[]{:S(2)}) collective-permute-start(f32[2,1024,128]{2,1,0:T(8,128)} %get-tuple-element.31), channel_id=1, source_target_pairs={{1,0},{2,1},{3,2},{4,3},{5,4},{6,5},{7,6},{9,8},{10,9},{11,10},{12... | collective-permute-start | bytes 3145736 | tf_op jit(solution)/shard_map/ppermute | solution.py:676
  16.8 58.3 %collective-permute-start.2 = (f32[2,128,1024]{2,1,0:T(8,128)}, f32[2,128,1024]{2,1,0:T(8,128)S(1)}, u32[]{:S(2)}, u32[]{:S(2)}) collective-permute-start(f32[2,128,1024]{2,1,0:T(8,128)} %get-tuple-element.58), channel_id=1, source_target_pairs={{0,8},{8,16},{16,24},{24,32},{32,40},{40,48},{48,56},{56,64},{64,7... | collective-permute-start | bytes 3145736 | tf_op jit(solution)/shard_map/ppermute | solution.py:676
  33.2 46.3 %collective-permute-start.5 = (f32[2,128,1024]{2,1,0:T(8,128)}, f32[2,128,1024]{2,1,0:T(8,128)S(1)}, u32[]{:S(2)}, u32[]{:S(2)}) collective-permute-start(f32[2,128,1024]{2,1,0:T(8,128)} %collective-permute-done.4), channel_id=1, source_target_pairs={{57,56},{59,58},{61,60},{63,62},{64,57},{66,59},{68,61},{70,63}} | collective-permute-start | bytes 3145736 | tf_op jit(solution)/shard_map/ppermute | solution.py:696
  75.1 9.8 %copy-start = (f32[2,1024,128]{2,1,0:T(8,128)}, f32[2,1024,128]{2,1,0:T(8,128)S(1)}, u32[]{:S(2)}) copy-start(f32[2,1024,128]{2,1,0:T(8,128)S(1)} %collective-permute-done.left) | copy-start | bytes 3145732
  75.1 9.8 %copy-start.1 = (f32[2,1024,128]{2,1,0:T(8,128)}, f32[2,1024,128]{2,1,0:T(8,128)S(1)}, u32[]{:S(2)}) copy-start(f32[2,1024,128]{2,1,0:T(8,128)S(1)} %collective-permute-done.1.right) | copy-start | bytes 3145732
  75.1 9.7 %copy-start.2 = (f32[2,128,1024]{2,1,0:T(8,128)}, f32[2,128,1024]{2,1,0:T(8,128)S(1)}, u32[]{:S(2)}) copy-start(f32[2,128,1024]{2,1,0:T(8,128)S(1)} %collective-permute-done.2.up) | copy-start | bytes 3145732
  75.2 6.8 %collective-permute-start.6 = (f32[2,128,256]{2,1,0:T(8,128)S(1)}, f32[2,128,256]{2,1,0:T(8,128)S(1)}, u32[]{:S(2)}, u32[]{:S(2)}) collective-permute-start(f32[2,128,256]{2,1,0:T(8,128)S(1)} %pad_maximum_fusion), channel_id=1, source_target_pairs={{0,8},{8,16},{16,24},{24,32},{32,40},{40,48},{48,56},{56,64},{64,7... | collective-permute-start | bytes 786440 | tf_op jit(solution)/shard_map/ppermute | solution.py:676
  77.1 7.7 %collective-permute-start.7 = (f32[2,128,256]{2,1,0:T(8,128)S(1)}, f32[2,128,256]{2,1,0:T(8,128)S(1)}, u32[]{:S(2)}, u32[]{:S(2)}) collective-permute-start(f32[2,128,256]{2,1,0:T(8,128)S(1)} %pad_maximum_fusion.1), channel_id=1, source_target_pairs={{8,0},{16,8},{24,16},{32,24},{40,32},{48,40},{56,48},{64,56},{72,6... | collective-permute-start | bytes 786440 | tf_op jit(solution)/shard_map/ppermute | solution.py:676
  82.0 2.9 %copy-start.4 = (f32[2,128,256]{2,1,0:T(8,128)}, f32[2,128,256]{2,1,0:T(8,128)S(1)}, u32[]{:S(2)}) copy-start(f32[2,128,256]{2,1,0:T(8,128)S(1)} %collective-permute-done.6.above) | copy-start | bytes 786436
  84.8 0.7 copy-start.5
  180.1 5.6 %copy-start.3 = (f32[2,256,256]{2,1,0:T(8,128)S(1)}, f32[2,256,256]{2,1,0:T(8,128)}, u32[]{:S(2)}) copy-start(f32[2,256,256]{2,1,0:T(8,128)} %get-tuple-element.71) | copy-start | bytes 1572868

commit v5 on v4

--- a/solution.py
+++ b/solution.py
@@ -74,8 +74,10 @@
     wave_re = probe_re * obj_re - probe_im * obj_im
     wave_im = probe_re * obj_im + probe_im * obj_re
     top, low = slice(0, HALF), slice(HALF, M)
+    yield None
     even = left_product(lefts[0], jnp.concatenate([wave_re[top] + wave_re[low], wave_im[top] + wave_im[low]], axis=0))
     odd = left_product(lefts[2], jnp.concatenate([wave_re[top] - wave_re[low], wave_im[top] - wave_im[low]], axis=0))
+    yield None
     half_re = jnp.concatenate([even[top], odd[top]], axis=0)
     half_im = jnp.concatenate([even[low], odd[low]], axis=0)
     far_e = right_product(
@@ -84,6 +86,7 @@
     far_o = right_product(
         jnp.concatenate([half_re[:, top] - half_re[:, low], half_im[:, top] - half_im[:, low]], axis=1), rights[3]
     )
+    yield None
     meas = jnp.concatenate(
         [
             jnp.concatenate([seen[slot, side, pl.ds(odd, HALF, stride=2), :] for side in range(2)], axis=1)
@@ -104,18 +107,22 @@
     back_e, loss_e = residual(far_e, meas[:, top])
     back_o, loss_o = residual(far_o, meas[:, low])
     loss = jnp.sum(loss_e + loss_o) * (0.5 / (M * M))
+    yield None
     up = right_product(back_e, rights[0])
     vp = right_product(back_o, rights[2])
+    yield None
     plus, minus = up + vp, up - vp
     half_re = jnp.concatenate([plus[:, top], minus[:, top]], axis=1)
     half_im = jnp.concatenate([plus[:, low], minus[:, low]], axis=1)
     up = left_product(lefts[1], jnp.concatenate([half_re[top], half_im[top]], axis=0))
     vp = left_product(lefts[3], jnp.concatenate([half_re[low], half_im[low]], axis=0))
+    yield None
     plus, minus = up + vp, up - vp
     back_re = jnp.concatenate([plus[top], minus[top]], axis=0)
     back_im = jnp.concatenate([plus[low], minus[low]], axis=0)
 
     grads = (probe_re * back_re + probe_im * back_im, probe_re * back_im - probe_im * back_re)
+    yield None
     if ready is not None:
         ready()
     for part, g in enumerate(grads):
@@ -129,7 +136,7 @@
         turned = pltpu.roll(term, unshift, 1)
         acc[part, 0] += turned[:, top]
         acc[part, 1] += turned[:, low]
-    return loss
+    yield loss
 
 
 INNER_COST = SLOTS_HERE
@@ -194,31 +201,53 @@
     ]
 
 
-def fetch_slots(live, centers, wanted, measured, seen, slot_sems):
+def fetch_slots(live, centers, wanted, measured, seen, slot_sems, order):
+    order[SLOTS_HERE] = 0
+
     def fetch(s, carry):
         @pl.when(wanted(live[s], centers[s, 0], centers[s, 1]))
         def _():
             for copy in slot_copies(measured, seen, slot_sems, s):
                 copy.start()
+            count = order[SLOTS_HERE]
+            order[count] = s
+            order[SLOTS_HERE] = count + 1
 
         return carry
 
     lax.fori_loop(0, SLOTS_HERE, fetch, 0)
 
 
-def run_slots(live, centers, wanted, offset, blocks, measured, seen, slot_sems, losses, body):
-    def step(s, carry):
-        row, column = centers[s, 0], centers[s, 1]
-
-        @pl.when(wanted(live[s], row, column))
-        def _():
+def run_slots(centers, offset, blocks, measured, seen, slot_sems, order, losses, body):
+    def together(first, size):
+        chosen = [order[first + i] for i in range(size)]
+        for s in chosen:
             wait_all(slot_copies(measured, seen, slot_sems, s))
-            block = lax.div(column - offset, HALF)
-            losses[s] = body(s, row - offset, block, jnp.minimum(block + 2, blocks - 1), lax.rem(column - offset, HALF))
-
+        runs = []
+        for i, s in enumerate(chosen):
+            row, column = centers[s, 0] - offset, centers[s, 1] - offset
+            block = lax.div(column, HALF)
+            runs.append(body(i, s, row, block, jnp.minimum(block + 2, blocks - 1), lax.rem(column, HALF)))
+        finished = 0
+        while finished < size:
+            for s, run in zip(chosen, runs):
+                loss = next(run)
+                if loss is not None:
+                    losses[s] = loss
+                    finished += 1
+
+    count = order[SLOTS_HERE]
+    pairs = lax.div(count, 2)
+
+    def step(p, carry):
+        together(2 * p, 2)
         return carry
 
-    lax.fori_loop(0, SLOTS_HERE, step, 0)
+    lax.fori_loop(0, pairs, step, 0)
+
+    @pl.when(count > 2 * pairs)
+    def _():
+        together(count - 1, 1)
 
 
 def within(row, column):
@@ -234,21 +263,21 @@
 
 
 def inner_kernel(
-    centers, live, probe, lefts, rights, pick, field, measured, grad_out, acc, losses, obj, grad, seen, sems, slot_sems
+    centers, live, probe, lefts, rights, pick, field, measured, grad_out, acc, losses, obj, grad, seen, sems, slot_sems, order
 ):
     slots = [(j, j) for j in range(8)]
     loads = start_all(inner_pairs(field, obj, slots, 0), sems)
-    fetch_slots(live, centers, is_inner, measured, seen, slot_sems)
+    fetch_slots(live, centers, is_inner, measured, seen, slot_sems, order)
     grad[...] = jnp.zeros_like(grad)
     acc[...] = jnp.zeros_like(acc)
     for s in range(SLOTS_HERE):
         losses[s] = 0.0
     wait_all(loads)
 
-    def body(s, row, block, block_end, shift):
+    def body(i, s, row, block, block_end, shift):
         return visit(obj, grad, probe, seen, s, lefts, rights, pick, acc, row, block, block_end, shift)
 
-    run_slots(live, centers, is_inner, HALF, 8, measured, seen, slot_sems, losses, body)
+    run_slots(centers, HALF, 8, measured, seen, slot_sems, order, losses, body)
     wait_all(start_all(flipped(inner_pairs(grad_out, grad, slots, 0)), sems))
 
 
@@ -256,7 +285,7 @@
     centers, live, probe, lefts, rights, pick, field, up, down, measured,
     left, right, above, below, grad_in, acc_in, losses_in,
     grad_out, acc, losses, up_out, down_out, gleft, gright, gabove, gbelow,
-    obj, grad, seen, sems, slot_sems, grad_sems, loaded,
+    obj, grad, seen, sems, slot_sems, order, grad_sems, loaded,
 ):
     slots = [(j + 1, j) for j in range(8)]
     loads = start_all(
@@ -266,7 +295,7 @@
         + strip_pairs(right, above, below, 1, obj, 9),
         sems,
     )
-    fetch_slots(live, centers, is_outer, measured, seen, slot_sems)
+    fetch_slots(live, centers, is_outer, measured, seen, slot_sems, order)
     grad_loads = start_all(border_pairs(grad_in, grad, slots), grad_sems)
     for place_at in (0, 9):
         grad[:, place_at] = jnp.zeros((2, ROWS, HALF), jnp.float32)
@@ -284,10 +313,10 @@
             wait_all(grad_loads)
             loaded[0] = 1
 
-    def body(s, row, block, block_end, shift):
-        return visit(obj, grad, probe, seen, s, lefts, rights, pick, acc, row, block, block_end, shift, have_grads)
-
-    run_slots(live, centers, is_outer, 0, 10, measured, seen, slot_sems, losses, body)
+    def body(i, s, row, block, block_end, shift):
+        return visit(obj, grad, probe, seen, s, lefts, rights, pick, acc, row, block, block_end, shift, None if i else have_grads)
+
+    run_slots(centers, 0, 10, measured, seen, slot_sems, order, losses, body)
     have_grads()
     wait_all(
         start_all(
@@ -318,6 +347,7 @@
         pltpu.VMEM((SLOTS_HERE, 2, M, HALF), jnp.float32),
         pltpu.SemaphoreType.DMA((copies,)),
         pltpu.SemaphoreType.DMA((SLOTS_HERE, 2)),
+        pltpu.SMEM((SLOTS_HERE + 1,), jnp.int32),
     ]
 
 

time: 188 us -> 184 us (0.979)
  waiting for transfers between devices: 44 us -> 38 us
  Pallas kernels: 113 us -> 115 us
    pallas_call x1, Pallas kernels: 12.4 us -> 18.4 us  [inner_slots(): pl.pallas_call(inner_kernel, out_shape=TILE_OUT, in_specs=[SMEM_SPEC] * 2...]
    ppermute x5, waiting for transfers between devices: 44 us -> 38 us  [shift_by_one(): return lax.ppermute(x, axis, steps)]
  transfers between devices with their start and end apart: 8 -> 8, of which waited for: 2 -> 2; matrix products, arithmetic and copies ran while one was open for 2% -> 2% of each run, Pallas kernels for 7% -> 10%
where the time goes in v5:
time: 184 us; the launch traced here: 183 us
  Pallas kernels  115 us (62%)
  waiting for transfers between devices  38 us (21%)
  starting transfers between devices  18.3 us (10%)
  local copies, waits for them, and re-layouts  8.4 us (5%)
  other arithmetic  2.44 us (1%)
    pallas_call x1, Pallas kernels, send_back(): pl.pallas_call(functools.partial(return_kernel, scale), out_shape=(shaped...  73.6 us
    ppermute x5, waiting for transfers between devices, shift_by_one(): return lax.ppermute(x, axis, steps)  38 us
    pallas_call x1, Pallas kernels, inner_slots(): pl.pallas_call(inner_kernel, out_shape=TILE_OUT, in_specs=[SMEM_SPEC] * 2...  18.4 us
    pallas_call x1, Pallas kernels, outer_slots(): pl.pallas_call(outer_kernel, out_shape=TILE_OUT + (shaped(2, HALF, TILE),...  17.8 us
    ppermute x5, starting transfers between devices, shift_by_one(): return lax.ppermute(x, axis, steps)  12.6 us
    pallas_call x1, Pallas kernels, fold(): pl.pallas_call(fold_kernel, out_shape=shaped(2, TILE, TILE), in_specs=[HB...  5.58 us
  transfers between devices with their start and end apart: 8, of which 2 were waited for; matrix products, arithmetic and copies ran while one was open for 2% of the time, Pallas kernels for 10%

profile of v5, /device:TPU:1, one launch (start us, length us, event | category | flops | bytes accessed | tf_op | source)
XLA Modules:
  0.0 183.3 jit_solution(1217736180047939716)
XLA Ops:
  0.6 0.0 copy-start.6
  0.6 3.1 %fusion.1 = (f32[2,1024,128]{2,1,0:T(8,128)}, f32[2,1024,128]{2,1,0:T(8,128)}) fusion(f32[2,1024,1024]{2,1,0:T(8,128)} %field.3), kind=kLoop, calls=%fused_computation.3 | loop fusion | bytes 4194304 | tf_op jit(solution)/shard_map/slice | solution.py:745
  3.7 3.1 %fusion = (f32[2,128,1024]{2,1,0:T(8,128)}, f32[2,128,1024]{2,1,0:T(8,128)}) fusion(f32[2,1024,1024]{2,1,0:T(8,128)} %field.3), kind=kLoop, calls=%fused_computation.2 | loop fusion | bytes 4194304 | tf_op jit(solution)/shard_map/slice | solution.py:747
  6.8 1.6 collective-permute-start.4
  8.5 3.3 %collective-permute-start.3 = (f32[2,128,1024]{2,1,0:T(8,128)}, f32[2,128,1024]{2,1,0:T(8,128)}, u32[]{:S(2)}, u32[]{:S(2)}) collective-permute-start(f32[2,128,1024]{2,1,0:T(8,128)} %get-tuple-element.57), channel_id=1, source_target_pairs={{8,0},{16,8},{24,16},{32,24},{40,32},{48,40},{56,48},{72,64},{80,7... | collective-permute-start | bytes 3145736 | tf_op jit(solution)/shard_map/ppermute | solution.py:740
  11.8 3.7 %collective-permute-start = (f32[2,1024,128]{2,1,0:T(8,128)}, f32[2,1024,128]{2,1,0:T(8,128)S(1)}, u32[]{:S(2)}, u32[]{:S(2)}) collective-permute-start(f32[2,1024,128]{2,1,0:T(8,128)} %get-tuple-element.30), channel_id=1, source_target_pairs={{0,1},{1,2},{2,3},{3,4},{4,5},{5,6},{6,7},{8,9},{9,10},{10,11},{11... | collective-permute-start | bytes 3145736 | tf_op jit(solution)/shard_map/ppermute | solution.py:706
  15.5 1.3 collective-permute-start.1
  16.8 3.3 %collective-permute-start.2 = (f32[2,128,1024]{2,1,0:T(8,128)}, f32[2,128,1024]{2,1,0:T(8,128)S(1)}, u32[]{:S(2)}, u32[]{:S(2)}) collective-permute-start(f32[2,128,1024]{2,1,0:T(8,128)} %get-tuple-element.58), channel_id=1, source_target_pairs={{0,8},{8,16},{16,24},{24,32},{32,40},{40,48},{48,56},{56,64},{64,7... | collective-permute-start | bytes 3145736 | tf_op jit(solution)/shard_map/ppermute | solution.py:706
  20.1 0.0 copy-done.6
  20.1 0.7 copy.14.centers
  20.8 18.4 %inner_slots.1 = (f32[2,1024,1024]{2,1,0:T(8,128)}, f32[2,2,256,128]{3,2,1,0:T(8,128)}, f32[16]{0:T(128)}) custom-call(s32[16,2]{1,0:T(8,128)} %copy.14.centers, s32[16]{0:T(128)} %live.3, f32[2,256,256]{2,1,0:T(8,128)} %probe.3, bf16[4,256,768]{2,1,0:T(8,128)(2,1)} %constant.6.clone.lefts, bf16[4,768,256]{2,1,0:T(8,128)(2,1)} %constant.7.clone.rights, ...), custom_call_target="tpu_custom_call" | custom-call | flops 13958643712 | bytes 31457280 | tf_op jit(solution)/shard_map/inner_slots/pallas_call | solution.py:363
  39.2 0.0 collective-permute-done.4
  39.2 0.7 collective-permute-start.5
  39.9 35.1 %collective-permute-done.left = f32[2,1024,128]{2,1,0:T(8,128)S(1)} collective-permute-done((f32[2,1024,128]{2,1,0:T(8,128)}, f32[2,1024,128]{2,1,0:T(8,128)S(1)}, u32[]{:S(2)}, u32[]{:S(2)}) %collective-permute-start) | collective-permute-done | bytes 1048608 | tf_op jit(solution)/shard_map/ppermute | solution.py:706
  75.1 0.0 copy-start
  75.1 0.0 collective-permute-done.1.right
  75.1 0.0 copy-start.1
  75.1 0.0 collective-permute-done.2.up
  75.1 0.0 copy-start.2
  75.1 0.0 collective-permute-done.3
  75.2 1.9 %collective-permute-start.6 = (f32[2,128,256]{2,1,0:T(8,128)S(1)}, f32[2,128,256]{2,1,0:T(8,128)S(1)}, u32[]{:S(2)}, u32[]{:S(2)}) collective-permute-start(f32[2,128,256]{2,1,0:T(8,128)S(1)} %pad_maximum_fusion), channel_id=1, source_target_pairs={{0,8},{8,16},{16,24},{24,32},{32,40},{40,48},{48,56},{56,64},{64,7... | collective-permute-start | bytes 786440 | tf_op jit(solution)/shard_map/ppermute | solution.py:706
  77.1 2.4 %collective-permute-start.7 = (f32[2,128,256]{2,1,0:T(8,128)S(1)}, f32[2,128,256]{2,1,0:T(8,128)S(1)}, u32[]{:S(2)}, u32[]{:S(2)}) collective-permute-start(f32[2,128,256]{2,1,0:T(8,128)S(1)} %pad_maximum_fusion.1), channel_id=1, source_target_pairs={{8,0},{16,8},{24,16},{32,24},{40,32},{48,40},{56,48},{64,56},{72,6... | collective-permute-start | bytes 786440 | tf_op jit(solution)/shard_map/ppermute | solution.py:706
  79.6 0.0 collective-permute-done.5
  79.6 2.4 %add.3.down = f32[2,128,1024]{2,1,0:T(8,128)} add(f32[2,128,1024]{2,1,0:T(8,128)} %collective-permute-done.3, f32[2,128,1024]{2,1,0:T(8,128)S(1)} %collective-permute-done.5) | non-fusion elementwise | flops 262144 | bytes 3145728 | tf_op jit(solution)/shard_map/add | solution.py:755
  82.0 0.0 collective-permute-done.6.above
  82.0 0.0 copy-start.4
  82.0 2.8 %collective-permute-done.7.below = f32[2,128,256]{2,1,0:T(8,128)S(1)} collective-permute-done((f32[2,128,256]{2,1,0:T(8,128)S(1)}, f32[2,128,256]{2,1,0:T(8,128)S(1)}, u32[]{:S(2)}, u32[]{:S(2)}) %collective-permute-start.7) | collective-permute-done | bytes 262176 | tf_op jit(solution)/shard_map/ppermute | solution.py:706
  84.8 0.0 copy-start.5
  84.8 0.0 copy-done
  84.8 0.0 copy-done.1
  84.8 0.0 copy-done.2
  84.8 0.0 copy-done.4
  84.9 0.7 copy-done.5
  85.5 17.8 %outer_slots.1 = (f32[2,1024,1024]{2,1,0:T(8,128)}, f32[2,2,256,128]{3,2,1,0:T(8,128)}, f32[16]{0:T(128)}, f32[2,128,1024]{2,1,0:T(8,128)}, f32[2,128,1024]{2,1,...) custom-call(s32[16,2]{1,0:T(8,128)} %copy.14.centers, ...), custom_call_target="tpu_custom_call", output_to_operand_aliasing={{0}: (14, {})} | custom-call | flops 6979321856 | bytes 31457280 | tf_op jit(solution)/shard_map/outer_slots/pallas_call | solution.py:376
  103.3 73.6 %send_back.1 = (f32[2,1024,128]{2,1,0:T(8,128)}, f32[2,1024,128]{2,1,0:T(8,128)}, f32[2,128,1024]{2,1,0:T(8,128)}, f32[2,128,1024]{2,1,0:T(8,128)}, f32[2,256,256]{2,1,0:T(8,128)}) custom-call(f32[2,1024,128]{2,1,0:T(8,128)} %get-tuple-element.43.gleft, f32[2,1024,128]{2,1,0:T(8,128)} %get-tuple-element.44.gright, f32[2,128,256]{2,1,0:T(8,128)} %get-tuple-element.45.gabove, ...), custom_call_target="tpu_custom_call" | custom-call | flops 524288 | bytes 104857600 | tf_op jit(solution)/shard_map/send_back/pallas_call | solution.py:614
  176.9 0.0 copy-start.3
  176.9 5.6 %fold.1 = f32[2,1024,1024]{2,1,0:T(8,128)} custom-call(f32[2,1024,128]{2,1,0:T(8,128)} %get-tuple-element.50.got_left, f32[2,1024,128]{2,1,0:T(8,128)} %get-tuple-element.51.got_right, f32[2,128,1024]{2,1,0:T(8,128)} %get-tuple-element.52.got_up, f32[2,128,1024]{2,1,0:T(8,128)} %get-tuple-element.53.got_down, ...), custom_call_target="tpu_custom_call", output_to_operand_aliasing={{}: (4, {})} | custom-call | tf_op jit(solution)/shard_map/fold/pallas_call | solution.py:685
  182.5 0.0 copy-done.3
  182.5 0.8 copy.18
  (3 shorter events, 0.1 us)
Async XLA Ops:
  0.6 19.5 %copy-start.6 = (s32[16,2]{0,1:T(2,128)S(1)}, s32[16,2]{0,1:T(2,128)}, u32[]{:S(2)}) copy-start(s32[16,2]{0,1:T(2,128)} %param.10) | copy-start | bytes 388
  6.8 32.4 %collective-permute-start.4 = (f32[2,128,1024]{2,1,0:T(8,128)}, f32[2,128,1024]{2,1,0:T(8,128)}, u32[]{:S(2)}, u32[]{:S(2)}) collective-permute-start(f32[2,128,1024]{2,1,0:T(8,128)} %get-tuple-element.57), channel_id=1, source_target_pairs={{64,57},{66,59},{68,61},{70,63},{65,64},{67,66},{69,68},{71,70}} | collective-permute-start | bytes 3145736 | tf_op jit(solution)/shard_map/ppermute | solution.py:726
  8.5 66.6 %collective-permute-start.3 = (f32[2,128,1024]{2,1,0:T(8,128)}, f32[2,128,1024]{2,1,0:T(8,128)}, u32[]{:S(2)}, u32[]{:S(2)}) collective-permute-start(f32[2,128,1024]{2,1,0:T(8,128)} %get-tuple-element.57), channel_id=1, source_target_pairs={{8,0},{16,8},{24,16},{32,24},{40,32},{48,40},{56,48},{72,64},{80,7... | collective-permute-start | bytes 3145736 | tf_op jit(solution)/shard_map/ppermute | solution.py:740
  11.8 63.3 %collective-permute-start = (f32[2,1024,128]{2,1,0:T(8,128)}, f32[2,1024,128]{2,1,0:T(8,128)S(1)}, u32[]{:S(2)}, u32[]{:S(2)}) collective-permute-start(f32[2,1024,128]{2,1,0:T(8,128)} %get-tuple-element.30), channel_id=1, source_target_pairs={{0,1},{1,2},{2,3},{3,4},{4,5},{5,6},{6,7},{8,9},{9,10},{10,11},{11... | collective-permute-start | bytes 3145736 | tf_op jit(solution)/shard_map/ppermute | solution.py:706
  15.5 59.6 %collective-permute-start.1 = (f32[2,1024,128]{2,1,0:T(8,128)}, f32[2,1024,128]{2,1,0:T(8,128)S(1)}, u32[]{:S(2)}, u32[]{:S(2)}) collective-permute-start(f32[2,1024,128]{2,1,0:T(8,128)} %get-tuple-element.31), channel_id=1, source_target_pairs={{1,0},{2,1},{3,2},{4,3},{5,4},{6,5},{7,6},{9,8},{10,9},{11,10},{12... | collective-permute-start | bytes 3145736 | tf_op jit(solution)/shard_map/ppermute | solution.py:706
  16.8 58.3 %collective-permute-start.2 = (f32[2,128,1024]{2,1,0:T(8,128)}, f32[2,128,1024]{2,1,0:T(8,128)S(1)}, u32[]{:S(2)}, u32[]{:S(2)}) collective-permute-start(f32[2,128,1024]{2,1,0:T(8,128)} %get-tuple-element.58), channel_id=1, source_target_pairs={{0,8},{8,16},{16,24},{24,32},{32,40},{40,48},{48,56},{56,64},{64,7... | collective-permute-start | bytes 3145736 | tf_op jit(solution)/shard_map/ppermute | solution.py:706
  39.2 40.4 %collective-permute-start.5 = (f32[2,128,1024]{2,1,0:T(8,128)}, f32[2,128,1024]{2,1,0:T(8,128)S(1)}, u32[]{:S(2)}, u32[]{:S(2)}) collective-permute-start(f32[2,128,1024]{2,1,0:T(8,128)} %collective-permute-done.4), channel_id=1, source_target_pairs={{57,56},{59,58},{61,60},{63,62},{64,57},{66,59},{68,61},{70,63}} | collective-permute-start | bytes 3145736 | tf_op jit(solution)/shard_map/ppermute | solution.py:726
  75.1 9.8 %copy-start = (f32[2,1024,128]{2,1,0:T(8,128)}, f32[2,1024,128]{2,1,0:T(8,128)S(1)}, u32[]{:S(2)}) copy-start(f32[2,1024,128]{2,1,0:T(8,128)S(1)} %collective-permute-done.left) | copy-start | bytes 3145732
  75.1 9.8 %copy-start.1 = (f32[2,1024,128]{2,1,0:T(8,128)}, f32[2,1024,128]{2,1,0:T(8,128)S(1)}, u32[]{:S(2)}) copy-start(f32[2,1024,128]{2,1,0:T(8,128)S(1)} %collective-permute-done.1.right) | copy-start | bytes 3145732
  75.1 9.7 %copy-start.2 = (f32[2,128,1024]{2,1,0:T(8,128)}, f32[2,128,1024]{2,1,0:T(8,128)S(1)}, u32[]{:S(2)}) copy-start(f32[2,128,1024]{2,1,0:T(8,128)S(1)} %collective-permute-done.2.up) | copy-start | bytes 3145732
  75.2 6.8 %collective-permute-start.6 = (f32[2,128,256]{2,1,0:T(8,128)S(1)}, f32[2,128,256]{2,1,0:T(8,128)S(1)}, u32[]{:S(2)}, u32[]{:S(2)}) collective-permute-start(f32[2,128,256]{2,1,0:T(8,128)S(1)} %pad_maximum_fusion), channel_id=1, source_target_pairs={{0,8},{8,16},{16,24},{24,32},{32,40},{40,48},{48,56},{56,64},{64,7... | collective-permute-start | bytes 786440 | tf_op jit(solution)/shard_map/ppermute | solution.py:706
  77.1 7.7 %collective-permute-start.7 = (f32[2,128,256]{2,1,0:T(8,128)S(1)}, f32[2,128,256]{2,1,0:T(8,128)S(1)}, u32[]{:S(2)}, u32[]{:S(2)}) collective-permute-start(f32[2,128,256]{2,1,0:T(8,128)S(1)} %pad_maximum_fusion.1), channel_id=1, source_target_pairs={{8,0},{16,8},{24,16},{32,24},{40,32},{48,40},{56,48},{64,56},{72,6... | collective-permute-start | bytes 786440 | tf_op jit(solution)/shard_map/ppermute | solution.py:706
  82.0 2.9 %copy-start.4 = (f32[2,128,256]{2,1,0:T(8,128)}, f32[2,128,256]{2,1,0:T(8,128)S(1)}, u32[]{:S(2)}) copy-start(f32[2,128,256]{2,1,0:T(8,128)S(1)} %collective-permute-done.6.above) | copy-start | bytes 786436
  84.8 0.7 copy-start.5
  176.9 5.6 %copy-start.3 = (f32[2,256,256]{2,1,0:T(8,128)S(1)}, f32[2,256,256]{2,1,0:T(8,128)}, u32[]{:S(2)}) copy-start(f32[2,256,256]{2,1,0:T(8,128)} %get-tuple-element.71) | copy-start | bytes 1572868

commit v6 on v5

--- a/solution.py
+++ b/solution.py
@@ -150,6 +150,10 @@
     return copies
 
 
+def start_only(pairs, sems):
+    start_all(pairs, sems)
+
+
 def wait_all(copies):
     for copy in copies:
         copy.wait()
@@ -174,12 +178,12 @@
     return pairs
 
 
+def row_pairs(rows, first_row, buffer, slots):
+    return [(block_of(rows, block), buffer.at[:, place, pl.ds(first_row, HALF)]) for place, block in slots]
+
+
 def band_pairs(up, down, buffer, slots):
-    pairs = []
-    for place, block in slots:
-        pairs.append((block_of(up, block), buffer.at[:, place, pl.ds(0, HALF)]))
-        pairs.append((block_of(down, block), buffer.at[:, place, pl.ds(HALF + TILE, HALF)]))
-    return pairs
+    return row_pairs(up, 0, buffer, slots) + row_pairs(down, HALF + TILE, buffer, slots)
 
 
 def strip_pairs(strip, above, below, side, buffer, place):
@@ -282,19 +286,22 @@
 
 
 def outer_kernel(
-    centers, live, probe, lefts, rights, pick, field, up, down, measured,
+    centers, live, probe, lefts, rights, pick, field, up, straight, second, measured,
     left, right, above, below, grad_in, acc_in, losses_in,
     grad_out, acc, losses, up_out, down_out, gleft, gright, gabove, gbelow,
-    obj, grad, seen, sems, slot_sems, order, grad_sems, loaded,
+    obj, grad, seen, sems, slot_sems, order, grad_sems, down_sems, loaded,
 ):
     slots = [(j + 1, j) for j in range(8)]
     loads = start_all(
         border_pairs(field, obj, slots)
-        + band_pairs(up, down, obj, slots)
+        + row_pairs(up, 0, obj, slots)
         + strip_pairs(left, above, below, 0, obj, 0)
         + strip_pairs(right, above, below, 1, obj, 9),
         sems,
     )
+    relayed = lax.axis_index("gx") == 7
+    for chosen, rows in ((relayed, second), (jnp.logical_not(relayed), straight)):
+        pl.when(chosen)(functools.partial(start_only, row_pairs(rows, HALF + TILE, obj, slots), down_sems))
     fetch_slots(live, centers, is_outer, measured, seen, slot_sems, order)
     grad_loads = start_all(border_pairs(grad_in, grad, slots), grad_sems)
     for place_at in (0, 9):
@@ -305,6 +312,8 @@
     for s in range(SLOTS_HERE):
         losses[s] = losses_in[s]
     wait_all(loads)
+    for i, (source, target) in enumerate(row_pairs(straight, HALF + TILE, obj, slots)):
+        pltpu.make_async_copy(source, target, down_sems.at[i]).wait()
     loaded[0] = 0
 
     def have_grads():
@@ -372,18 +381,19 @@
     )(centers, live, probe, *tables, field, measured)
 
 
-def outer_slots(centers, live, probe, tables, field, up, down, measured, halos, partial):
+def outer_slots(centers, live, probe, tables, field, up, straight, second, measured, halos, partial):
     return pl.pallas_call(
         outer_kernel,
         out_shape=TILE_OUT + (shaped(2, HALF, TILE),) * 2 + (shaped(2, TILE, HALF),) * 2 + (shaped(2, HALF, 2 * HALF),) * 2,
-        in_specs=[SMEM_SPEC] * 2 + [VMEM_SPEC] * 4 + [HBM_SPEC] * 9 + [VMEM_SPEC, SMEM_SPEC],
+        in_specs=[SMEM_SPEC] * 2 + [VMEM_SPEC] * 4 + [HBM_SPEC] * 10 + [VMEM_SPEC, SMEM_SPEC],
         out_specs=TILE_SPECS + (HBM_SPEC,) * 6,
-        scratch_shapes=slot_scratch(10, 34) + [pltpu.SemaphoreType.DMA((12,)), pltpu.SMEM((1,), jnp.int32)],
-        input_output_aliases={14: 0},
+        scratch_shapes=slot_scratch(10, 34)
+        + [pltpu.SemaphoreType.DMA((12,)), pltpu.SemaphoreType.DMA((8,)), pltpu.SMEM((1,), jnp.int32)],
+        input_output_aliases={15: 0},
         compiler_params=pltpu.CompilerParams(vmem_limit_bytes=VMEM),
         cost_estimate=cost(SLOTS_HERE // 2),
         name="outer_slots",
-    )(centers, live, probe, *tables, field, up, down, measured, *halos, *partial)
+    )(centers, live, probe, *tables, field, up, straight, second, measured, *halos, *partial)
 
 
 MESH = pl.DeviceIdType.MESH
@@ -646,7 +656,7 @@
     )(gleft, gright, gabove, gbelow, gup, gdown, part.reshape(1024, HALF))
 
 
-def fold_kernel(got_left, got_right, got_up, got_down, tile, out, band, side_band, row_in, strip_in, sems):
+def fold_kernel(got_left, got_right, got_up, got_down, tile, out, band, side_band, row_in, strip_in, sems, out_sems):
     gx, gy = lax.axis_index("gx"), lax.axis_index("gy")
     end = TILE - HALF
     frame = [
@@ -657,28 +667,37 @@
     ]
     arrived = [(got_up, row_in.at[0]), (got_down, row_in.at[1]), (got_left, strip_in.at[0]), (got_right, strip_in.at[1])]
     loads = start_all(frame + arrived, sems)
-    wait_all(loads)
-    for i, there in enumerate((gx > 0, gx < 15)):
+    below, right = gx < 15, gy < 7
+    above, left = gx > 0, gy > 0
+
+    def add_strip(i, there, target, rows):
+        @pl.when(there)
+        def _():
+            target[...] += strip_in[i, :, rows]
+
+    def write(i, source, target):
+        copy = pltpu.make_async_copy(source, target, out_sems.at[i])
+        copy.start()
+        return copy
+
+    stores = []
+    for i, there in enumerate((left, right)):
+        loads[2 + i].wait()
+        loads[6 + i].wait()
+        add_strip(i, there, side_band.at[i], slice(HALF, end))
+        stores.append(write(i, side_band.at[i], out.at[:, pl.ds(HALF, CORE), pl.ds(end * i, HALF)]))
+    for i, there in enumerate((above, below)):
+        loads[i].wait()
+        loads[4 + i].wait()
+
         @pl.when(there)
         def _():
             band[i] += row_in[i]
 
-    for i, there in enumerate((gy > 0, gy < 7)):
-        lanes = slice(end * i, end * i + HALF)
-
-        @pl.when(there)
-        def _():
-            band[0, :, :, lanes] += strip_in[i, :, :HALF]
-            side_band[i] += strip_in[i, :, HALF:end]
-            band[1, :, :, lanes] += strip_in[i, :, end:]
-
-    back = [
-        (band.at[0], out.at[:, pl.ds(0, HALF)]),
-        (band.at[1], out.at[:, pl.ds(end, HALF)]),
-        (side_band.at[0], out.at[:, pl.ds(HALF, CORE), pl.ds(0, HALF)]),
-        (side_band.at[1], out.at[:, pl.ds(HALF, CORE), pl.ds(end, HALF)]),
-    ]
-    wait_all(start_all(back, sems))
+        for j, beside in enumerate((left, right)):
+            add_strip(j, beside, band.at[i, :, :, pl.ds(end * j, HALF)], slice(end * i, end * i + HALF))
+        stores.append(write(2 + i, band.at[i], out.at[:, pl.ds(end * i, HALF)]))
+    wait_all(stores)
 
 
 def fold(tile, got_left, got_right, got_up, got_down):
@@ -693,6 +712,7 @@
             pltpu.VMEM((2, 2, HALF, TILE), jnp.float32),
             pltpu.VMEM((2, 2, TILE, HALF), jnp.float32),
             pltpu.SemaphoreType.DMA((8,)),
+            pltpu.SemaphoreType.DMA((4,)),
         ],
         input_output_aliases={4: 0},
         compiler_params=pltpu.CompilerParams(vmem_limit_bytes=VMEM),
@@ -752,11 +772,10 @@
     left, right, up, straight, acc = lax.optimization_barrier((left, right, up, straight, acc))
     above = to_down(jnp.concatenate([left[:, TILE - HALF :], right[:, TILE - HALF :]], axis=2))
     below = to_up(jnp.concatenate([left[:, :HALF], right[:, :HALF]], axis=2))
-    down = straight + second
     halos = (left, right, above, below)
     partial = (grad, acc, losses)
     grad, acc, losses, gup, gdown, gleft, gright, gabove, gbelow = outer_slots(
-        centers, live, probe, tables, field, up, down, measured, halos, partial
+        centers, live, probe, tables, field, up, straight, second, measured, halos, partial
     )
     slots_all = SLOTS_HERE * lax.axis_size("gx") * lax.axis_size("gy")
     *got, probe_grad = send_back(gleft, gright, gabove, gbelow, gup, gdown, acc, 1.0 / math.sqrt(slots_all))

time: 184 us -> 183 us (level)
  Pallas kernels: 115 us -> 120 us
  waiting for transfers between devices: 38 us -> 33.4 us
  other arithmetic: 2.44 us -> 0.04 us
    pallas_call x1, Pallas kernels: 18.4 us -> 24.5 us  [inner_slots(): pl.pallas_call(inner_kernel, out_shape=TILE_OUT, in_specs=[SMEM_SPEC] * 2...]
    ppermute x5, waiting for transfers between devices: 38 us -> 33.3 us  [shift_by_one(): return lax.ppermute(x, axis, steps)]
    add x1 -> x0, other arithmetic: 2.4 us -> none  [on_device(): down = straight + second]
  transfers between devices with their start and end apart: 8 -> 8, of which waited for: 2 -> 3; matrix products, arithmetic and copies ran while one was open for 2% -> 0% of each run, Pallas kernels for 10% -> 14%
where the time goes in v6:
time: 183 us; the launch traced here: 181 us
  Pallas kernels  120 us (66%)
  waiting for transfers between devices  33.4 us (18%)
  starting transfers between devices  19.2 us (10%)
  local copies, waits for them, and re-layouts  7.93 us (4%)
    pallas_call x1, Pallas kernels, send_back(): pl.pallas_call(functools.partial(return_kernel, scale), out_shape=(shaped...  72.5 us
    ppermute x5, waiting for transfers between devices, shift_by_one(): return lax.ppermute(x, axis, steps)  33.3 us
    pallas_call x1, Pallas kernels, inner_slots(): pl.pallas_call(inner_kernel, out_shape=TILE_OUT, in_specs=[SMEM_SPEC] * 2...  24.5 us
    pallas_call x1, Pallas kernels, outer_slots(): pl.pallas_call(outer_kernel, out_shape=TILE_OUT + (shaped(2, HALF, TILE),...  17.8 us
    ppermute x5, starting transfers between devices, shift_by_one(): return lax.ppermute(x, axis, steps)  12.6 us
    pallas_call x1, Pallas kernels, fold(): pl.pallas_call(fold_kernel, out_shape=shaped(2, TILE, TILE), in_specs=[HB...  5.09 us
  transfers between devices with their start and end apart: 8, of which 3 were waited for; matrix products, arithmetic and copies ran while one was open for 0% of the time, Pallas kernels for 14%

profile of v6, /device:TPU:1, one launch (start us, length us, event | category | flops | bytes accessed | tf_op | source)
XLA Modules:
  0.0 181.3 jit_solution(12708997097451391201)
XLA Ops:
  0.6 0.0 copy-start.5
  0.6 3.0 %fusion.1 = (f32[2,1024,128]{2,1,0:T(8,128)}, f32[2,1024,128]{2,1,0:T(8,128)}) fusion(f32[2,1024,1024]{2,1,0:T(8,128)} %field.3), kind=kLoop, calls=%fused_computation.3 | loop fusion | bytes 4194304 | tf_op jit(solution)/shard_map/slice | solution.py:765
  3.7 2.7 %fusion = (f32[2,128,1024]{2,1,0:T(8,128)S(1)}, f32[2,128,1024]{2,1,0:T(8,128)}) fusion(f32[2,1024,1024]{2,1,0:T(8,128)} %field.3), kind=kLoop, calls=%fused_computation.2 | loop fusion | bytes 4194304 | tf_op jit(solution)/shard_map/slice | solution.py:767
  6.4 1.6 collective-permute-start.4
  8.0 3.3 %collective-permute-start.3 = (f32[2,128,1024]{2,1,0:T(8,128)S(1)}, f32[2,128,1024]{2,1,0:T(8,128)}, u32[]{:S(2)}, u32[]{:S(2)}) collective-permute-start(f32[2,128,1024]{2,1,0:T(8,128)S(1)} %get-tuple-element.57), channel_id=1, source_target_pairs={{8,0},{16,8},{24,16},{32,24},{40,32},{48,40},{56,48},{72,64},{80,7... | collective-permute-start | bytes 3145736 | tf_op jit(solution)/shard_map/ppermute | solution.py:760
  11.3 3.7 %collective-permute-start = (f32[2,1024,128]{2,1,0:T(8,128)}, f32[2,1024,128]{2,1,0:T(8,128)S(1)}, u32[]{:S(2)}, u32[]{:S(2)}) collective-permute-start(f32[2,1024,128]{2,1,0:T(8,128)} %get-tuple-element.30), channel_id=1, source_target_pairs={{0,1},{1,2},{2,3},{3,4},{4,5},{5,6},{6,7},{8,9},{9,10},{10,11},{11... | collective-permute-start | bytes 3145736 | tf_op jit(solution)/shard_map/ppermute | solution.py:726
  15.0 1.3 collective-permute-start.1
  16.3 3.3 %collective-permute-start.2 = (f32[2,128,1024]{2,1,0:T(8,128)}, f32[2,128,1024]{2,1,0:T(8,128)}, u32[]{:S(2)}, u32[]{:S(2)}) collective-permute-start(f32[2,128,1024]{2,1,0:T(8,128)} %get-tuple-element.58), channel_id=1, source_target_pairs={{0,8},{8,16},{16,24},{24,32},{32,40},{40,48},{48,56},{56,64},{64,7... | collective-permute-start | bytes 3145736 | tf_op jit(solution)/shard_map/ppermute | solution.py:726
  19.6 0.0 copy-done.5
  19.6 0.7 copy.14.centers
  20.3 24.5 %inner_slots.1 = (f32[2,1024,1024]{2,1,0:T(8,128)}, f32[2,2,256,128]{3,2,1,0:T(8,128)}, f32[16]{0:T(128)}) custom-call(s32[16,2]{1,0:T(8,128)} %copy.14.centers, s32[16]{0:T(128)} %live.3, f32[2,256,256]{2,1,0:T(8,128)} %probe.3, bf16[4,256,768]{2,1,0:T(8,128)(2,1)} %constant.6.clone.lefts, bf16[4,768,256]{2,1,0:T(8,128)(2,1)} %constant.7.clone.rights, ...), custom_call_target="tpu_custom_call" | custom-call | flops 13958643712 | bytes 31457280 | tf_op jit(solution)/shard_map/inner_slots/pallas_call | solution.py:372
  44.9 0.0 collective-permute-done.4
  44.9 1.6 collective-permute-start.5
  46.5 28.1 %collective-permute-done.left = f32[2,1024,128]{2,1,0:T(8,128)S(1)} collective-permute-done((f32[2,1024,128]{2,1,0:T(8,128)}, f32[2,1024,128]{2,1,0:T(8,128)S(1)}, u32[]{:S(2)}, u32[]{:S(2)}) %collective-permute-start) | collective-permute-done | bytes 1048608 | tf_op jit(solution)/shard_map/ppermute | solution.py:726
  74.6 0.0 copy-start
  74.6 0.0 collective-permute-done.1.right
  74.6 0.0 copy-start.1
  74.6 0.0 collective-permute-done.2.up
  74.6 0.0 collective-permute-done.3.straight
  74.7 1.9 %collective-permute-start.6 = (f32[2,128,256]{2,1,0:T(8,128)S(1)}, f32[2,128,256]{2,1,0:T(8,128)S(1)}, u32[]{:S(2)}, u32[]{:S(2)}) collective-permute-start(f32[2,128,256]{2,1,0:T(8,128)S(1)} %pad_maximum_fusion), channel_id=1, source_target_pairs={{0,8},{8,16},{16,24},{24,32},{32,40},{40,48},{48,56},{56,64},{64,7... | collective-permute-start | bytes 786440 | tf_op jit(solution)/shard_map/ppermute | solution.py:726
  76.7 2.4 %collective-permute-start.7 = (f32[2,128,256]{2,1,0:T(8,128)S(1)}, f32[2,128,256]{2,1,0:T(8,128)S(1)}, u32[]{:S(2)}, u32[]{:S(2)}) collective-permute-start(f32[2,128,256]{2,1,0:T(8,128)S(1)} %pad_maximum_fusion.1), channel_id=1, source_target_pairs={{8,0},{16,8},{24,16},{32,24},{40,32},{48,40},{56,48},{64,56},{72,6... | collective-permute-start | bytes 786440 | tf_op jit(solution)/shard_map/ppermute | solution.py:726
  79.1 0.8 collective-permute-done.6.above
  79.9 0.0 copy-start.3
  79.9 4.4 %collective-permute-done.7.below = f32[2,128,256]{2,1,0:T(8,128)S(1)} collective-permute-done((f32[2,128,256]{2,1,0:T(8,128)S(1)}, f32[2,128,256]{2,1,0:T(8,128)S(1)}, u32[]{:S(2)}, u32[]{:S(2)}) %collective-permute-start.7) | collective-permute-done | bytes 262176 | tf_op jit(solution)/shard_map/ppermute | solution.py:726
  84.3 0.0 copy-start.4
  84.3 0.0 collective-permute-done.5.second
  84.4 0.0 copy-done
  84.4 0.0 copy-done.1
  84.4 0.0 copy-done.3
  84.4 0.7 copy-done.4
  85.0 17.8 %outer_slots.1 = (f32[2,1024,1024]{2,1,0:T(8,128)}, f32[2,2,256,128]{3,2,1,0:T(8,128)}, f32[16]{0:T(128)}, f32[2,128,1024]{2,1,0:T(8,128)}, f32[2,128,1024]{2,1,...) custom-call(s32[16,2]{1,0:T(8,128)} %copy.14.centers, ...), custom_call_target="tpu_custom_call", output_to_operand_aliasing={{0}: (15, {})} | custom-call | flops 6979321856 | bytes 31457280 | tf_op jit(solution)/shard_map/outer_slots/pallas_call | solution.py:385
  102.9 72.5 %send_back.1 = (f32[2,1024,128]{2,1,0:T(8,128)}, f32[2,1024,128]{2,1,0:T(8,128)}, f32[2,128,1024]{2,1,0:T(8,128)}, f32[2,128,1024]{2,1,0:T(8,128)}, f32[2,256,256]{2,1,0:T(8,128)}) custom-call(f32[2,1024,128]{2,1,0:T(8,128)} %get-tuple-element.43.gleft, f32[2,1024,128]{2,1,0:T(8,128)} %get-tuple-element.44.gright, f32[2,128,256]{2,1,0:T(8,128)} %get-tuple-element.45.gabove, ...), custom_call_target="tpu_custom_call" | custom-call | flops 524288 | bytes 104857600 | tf_op jit(solution)/shard_map/send_back/pallas_call | solution.py:624
  175.3 0.0 copy-start.2
  175.3 5.1 %fold.1 = f32[2,1024,1024]{2,1,0:T(8,128)} custom-call(f32[2,1024,128]{2,1,0:T(8,128)} %get-tuple-element.50.got_left, f32[2,1024,128]{2,1,0:T(8,128)} %get-tuple-element.51.got_right, f32[2,128,1024]{2,1,0:T(8,128)} %get-tuple-element.52.got_up, f32[2,128,1024]{2,1,0:T(8,128)} %get-tuple-element.53.got_down, ...), custom_call_target="tpu_custom_call", output_to_operand_aliasing={{}: (4, {})} | custom-call | tf_op jit(solution)/shard_map/fold/pallas_call | solution.py:704
  180.4 0.0 copy-done.2
  180.5 0.8 copy.18
  (3 shorter events, 0.1 us)
Async XLA Ops:
  0.6 19.0 %copy-start.5 = (s32[16,2]{0,1:T(2,128)S(1)}, s32[16,2]{0,1:T(2,128)}, u32[]{:S(2)}) copy-start(s32[16,2]{0,1:T(2,128)} %param.10) | copy-start | bytes 388
  6.4 38.5 %collective-permute-start.4 = (f32[2,128,1024]{2,1,0:T(8,128)S(1)}, f32[2,128,1024]{2,1,0:T(8,128)}, u32[]{:S(2)}, u32[]{:S(2)}) collective-permute-start(f32[2,128,1024]{2,1,0:T(8,128)S(1)} %get-tuple-element.57), channel_id=1, source_target_pairs={{64,57},{66,59},{68,61},{70,63},{65,64},{67,66},{69,68},{71,70}} | collective-permute-start | bytes 3145736 | tf_op jit(solution)/shard_map/ppermute | solution.py:746
  8.0 66.6 %collective-permute-start.3 = (f32[2,128,1024]{2,1,0:T(8,128)S(1)}, f32[2,128,1024]{2,1,0:T(8,128)}, u32[]{:S(2)}, u32[]{:S(2)}) collective-permute-start(f32[2,128,1024]{2,1,0:T(8,128)S(1)} %get-tuple-element.57), channel_id=1, source_target_pairs={{8,0},{16,8},{24,16},{32,24},{40,32},{48,40},{56,48},{72,64},{80,7... | collective-permute-start | bytes 3145736 | tf_op jit(solution)/shard_map/ppermute | solution.py:760
  11.3 63.3 %collective-permute-start = (f32[2,1024,128]{2,1,0:T(8,128)}, f32[2,1024,128]{2,1,0:T(8,128)S(1)}, u32[]{:S(2)}, u32[]{:S(2)}) collective-permute-start(f32[2,1024,128]{2,1,0:T(8,128)} %get-tuple-element.30), channel_id=1, source_target_pairs={{0,1},{1,2},{2,3},{3,4},{4,5},{5,6},{6,7},{8,9},{9,10},{10,11},{11... | collective-permute-start | bytes 3145736 | tf_op jit(solution)/shard_map/ppermute | solution.py:726
  15.0 59.6 %collective-permute-start.1 = (f32[2,1024,128]{2,1,0:T(8,128)}, f32[2,1024,128]{2,1,0:T(8,128)S(1)}, u32[]{:S(2)}, u32[]{:S(2)}) collective-permute-start(f32[2,1024,128]{2,1,0:T(8,128)} %get-tuple-element.31), channel_id=1, source_target_pairs={{1,0},{2,1},{3,2},{4,3},{5,4},{6,5},{7,6},{9,8},{10,9},{11,10},{12... | collective-permute-start | bytes 3145736 | tf_op jit(solution)/shard_map/ppermute | solution.py:726
  16.3 58.3 %collective-permute-start.2 = (f32[2,128,1024]{2,1,0:T(8,128)}, f32[2,128,1024]{2,1,0:T(8,128)}, u32[]{:S(2)}, u32[]{:S(2)}) collective-permute-start(f32[2,128,1024]{2,1,0:T(8,128)} %get-tuple-element.58), channel_id=1, source_target_pairs={{0,8},{8,16},{16,24},{24,32},{32,40},{40,48},{48,56},{56,64},{64,7... | collective-permute-start | bytes 3145736 | tf_op jit(solution)/shard_map/ppermute | solution.py:726
  44.9 39.5 %collective-permute-start.5 = (f32[2,128,1024]{2,1,0:T(8,128)}, f32[2,128,1024]{2,1,0:T(8,128)}, u32[]{:S(2)}, u32[]{:S(2)}) collective-permute-start(f32[2,128,1024]{2,1,0:T(8,128)} %collective-permute-done.4), channel_id=1, source_target_pairs={{57,56},{59,58},{61,60},{63,62},{64,57},{66,59},{68,61},{70,63}} | collective-permute-start | bytes 3145736 | tf_op jit(solution)/shard_map/ppermute | solution.py:746
  74.6 9.8 %copy-start = (f32[2,1024,128]{2,1,0:T(8,128)}, f32[2,1024,128]{2,1,0:T(8,128)S(1)}, u32[]{:S(2)}) copy-start(f32[2,1024,128]{2,1,0:T(8,128)S(1)} %collective-permute-done.left) | copy-start | bytes 3145732
  74.6 9.8 %copy-start.1 = (f32[2,1024,128]{2,1,0:T(8,128)}, f32[2,1024,128]{2,1,0:T(8,128)S(1)}, u32[]{:S(2)}) copy-start(f32[2,1024,128]{2,1,0:T(8,128)S(1)} %collective-permute-done.1.right) | copy-start | bytes 3145732
  74.7 5.2 %collective-permute-start.6 = (f32[2,128,256]{2,1,0:T(8,128)S(1)}, f32[2,128,256]{2,1,0:T(8,128)S(1)}, u32[]{:S(2)}, u32[]{:S(2)}) collective-permute-start(f32[2,128,256]{2,1,0:T(8,128)S(1)} %pad_maximum_fusion), channel_id=1, source_target_pairs={{0,8},{8,16},{16,24},{24,32},{32,40},{40,48},{48,56},{56,64},{64,7... | collective-permute-start | bytes 786440 | tf_op jit(solution)/shard_map/ppermute | solution.py:726
  76.7 7.7 %collective-permute-start.7 = (f32[2,128,256]{2,1,0:T(8,128)S(1)}, f32[2,128,256]{2,1,0:T(8,128)S(1)}, u32[]{:S(2)}, u32[]{:S(2)}) collective-permute-start(f32[2,128,256]{2,1,0:T(8,128)S(1)} %pad_maximum_fusion.1), channel_id=1, source_target_pairs={{8,0},{16,8},{24,16},{32,24},{40,32},{48,40},{56,48},{64,56},{72,6... | collective-permute-start | bytes 786440 | tf_op jit(solution)/shard_map/ppermute | solution.py:726
  79.9 4.4 %copy-start.3 = (f32[2,128,256]{2,1,0:T(8,128)}, f32[2,128,256]{2,1,0:T(8,128)S(1)}, u32[]{:S(2)}) copy-start(f32[2,128,256]{2,1,0:T(8,128)S(1)} %collective-permute-done.6.above) | copy-start | bytes 786436
  84.3 0.7 copy-start.4
  175.3 5.1 %copy-start.2 = (f32[2,256,256]{2,1,0:T(8,128)S(1)}, f32[2,256,256]{2,1,0:T(8,128)}, u32[]{:S(2)}) copy-start(f32[2,256,256]{2,1,0:T(8,128)} %get-tuple-element.71) | copy-start | bytes 1572868
